TPU v7x, 1024 devices: a whole 8x8x8 slice. The times are simulated.
1024 devices in a mesh: dom: 64 (over y, z), sub: 8 (over x_hi, core), lane: 2 (over x_lo).
Axes of the slice: x: 8 (x_hi: 4, x_lo: 2; x = x_hi * 2 + x_lo), y: 8, z: 8, core: 2. Of those that a mesh axis runs over, the one named last changes fastest.
Arguments:
- rhs_field: float32 [2048, 128, 256], P('dom', 'sub', 'lane'), may hold values from -6 to 6
- coef_field: float32 [2048, 128, 256], P('dom', 'sub', 'lane'), may hold values from 0.5 to 4
- pressure_old: float32 [2048, 128, 256], P('dom', 'sub', 'lane'), may hold values from -6 to 6
- cell_index: int32 [262144], P(('dom', 'sub', 'lane')), may hold values from 0 to 65535, as said below
- normals: float32 [3, 262144], P(None, ('dom', 'sub', 'lane')), may hold values from -1 to 1
- point_coords: float32 [3, 262144], P(None, ('dom', 'sub', 'lane')), may hold values from 0 to 1.8
- partner: int32 [262144, 1], P(('dom', 'sub', 'lane')), may hold values from 0 to 63; in each aligned block of 256 rows (0 to 255, 256 to 511, ...) at most 8 rows name the same one
- node_coords: float32 [3, 524288], P(None, ('dom', 'sub', 'lane')), may hold values from 0 to 1
- shell_block: float32 [524288, 512], P(('dom', 'sub', 'lane')), may hold values from -0.25 to 0.25
- disp_old: float32 [3, 262144], P(None, ('dom', 'sub', 'lane')), may hold values from -3 to 3
Outputs:
- pressure_new: float32 [2048, 128, 256], P('dom', 'sub', 'lane')
- disp_new: float32 [3, 262144], P(None, ('dom', 'sub', 'lane'))
- residual_rms: float32 [], replicated
Inputs may be any that keep to these rules, and one draw needn't show every extreme that they name: `partner`: among the 256 points of one device, at most 8 name the same dom index, and that bound is reached. `cell_index`: A cell of the point's own device's block, numbered row-major over 32 x 16 x 128.
All inputs are finite; a program needn't handle non-finite values.
Results may differ from a plain program's by a relative error of at most 0.0003.
Values sent between devices are 32-bit elements; how exact they have to be, the bound alone decides.
No kernel may reach another device: no remote copies, remote signals or barrier semaphores. Data moves between devices by JAX's collectives and lax.ppermute only.
A program may use at most 32 MiB of HBM per device.

v0:
```python
import math

import jax
import jax.numpy as jnp
from jax import lax
from jax.sharding import PartitionSpec as P

SWEEPS = 4


source_gain = 16.0
relaxation = 0.5
inv_radius_sq = 11.111111
epsilon = 1e-06


def with_halo(cells, sides, width):
    for axis, dim in sides:
        count = lax.axis_size(axis)
        ends = count - 1
        head = lax.slice_in_dim(cells, 0, width, axis=dim)
        tail = lax.slice_in_dim(cells, cells.shape[dim] - width, cells.shape[dim], axis=dim)
        cells = jnp.concatenate(
            [
                lax.ppermute(tail, axis, [(i, (i + 1) % count) for i in range(ends)]),
                cells,
                lax.ppermute(head, axis, [((i + 1) % count, i) for i in range(ends)]),
            ],
            axis=dim,
        )
    return cells


def neighbours(padded):
    total = padded[2:, 1:-1, 1:-1] + padded[:-2, 1:-1, 1:-1]
    total = total + padded[1:-1, 2:, 1:-1] + padded[1:-1, :-2, 1:-1]
    total = total + padded[1:-1, 1:-1, 2:] + padded[1:-1, 1:-1, :-2]
    return total


def structure(received, nodes, shell, point_count):
    coords = received[:3]
    forces = received[3:]
    distance = jnp.zeros((coords.shape[1], nodes.shape[1]), jnp.float32)
    for comp in range(3):
        distance = distance + (coords[comp][:, None] - nodes[comp][None, :]) ** 2
    kernel = jnp.exp(-distance * inv_radius_sq)
    loading = jnp.dot(forces, kernel, precision=lax.Precision.HIGHEST) / math.sqrt(point_count)
    displaced = loading + jnp.dot(loading, shell, precision=lax.Precision.HIGHEST)
    return jnp.dot(displaced, kernel.T, precision=lax.Precision.HIGHEST) / math.sqrt(nodes.shape[1])


def body(
    rhs_field,
    coef_field,
    pressure_old,
    cell_index,
    normals,
    point_coords,
    partner,
    node_coords,
    shell_block,
    disp_old,
):
    dom_count = lax.axis_size("dom")
    point_count = cell_index.shape[0]
    capacity = 2 * point_count // dom_count
    target = partner[:, 0]
    onehot = (target[:, None] == jnp.arange(dom_count, dtype=jnp.int32)[None, :]).astype(jnp.int32)
    slot_rank = jnp.sum((jnp.cumsum(onehot, axis=0) - onehot) * onehot, axis=1)
    slot_index = target * capacity + slot_rank
    denom = 6.0 + coef_field
    shape = rhs_field.shape

    def fluid_solve(source_field):
        pressure = pressure_old
        for sweep_no in range(SWEEPS):
            padded = with_halo(pressure, (("dom", 0), ("sub", 1), ("lane", 2)), 1)
            pressure = (source_field + neighbours(padded)) / denom
        return pressure

    def couple(disp):
        values = source_gain * jnp.sum(disp * normals, axis=0)
        source_field = rhs_field.reshape(-1).at[cell_index].add(values).reshape(shape)
        pressure = fluid_solve(source_field)
        press_pts = pressure.reshape(-1)[cell_index]
        force = press_pts[None, :] * normals
        payload = jnp.concatenate([point_coords, force], axis=0)
        sending = jnp.zeros((6, dom_count * capacity), jnp.float32).at[:, slot_index].set(payload)
        received = lax.all_to_all(
            sending.reshape(6, dom_count, capacity), "dom", split_axis=1, concat_axis=1, tiled=True
        )
        returned = structure(
            received.reshape(6, dom_count * capacity), node_coords, shell_block, point_count
        )
        arrived = lax.all_to_all(
            returned.reshape(3, dom_count, capacity), "dom", split_axis=1, concat_axis=1, tiled=True
        )
        return (pressure, arrived.reshape(3, dom_count * capacity)[:, slot_index])

    pressure_a, mapped_a = couple(disp_old)
    resid_a = mapped_a - disp_old
    second = disp_old + relaxation * resid_a
    pressure_new, mapped_b = couple(second)
    resid_b = mapped_b - second
    delta = resid_b - resid_a
    dot_vr, dot_vv, dot_rr = lax.psum(
        (jnp.sum(delta * resid_b), jnp.sum(delta * delta), jnp.sum(resid_b * resid_b)),
        ("dom", "sub", "lane"),
    )
    weight_iqn = dot_vr / (dot_vv + epsilon)
    disp_new = mapped_b - weight_iqn * (mapped_b - mapped_a)
    total_count = 3.0 * point_count * dom_count * lax.axis_size("sub") * lax.axis_size("lane")
    residual_rms = jnp.sqrt(dot_rr / total_count)
    return (pressure_new, disp_new, residual_rms)


def solution(mesh):
    placed = (
        P("dom", "sub", "lane"),
        P("dom", "sub", "lane"),
        P("dom", "sub", "lane"),
        P(("dom", "sub", "lane")),
        P(None, ("dom", "sub", "lane")),
        P(None, ("dom", "sub", "lane")),
        P(("dom", "sub", "lane"), None),
        P(None, ("dom", "sub", "lane")),
        P(("dom", "sub", "lane"), None),
        P(None, ("dom", "sub", "lane")),
    )
    return jax.shard_map(
        body,
        mesh=mesh,
        in_specs=placed,
        out_specs=(P("dom", "sub", "lane"), P(None, ("dom", "sub", "lane")), P()),
        check_vma=False,
    )
```

profile of v0, /device:TPU:1, one launch (start us, length us, event | category | flops | bytes accessed | tf_op | source)
XLA Modules:
  0.0 459.4 jit_solution(15185736718135129348)
XLA Ops:
  1.8 5.9 %collective-permute-start.1 = (f32[1,16,128]{2,1,0:T(8,128)S(1)}, f32[1,16,128]{2,1,0:T(8,128)S(1)}, u32[]{:S(2)}, u32[]{:S(2)}) collective-permute-start(f32[1,16,128]{2,1,0:T(8,128)S(1)} %get-tuple-element.70), channel_id=1, source_target_pairs={{0,16},{16,32},{32,48},{48,64},{64,80},{80,96},{96,112},{112,128},... | collective-permute-start | bytes 24584 | tf_op jit(solution)/shard_map/ppermute | solution.py:25
  7.6 1.3 collective-permute-start
  9.0 4.6 collective-permute-done
  13.6 11.2 %collective-permute-start.2 = (f32[34,1,128]{2,1,0:T(1,128)S(1)}, f32[34,1,128]{2,1,0:T(1,128)S(1)}, u32[]{:S(2)}, u32[]{:S(2)}) collective-permute-start(f32[34,1,128]{2,1,0:T(1,128)S(1)} %get-tuple-element.56), channel_id=1, source_target_pairs={{2,0},{4,2},{6,4},{8,6},{10,8},{12,10},{14,12},{3,1},{5,3},{7,5},{... | collective-permute-start | bytes 52232 | tf_op jit(solution)/shard_map/ppermute | solution.py:27
  24.8 1.9 collective-permute-start.3
  28.2 1.3 collective-permute-start.4
  29.5 5.5 %collective-permute-start.5 = (f32[34,18,1]{2,1,0:T(8,128)S(1)}, f32[34,18,1]{2,1,0:T(8,128)}, u32[]{:S(2)}, u32[]{:S(2)}) collective-permute-start(f32[34,18,1]{2,1,0:T(8,128)S(1)} %get-tuple-element.42), channel_id=1, source_target_pairs={{0,1},{2,3},{4,5},{6,7},{8,9},{10,11},{12,13},{14,15},{16,17},{18,... | collective-permute-start | bytes 7352 | tf_op jit(solution)/shard_map/ppermute | solution.py:25
  35.0 2.1 scatter_fusion
  37.1 4.1 collective-permute-done.4
  41.3 1.5 collective-permute-done.5
  42.8 1.5 add_divide_fusion.1
  44.3 1.3 collective-permute-start.6
  45.6 4.0 collective-permute-start.7
  50.4 4.3 collective-permute-start.8
  54.7 2.1 collective-permute-start.9
  58.0 1.3 collective-permute-start.10
  59.3 4.3 collective-permute-start.11
  63.6 7.9 %collective-permute-done.10 = f32[34,18,1]{2,1,0:T(8,128)S(1)} collective-permute-done((f32[34,18,1]{2,1,0:T(8,128)S(1)}, f32[34,18,1]{2,1,0:T(8,128)S(1)}, u32[]{:S(2)}, u32[]{:S(2)}) %collective-permute-start.10) | collective-permute-done | bytes 2480 | tf_op jit(solution)/shard_map/ppermute | solution.py:27
  72.8 1.3 collective-permute-start.12
  74.1 5.8 %collective-permute-start.13 = (f32[1,16,128]{2,1,0:T(8,128)S(1)}, f32[1,16,128]{2,1,0:T(8,128)S(1)}, u32[]{:S(2)}, u32[]{:S(2)}) collective-permute-start(f32[1,16,128]{2,1,0:T(8,128)S(1)} %get-tuple-element.65), channel_id=1, source_target_pairs={{0,16},{16,32},{32,48},{48,64},{64,80},{80,96},{96,112},{112,128},... | collective-permute-start | bytes 24584 | tf_op jit(solution)/shard_map/ppermute | solution.py:25
  80.7 3.2 collective-permute-start.14
  83.9 3.8 collective-permute-start.15
  91.0 4.2 collective-permute-start.17
  96.0 6.2 %collective-permute-done.16 = f32[34,18,1]{2,1,0:T(8,128)S(1)} collective-permute-done((f32[34,18,1]{2,1,0:T(8,128)}, f32[34,18,1]{2,1,0:T(8,128)S(1)}, u32[]{:S(2)}, u32[]{:S(2)}) %collective-permute-start.16) | collective-permute-done | bytes 2480 | tf_op jit(solution)/shard_map/ppermute | solution.py:27
  102.2 1.9 collective-permute-done.17
  105.8 4.5 collective-permute-start.19
  111.1 2.1 collective-permute-start.20
  113.2 5.5 %collective-permute-start.21 = (f32[34,1,128]{2,1,0:T(1,128)S(1)}, f32[34,1,128]{2,1,0:T(1,128)S(1)}, u32[]{:S(2)}, u32[]{:S(2)}) collective-permute-start(f32[34,1,128]{2,1,0:T(1,128)S(1)} %get-tuple-element.49), channel_id=1, source_target_pairs={{0,2},{2,4},{4,6},{6,8},{8,10},{10,12},{12,14},{1,3},{3,5},{5,7},{... | collective-permute-start | bytes 52232 | tf_op jit(solution)/shard_map/ppermute | solution.py:25
  121.1 4.0 collective-permute-start.23
  125.2 5.2 %collective-permute-done.22 = f32[34,18,1]{2,1,0:T(8,128)S(1)} collective-permute-done((f32[34,18,1]{2,1,0:T(8,128)S(1)}, f32[34,18,1]{2,1,0:T(8,128)S(1)}, u32[]{:S(2)}, u32[]{:S(2)}) %collective-permute-start.22) | collective-permute-done | bytes 2480 | tf_op jit(solution)/shard_map/ppermute | solution.py:27
  130.4 1.8 collective-permute-done.23
  132.6 1.7 gather_fusion
  137.5 25.3 %all-to-all-start = ((f32[6,64,8]{2,0,1:T(8,128)}), f32[6,64,8]{2,0,1:T(8,128)S(1)}, u32[]{:S(2)}, u32[]{:S(2)}) async-start(f32[6,64,8]{2,0,1:T(8,128)} %copy.68), calls=%async_computation | async-start | bytes 524288 | tf_op jit(solution)/shard_map/all_to_all | solution.py:90
  162.8 12.3 %all-to-all-done = f32[6,64,8]{2,0,1:T(8,128)S(1)} async-done(((f32[6,64,8]{2,0,1:T(8,128)}), f32[6,64,8]{2,0,1:T(8,128)S(1)}, u32[]{:S(2)}, u32[]{:S(2)}) %all-to-all-start) | async-done | bytes 12320 | tf_op jit(solution)/shard_map/all_to_all | solution.py:90
  177.5 1.3 convolution_multiply_fusion.2
  179.7 4.8 %all-to-all-start.1 = ((f32[3,64,8]{2,0,1:T(4,128)}), f32[3,64,8]{2,0,1:T(4,128)S(1)}, u32[]{:S(2)}, u32[]{:S(2)}) async-start(f32[3,64,8]{2,0,1:T(4,128)} %copy.70), calls=%async_computation.1 | async-start | bytes 262144 | tf_op jit(solution)/shard_map/all_to_all | solution.py:96
  184.5 11.6 %all-to-all-done.1 = f32[3,64,8]{2,0,1:T(4,128)S(1)} async-done(((f32[3,64,8]{2,0,1:T(4,128)}), f32[3,64,8]{2,0,1:T(4,128)S(1)}, u32[]{:S(2)}, u32[]{:S(2)}) %all-to-all-start.1) | async-done | bytes 6176 | tf_op jit(solution)/shard_map/all_to_all | solution.py:96
  197.4 2.1 scatter_fusion.1
  200.8 4.0 collective-permute-start.25
  205.6 1.9 collective-permute-start.26
  207.5 11.2 %collective-permute-start.27 = (f32[34,1,128]{2,1,0:T(1,128)S(1)}, f32[34,1,128]{2,1,0:T(1,128)S(1)}, u32[]{:S(2)}, u32[]{:S(2)}) collective-permute-start(f32[34,1,128]{2,1,0:T(1,128)S(1)} %get-tuple-element.47), channel_id=1, source_target_pairs={{0,2},{2,4},{4,6},{6,8},{8,10},{10,12},{12,14},{1,3},{3,5},{5,7},{... | collective-permute-start | bytes 52232 | tf_op jit(solution)/shard_map/ppermute | solution.py:25
  221.2 4.1 collective-permute-start.29
  225.3 3.4 collective-permute-done.28
  228.7 1.5 collective-permute-done.29
  230.6 1.3 collective-permute-start.30
  231.9 4.5 collective-permute-start.31
  237.3 1.9 collective-permute-start.32
  239.2 8.4 %collective-permute-start.33 = (f32[34,1,128]{2,1,0:T(1,128)S(1)}, f32[34,1,128]{2,1,0:T(1,128)S(1)}, u32[]{:S(2)}, u32[]{:S(2)}) collective-permute-start(f32[34,1,128]{2,1,0:T(1,128)S(1)} %get-tuple-element.45), channel_id=1, source_target_pairs={{0,2},{2,4},{4,6},{6,8},{8,10},{10,12},{12,14},{1,3},{3,5},{5,7},{... | collective-permute-start | bytes 52232 | tf_op jit(solution)/shard_map/ppermute | solution.py:25
  248.7 1.3 collective-permute-start.34
  250.0 4.2 collective-permute-start.35
  254.2 3.4 collective-permute-done.34
  257.6 1.5 collective-permute-done.35
  260.8 4.5 collective-permute-start.37
  266.1 1.9 collective-permute-start.38
  268.1 8.2 %collective-permute-start.39 = (f32[34,1,128]{2,1,0:T(1,128)S(1)}, f32[34,1,128]{2,1,0:T(1,128)S(1)}, u32[]{:S(2)}, u32[]{:S(2)}) collective-permute-start(f32[34,1,128]{2,1,0:T(1,128)S(1)} %get-tuple-element.43), channel_id=1, source_target_pairs={{0,2},{2,4},{4,6},{6,8},{8,10},{10,12},{12,14},{1,3},{3,5},{5,7},{... | collective-permute-start | bytes 52232 | tf_op jit(solution)/shard_map/ppermute | solution.py:25
  277.4 1.3 collective-permute-start.40
  278.7 4.2 collective-permute-start.41
  282.8 3.4 collective-permute-done.40
  286.3 1.5 collective-permute-done.41
  288.2 1.7 gather_fusion.2
  291.8 28.0 %all_to_all.20 = f32[6,64,8]{2,0,1:T(8,128)S(1)} all-to-all(f32[6,64,8]{2,0,1:T(8,128)S(1)} %copy.74), channel_id=1, replica_groups=mesh['dom'=64,'sub'=8,'lane'=2] {'dom'}, dimensions={1} | all-to-all | bytes 24576 | tf_op jit(solution)/shard_map/all_to_all | solution.py:90
  322.1 1.3 convolution_multiply_fusion
  323.7 15.3 %all_to_all.21 = f32[3,64,8]{2,0,1:T(4,128)S(1)} all-to-all(f32[3,64,8]{2,0,1:T(4,128)S(1)} %copy.76), channel_id=1, replica_groups=mesh['dom'=64,'sub'=8,'lane'=2] {'dom'}, dimensions={1} | all-to-all | bytes 12288 | tf_op jit(solution)/shard_map/all_to_all | solution.py:96
  341.0 114.7 %all-reduce = (f32[]{:T(128)}, f32[]{:T(128)}, f32[]{:T(128)}) all-reduce(f32[]{:T(128)} %get-tuple-element.22, f32[]{:T(128)} %get-tuple-element.23, f32[]{:T(128)} %get-tuple-element.21), channel_id=1, replica_groups=mesh['dom'=64,'sub'=8,'lane'=2] {'dom','sub','lane'}, use_global_device_ids=true, to_apply=%region_10.11 | all-reduce | flops 3 | bytes 24 | tf_op jit(solution)/shard_map/psum | solution.py:107
  (152 shorter events, 41.3 us)
Async XLA Ops:
  0.6 176.2 %copy-start = (f32[512,512]{1,0:T(8,128)S(1)}, f32[512,512]{1,0:T(8,128)}, u32[]{:S(2)}) copy-start(f32[512,512]{1,0:T(8,128)} %param.18) | copy-start | bytes 3145732
  0.6 1.1 copy-start.3
  1.8 7.2 %copy-start.10 = (s32[256]{0:T(256)S(1)}, s32[256]{0:T(256)}, u32[]{:S(2)}) copy-start(s32[256]{0:T(256)} %param.13) | copy-start | bytes 3076
  1.8 7.2 %collective-permute-start.1 = (f32[1,16,128]{2,1,0:T(8,128)S(1)}, f32[1,16,128]{2,1,0:T(8,128)S(1)}, u32[]{:S(2)}, u32[]{:S(2)}) collective-permute-start(f32[1,16,128]{2,1,0:T(8,128)S(1)} %get-tuple-element.70), channel_id=1, source_target_pairs={{0,16},{16,32},{32,48},{48,64},{64,80},{80,96},{96,112},{112,128},... | collective-permute-start | bytes 24584 | tf_op jit(solution)/shard_map/ppermute | solution.py:25
  7.6 5.9 %collective-permute-start = (f32[1,16,128]{2,1,0:T(8,128)S(1)}, f32[1,16,128]{2,1,0:T(8,128)S(1)}, u32[]{:S(2)}, u32[]{:S(2)}) collective-permute-start(f32[1,16,128]{2,1,0:T(8,128)S(1)} %get-tuple-element.69), channel_id=1, source_target_pairs={{16,0},{32,16},{48,32},{64,48},{80,64},{96,80},{112,96},{128,112},... | collective-permute-start | bytes 24584 | tf_op jit(solution)/shard_map/ppermute | solution.py:27
  13.6 13.2 %copy-start.4 = (f32[3,256]{1,0:T(4,128)S(1)}, f32[3,256]{1,0:T(4,128)}, u32[]{:S(2)}) copy-start(f32[3,256]{1,0:T(4,128)} %param.14) | copy-start | bytes 9220
  13.6 13.2 %copy-start.5 = (f32[3,256]{1,0:T(4,128)S(1)}, f32[3,256]{1,0:T(4,128)}, u32[]{:S(2)}) copy-start(f32[3,256]{1,0:T(4,128)} %param.19) | copy-start | bytes 9220
  13.6 13.2 %collective-permute-start.2 = (f32[34,1,128]{2,1,0:T(1,128)S(1)}, f32[34,1,128]{2,1,0:T(1,128)S(1)}, u32[]{:S(2)}, u32[]{:S(2)}) collective-permute-start(f32[34,1,128]{2,1,0:T(1,128)S(1)} %get-tuple-element.56), channel_id=1, source_target_pairs={{2,0},{4,2},{6,4},{8,6},{10,8},{12,10},{14,12},{3,1},{5,3},{7,5},{... | collective-permute-start | bytes 52232 | tf_op jit(solution)/shard_map/ppermute | solution.py:27
  24.8 3.1 collective-permute-start.3
  28.2 13.1 %collective-permute-start.4 = (f32[34,18,1]{2,1,0:T(8,128)S(1)}, f32[34,18,1]{2,1,0:T(8,128)}, u32[]{:S(2)}, u32[]{:S(2)}) collective-permute-start(f32[34,18,1]{2,1,0:T(8,128)S(1)} %get-tuple-element.41), channel_id=1, source_target_pairs={{1,0},{3,2},{5,4},{7,6},{9,8},{11,10},{13,12},{15,14},{17,16},{19,... | collective-permute-start | bytes 7352 | tf_op jit(solution)/shard_map/ppermute | solution.py:27
  29.5 13.3 %collective-permute-start.5 = (f32[34,18,1]{2,1,0:T(8,128)S(1)}, f32[34,18,1]{2,1,0:T(8,128)}, u32[]{:S(2)}, u32[]{:S(2)}) collective-permute-start(f32[34,18,1]{2,1,0:T(8,128)S(1)} %get-tuple-element.42), channel_id=1, source_target_pairs={{0,1},{2,3},{4,5},{6,7},{8,9},{10,11},{12,13},{14,15},{16,17},{18,... | collective-permute-start | bytes 7352 | tf_op jit(solution)/shard_map/ppermute | solution.py:25
  35.0 7.8 %copy-start.1 = (f32[32,16,128]{2,1,0:T(8,128)S(1)}, f32[32,16,128]{2,1,0:T(8,128)}, u32[]{:S(2)}) copy-start(f32[32,16,128]{2,1,0:T(8,128)} %param.11) | copy-start | bytes 786436
  44.3 5.3 %collective-permute-start.6 = (f32[1,16,128]{2,1,0:T(8,128)S(1)}, f32[1,16,128]{2,1,0:T(8,128)S(1)}, u32[]{:S(2)}, u32[]{:S(2)}) collective-permute-start(f32[1,16,128]{2,1,0:T(8,128)S(1)} %get-tuple-element.68), channel_id=1, source_target_pairs={{16,0},{32,16},{48,32},{64,48},{80,64},{96,80},{112,96},{128,112},... | collective-permute-start | bytes 24584 | tf_op jit(solution)/shard_map/ppermute | solution.py:27
  45.6 4.8 %collective-permute-start.7 = (f32[1,16,128]{2,1,0:T(8,128)S(1)}, f32[1,16,128]{2,1,0:T(8,128)S(1)}, u32[]{:S(2)}, u32[]{:S(2)}) collective-permute-start(f32[1,16,128]{2,1,0:T(8,128)S(1)} %get-tuple-element.67), channel_id=1, source_target_pairs={{0,16},{16,32},{32,48},{48,64},{64,80},{80,96},{96,112},{112,128},... | collective-permute-start | bytes 24584 | tf_op jit(solution)/shard_map/ppermute | solution.py:25
  50.4 6.5 %collective-permute-start.8 = (f32[34,1,128]{2,1,0:T(1,128)S(1)}, f32[34,1,128]{2,1,0:T(1,128)S(1)}, u32[]{:S(2)}, u32[]{:S(2)}) collective-permute-start(f32[34,1,128]{2,1,0:T(1,128)S(1)} %get-tuple-element.54), channel_id=1, source_target_pairs={{2,0},{4,2},{6,4},{8,6},{10,8},{12,10},{14,12},{3,1},{5,3},{7,5},{... | collective-permute-start | bytes 52232 | tf_op jit(solution)/shard_map/ppermute | solution.py:27
  54.7 3.1 collective-permute-start.9
  58.0 13.5 %collective-permute-start.10 = (f32[34,18,1]{2,1,0:T(8,128)S(1)}, f32[34,18,1]{2,1,0:T(8,128)S(1)}, u32[]{:S(2)}, u32[]{:S(2)}) collective-permute-start(f32[34,18,1]{2,1,0:T(8,128)S(1)} %get-tuple-element.39), channel_id=1, source_target_pairs={{1,0},{3,2},{5,4},{7,6},{9,8},{11,10},{13,12},{15,14},{17,16},{19,... | collective-permute-start | bytes 7352 | tf_op jit(solution)/shard_map/ppermute | solution.py:27
  59.3 13.1 %collective-permute-start.11 = (f32[34,18,1]{2,1,0:T(8,128)S(1)}, f32[34,18,1]{2,1,0:T(8,128)S(1)}, u32[]{:S(2)}, u32[]{:S(2)}) collective-permute-start(f32[34,18,1]{2,1,0:T(8,128)S(1)} %get-tuple-element.40), channel_id=1, source_target_pairs={{0,1},{2,3},{4,5},{6,7},{8,9},{10,11},{12,13},{14,15},{16,17},{18,... | collective-permute-start | bytes 7352 | tf_op jit(solution)/shard_map/ppermute | solution.py:25
  72.8 7.1 %collective-permute-start.12 = (f32[1,16,128]{2,1,0:T(8,128)S(1)}, f32[1,16,128]{2,1,0:T(8,128)S(1)}, u32[]{:S(2)}, u32[]{:S(2)}) collective-permute-start(f32[1,16,128]{2,1,0:T(8,128)S(1)} %get-tuple-element.66), channel_id=1, source_target_pairs={{16,0},{32,16},{48,32},{64,48},{80,64},{96,80},{112,96},{128,112},... | collective-permute-start | bytes 24584 | tf_op jit(solution)/shard_map/ppermute | solution.py:27
  74.1 6.6 %collective-permute-start.13 = (f32[1,16,128]{2,1,0:T(8,128)S(1)}, f32[1,16,128]{2,1,0:T(8,128)S(1)}, u32[]{:S(2)}, u32[]{:S(2)}) collective-permute-start(f32[1,16,128]{2,1,0:T(8,128)S(1)} %get-tuple-element.65), channel_id=1, source_target_pairs={{0,16},{16,32},{32,48},{48,64},{64,80},{80,96},{96,112},{112,128},... | collective-permute-start | bytes 24584 | tf_op jit(solution)/shard_map/ppermute | solution.py:25
  80.7 7.7 %collective-permute-start.14 = (f32[34,1,128]{2,1,0:T(1,128)S(1)}, f32[34,1,128]{2,1,0:T(1,128)S(1)}, u32[]{:S(2)}, u32[]{:S(2)}) collective-permute-start(f32[34,1,128]{2,1,0:T(1,128)S(1)} %get-tuple-element.52), channel_id=1, source_target_pairs={{2,0},{4,2},{6,4},{8,6},{10,8},{12,10},{14,12},{3,1},{5,3},{7,5},{... | collective-permute-start | bytes 52232 | tf_op jit(solution)/shard_map/ppermute | solution.py:27
  83.9 3.9 copy-start.7
  83.9 4.7 %collective-permute-start.15 = (f32[34,1,128]{2,1,0:T(1,128)S(1)}, f32[34,1,128]{2,1,0:T(1,128)S(1)}, u32[]{:S(2)}, u32[]{:S(2)}) collective-permute-start(f32[34,1,128]{2,1,0:T(1,128)S(1)} %get-tuple-element.51), channel_id=1, source_target_pairs={{0,2},{2,4},{4,6},{6,8},{8,10},{10,12},{12,14},{1,3},{3,5},{5,7},{... | collective-permute-start | bytes 52232 | tf_op jit(solution)/shard_map/ppermute | solution.py:25
  89.7 12.5 %collective-permute-start.16 = (f32[34,18,1]{2,1,0:T(8,128)}, f32[34,18,1]{2,1,0:T(8,128)S(1)}, u32[]{:S(2)}, u32[]{:S(2)}) collective-permute-start(f32[34,18,1]{2,1,0:T(8,128)} %get-tuple-element.37), channel_id=1, source_target_pairs={{1,0},{3,2},{5,4},{7,6},{9,8},{11,10},{13,12},{15,14},{17,16},{19,... | collective-permute-start | bytes 7352 | tf_op jit(solution)/shard_map/ppermute | solution.py:27
  91.0 13.1 %collective-permute-start.17 = (f32[34,18,1]{2,1,0:T(8,128)}, f32[34,18,1]{2,1,0:T(8,128)S(1)}, u32[]{:S(2)}, u32[]{:S(2)}) collective-permute-start(f32[34,18,1]{2,1,0:T(8,128)} %get-tuple-element.38), channel_id=1, source_target_pairs={{0,1},{2,3},{4,5},{6,7},{8,9},{10,11},{12,13},{14,15},{16,17},{18,... | collective-permute-start | bytes 7352 | tf_op jit(solution)/shard_map/ppermute | solution.py:25
  95.4 0.6 copy-start.9
  104.4 6.0 %collective-permute-start.18 = (f32[1,16,128]{2,1,0:T(8,128)S(1)}, f32[1,16,128]{2,1,0:T(8,128)S(1)}, u32[]{:S(2)}, u32[]{:S(2)}) collective-permute-start(f32[1,16,128]{2,1,0:T(8,128)S(1)} %get-tuple-element.64), channel_id=1, source_target_pairs={{16,0},{32,16},{48,32},{64,48},{80,64},{96,80},{112,96},{128,112},... | collective-permute-start | bytes 24584 | tf_op jit(solution)/shard_map/ppermute | solution.py:27
  105.7 4.6 slice-start
  105.8 5.3 %collective-permute-start.19 = (f32[1,16,128]{2,1,0:T(8,128)S(1)}, f32[1,16,128]{2,1,0:T(8,128)S(1)}, u32[]{:S(2)}, u32[]{:S(2)}) collective-permute-start(f32[1,16,128]{2,1,0:T(8,128)S(1)} %get-tuple-element.63), channel_id=1, source_target_pairs={{0,16},{16,32},{32,48},{48,64},{64,80},{80,96},{96,112},{112,128},... | collective-permute-start | bytes 24584 | tf_op jit(solution)/shard_map/ppermute | solution.py:25
  111.1 7.6 %collective-permute-start.20 = (f32[34,1,128]{2,1,0:T(1,128)S(1)}, f32[34,1,128]{2,1,0:T(1,128)S(1)}, u32[]{:S(2)}, u32[]{:S(2)}) collective-permute-start(f32[34,1,128]{2,1,0:T(1,128)S(1)} %get-tuple-element.50), channel_id=1, source_target_pairs={{2,0},{4,2},{6,4},{8,6},{10,8},{12,10},{14,12},{3,1},{5,3},{7,5},{... | collective-permute-start | bytes 52232 | tf_op jit(solution)/shard_map/ppermute | solution.py:27
  113.2 6.4 %collective-permute-start.21 = (f32[34,1,128]{2,1,0:T(1,128)S(1)}, f32[34,1,128]{2,1,0:T(1,128)S(1)}, u32[]{:S(2)}, u32[]{:S(2)}) collective-permute-start(f32[34,1,128]{2,1,0:T(1,128)S(1)} %get-tuple-element.49), channel_id=1, source_target_pairs={{0,2},{2,4},{4,6},{6,8},{8,10},{10,12},{12,14},{1,3},{3,5},{5,7},{... | collective-permute-start | bytes 52232 | tf_op jit(solution)/shard_map/ppermute | solution.py:25
  119.8 10.6 %collective-permute-start.22 = (f32[34,18,1]{2,1,0:T(8,128)S(1)}, f32[34,18,1]{2,1,0:T(8,128)S(1)}, u32[]{:S(2)}, u32[]{:S(2)}) collective-permute-start(f32[34,18,1]{2,1,0:T(8,128)S(1)} %get-tuple-element.35), channel_id=1, source_target_pairs={{1,0},{3,2},{5,4},{7,6},{9,8},{11,10},{13,12},{15,14},{17,16},{19,... | collective-permute-start | bytes 7352 | tf_op jit(solution)/shard_map/ppermute | solution.py:27
  121.1 11.1 %collective-permute-start.23 = (f32[34,18,1]{2,1,0:T(8,128)S(1)}, f32[34,18,1]{2,1,0:T(8,128)S(1)}, u32[]{:S(2)}, u32[]{:S(2)}) collective-permute-start(f32[34,18,1]{2,1,0:T(8,128)S(1)} %get-tuple-element.36), channel_id=1, source_target_pairs={{0,1},{2,3},{4,5},{6,7},{8,9},{10,11},{12,13},{14,15},{16,17},{18,... | collective-permute-start | bytes 7352 | tf_op jit(solution)/shard_map/ppermute | solution.py:25
  134.3 0.7 copy-start.6
  137.5 25.3 %copy-start.8 = (f32[3,512]{1,0:T(4,128)S(1)}, f32[3,512]{1,0:T(4,128)}, u32[]{:S(2)}) copy-start(f32[3,512]{1,0:T(4,128)} %param.17) | copy-start | bytes 18436
  137.5 37.6 %all-to-all-start = ((f32[6,64,8]{2,0,1:T(8,128)}), f32[6,64,8]{2,0,1:T(8,128)S(1)}, u32[]{:S(2)}, u32[]{:S(2)}) async-start(f32[6,64,8]{2,0,1:T(8,128)} %copy.68), calls=%async_computation | async-start | bytes 524288 | tf_op jit(solution)/shard_map/all_to_all | solution.py:90
  179.7 16.4 %all-to-all-start.1 = ((f32[3,64,8]{2,0,1:T(4,128)}), f32[3,64,8]{2,0,1:T(4,128)S(1)}, u32[]{:S(2)}, u32[]{:S(2)}) async-start(f32[3,64,8]{2,0,1:T(4,128)} %copy.70), calls=%async_computation.1 | async-start | bytes 262144 | tf_op jit(solution)/shard_map/all_to_all | solution.py:96
  199.5 5.3 %collective-permute-start.24 = (f32[1,16,128]{2,1,0:T(8,128)S(1)}, f32[1,16,128]{2,1,0:T(8,128)S(1)}, u32[]{:S(2)}, u32[]{:S(2)}) collective-permute-start(f32[1,16,128]{2,1,0:T(8,128)S(1)} %get-tuple-element.62), channel_id=1, source_target_pairs={{16,0},{32,16},{48,32},{64,48},{80,64},{96,80},{112,96},{128,112},... | collective-permute-start | bytes 24584 | tf_op jit(solution)/shard_map/ppermute | solution.py:27
  200.8 4.8 %collective-permute-start.25 = (f32[1,16,128]{2,1,0:T(8,128)S(1)}, f32[1,16,128]{2,1,0:T(8,128)S(1)}, u32[]{:S(2)}, u32[]{:S(2)}) collective-permute-start(f32[1,16,128]{2,1,0:T(8,128)S(1)} %get-tuple-element.61), channel_id=1, source_target_pairs={{0,16},{16,32},{32,48},{48,64},{64,80},{80,96},{96,112},{112,128},... | collective-permute-start | bytes 24584 | tf_op jit(solution)/shard_map/ppermute | solution.py:25
  205.6 13.1 %collective-permute-start.26 = (f32[34,1,128]{2,1,0:T(1,128)S(1)}, f32[34,1,128]{2,1,0:T(1,128)S(1)}, u32[]{:S(2)}, u32[]{:S(2)}) collective-permute-start(f32[34,1,128]{2,1,0:T(1,128)S(1)} %get-tuple-element.48), channel_id=1, source_target_pairs={{2,0},{4,2},{6,4},{8,6},{10,8},{12,10},{14,12},{3,1},{5,3},{7,5},{... | collective-permute-start | bytes 52232 | tf_op jit(solution)/shard_map/ppermute | solution.py:27
  207.5 12.1 %collective-permute-start.27 = (f32[34,1,128]{2,1,0:T(1,128)S(1)}, f32[34,1,128]{2,1,0:T(1,128)S(1)}, u32[]{:S(2)}, u32[]{:S(2)}) collective-permute-start(f32[34,1,128]{2,1,0:T(1,128)S(1)} %get-tuple-element.47), channel_id=1, source_target_pairs={{0,2},{2,4},{4,6},{6,8},{8,10},{10,12},{12,14},{1,3},{3,5},{5,7},{... | collective-permute-start | bytes 52232 | tf_op jit(solution)/shard_map/ppermute | solution.py:25
  219.9 8.8 %collective-permute-start.28 = (f32[34,18,1]{2,1,0:T(8,128)S(1)}, f32[34,18,1]{2,1,0:T(8,128)S(1)}, u32[]{:S(2)}, u32[]{:S(2)}) collective-permute-start(f32[34,18,1]{2,1,0:T(8,128)S(1)} %get-tuple-element.33), channel_id=1, source_target_pairs={{1,0},{3,2},{5,4},{7,6},{9,8},{11,10},{13,12},{15,14},{17,16},{19,... | collective-permute-start | bytes 7352 | tf_op jit(solution)/shard_map/ppermute | solution.py:27
  221.2 9.0 %collective-permute-start.29 = (f32[34,18,1]{2,1,0:T(8,128)S(1)}, f32[34,18,1]{2,1,0:T(8,128)S(1)}, u32[]{:S(2)}, u32[]{:S(2)}) collective-permute-start(f32[34,18,1]{2,1,0:T(8,128)S(1)} %get-tuple-element.34), channel_id=1, source_target_pairs={{0,1},{2,3},{4,5},{6,7},{8,9},{10,11},{12,13},{14,15},{16,17},{18,... | collective-permute-start | bytes 7352 | tf_op jit(solution)/shard_map/ppermute | solution.py:25
  230.6 5.8 %collective-permute-start.30 = (f32[1,16,128]{2,1,0:T(8,128)S(1)}, f32[1,16,128]{2,1,0:T(8,128)S(1)}, u32[]{:S(2)}, u32[]{:S(2)}) collective-permute-start(f32[1,16,128]{2,1,0:T(8,128)S(1)} %get-tuple-element.60), channel_id=1, source_target_pairs={{16,0},{32,16},{48,32},{64,48},{80,64},{96,80},{112,96},{128,112},... | collective-permute-start | bytes 24584 | tf_op jit(solution)/shard_map/ppermute | solution.py:27
  231.9 5.3 %collective-permute-start.31 = (f32[1,16,128]{2,1,0:T(8,128)S(1)}, f32[1,16,128]{2,1,0:T(8,128)S(1)}, u32[]{:S(2)}, u32[]{:S(2)}) collective-permute-start(f32[1,16,128]{2,1,0:T(8,128)S(1)} %get-tuple-element.59), channel_id=1, source_target_pairs={{0,16},{16,32},{32,48},{48,64},{64,80},{80,96},{96,112},{112,128},... | collective-permute-start | bytes 24584 | tf_op jit(solution)/shard_map/ppermute | solution.py:25
  237.3 10.3 %collective-permute-start.32 = (f32[34,1,128]{2,1,0:T(1,128)S(1)}, f32[34,1,128]{2,1,0:T(1,128)S(1)}, u32[]{:S(2)}, u32[]{:S(2)}) collective-permute-start(f32[34,1,128]{2,1,0:T(1,128)S(1)} %get-tuple-element.46), channel_id=1, source_target_pairs={{2,0},{4,2},{6,4},{8,6},{10,8},{12,10},{14,12},{3,1},{5,3},{7,5},{... | collective-permute-start | bytes 52232 | tf_op jit(solution)/shard_map/ppermute | solution.py:27
  239.2 9.2 %collective-permute-start.33 = (f32[34,1,128]{2,1,0:T(1,128)S(1)}, f32[34,1,128]{2,1,0:T(1,128)S(1)}, u32[]{:S(2)}, u32[]{:S(2)}) collective-permute-start(f32[34,1,128]{2,1,0:T(1,128)S(1)} %get-tuple-element.45), channel_id=1, source_target_pairs={{0,2},{2,4},{4,6},{6,8},{8,10},{10,12},{12,14},{1,3},{3,5},{5,7},{... | collective-permute-start | bytes 52232 | tf_op jit(solution)/shard_map/ppermute | solution.py:25
  248.7 8.9 %collective-permute-start.34 = (f32[34,18,1]{2,1,0:T(8,128)S(1)}, f32[34,18,1]{2,1,0:T(8,128)S(1)}, u32[]{:S(2)}, u32[]{:S(2)}) collective-permute-start(f32[34,18,1]{2,1,0:T(8,128)S(1)} %get-tuple-element.31), channel_id=1, source_target_pairs={{1,0},{3,2},{5,4},{7,6},{9,8},{11,10},{13,12},{15,14},{17,16},{19,... | collective-permute-start | bytes 7352 | tf_op jit(solution)/shard_map/ppermute | solution.py:27
  250.0 9.1 %collective-permute-start.35 = (f32[34,18,1]{2,1,0:T(8,128)S(1)}, f32[34,18,1]{2,1,0:T(8,128)S(1)}, u32[]{:S(2)}, u32[]{:S(2)}) collective-permute-start(f32[34,18,1]{2,1,0:T(8,128)S(1)} %get-tuple-element.32), channel_id=1, source_target_pairs={{0,1},{2,3},{4,5},{6,7},{8,9},{10,11},{12,13},{14,15},{16,17},{18,... | collective-permute-start | bytes 7352 | tf_op jit(solution)/shard_map/ppermute | solution.py:25
  259.5 5.8 %collective-permute-start.36 = (f32[1,16,128]{2,1,0:T(8,128)S(1)}, f32[1,16,128]{2,1,0:T(8,128)S(1)}, u32[]{:S(2)}, u32[]{:S(2)}) collective-permute-start(f32[1,16,128]{2,1,0:T(8,128)S(1)} %get-tuple-element.58), channel_id=1, source_target_pairs={{16,0},{32,16},{48,32},{64,48},{80,64},{96,80},{112,96},{128,112},... | collective-permute-start | bytes 24584 | tf_op jit(solution)/shard_map/ppermute | solution.py:27
  260.8 5.3 %collective-permute-start.37 = (f32[1,16,128]{2,1,0:T(8,128)S(1)}, f32[1,16,128]{2,1,0:T(8,128)S(1)}, u32[]{:S(2)}, u32[]{:S(2)}) collective-permute-start(f32[1,16,128]{2,1,0:T(8,128)S(1)} %get-tuple-element.57), channel_id=1, source_target_pairs={{0,16},{16,32},{32,48},{48,64},{64,80},{80,96},{96,112},{112,128},... | collective-permute-start | bytes 24584 | tf_op jit(solution)/shard_map/ppermute | solution.py:25
  266.1 10.1 %collective-permute-start.38 = (f32[34,1,128]{2,1,0:T(1,128)S(1)}, f32[34,1,128]{2,1,0:T(1,128)S(1)}, u32[]{:S(2)}, u32[]{:S(2)}) collective-permute-start(f32[34,1,128]{2,1,0:T(1,128)S(1)} %get-tuple-element.44), channel_id=1, source_target_pairs={{2,0},{4,2},{6,4},{8,6},{10,8},{12,10},{14,12},{3,1},{5,3},{7,5},{... | collective-permute-start | bytes 52232 | tf_op jit(solution)/shard_map/ppermute | solution.py:27
  268.1 9.0 %collective-permute-start.39 = (f32[34,1,128]{2,1,0:T(1,128)S(1)}, f32[34,1,128]{2,1,0:T(1,128)S(1)}, u32[]{:S(2)}, u32[]{:S(2)}) collective-permute-start(f32[34,1,128]{2,1,0:T(1,128)S(1)} %get-tuple-element.43), channel_id=1, source_target_pairs={{0,2},{2,4},{4,6},{6,8},{8,10},{10,12},{12,14},{1,3},{3,5},{5,7},{... | collective-permute-start | bytes 52232 | tf_op jit(solution)/shard_map/ppermute | solution.py:25
  277.4 8.9 %collective-permute-start.40 = (f32[34,18,1]{2,1,0:T(8,128)S(1)}, f32[34,18,1]{2,1,0:T(8,128)S(1)}, u32[]{:S(2)}, u32[]{:S(2)}) collective-permute-start(f32[34,18,1]{2,1,0:T(8,128)S(1)} %get-tuple-element.29), channel_id=1, source_target_pairs={{1,0},{3,2},{5,4},{7,6},{9,8},{11,10},{13,12},{15,14},{17,16},{19,... | collective-permute-start | bytes 7352 | tf_op jit(solution)/shard_map/ppermute | solution.py:27
  278.7 9.1 %collective-permute-start.41 = (f32[34,18,1]{2,1,0:T(8,128)S(1)}, f32[34,18,1]{2,1,0:T(8,128)S(1)}, u32[]{:S(2)}, u32[]{:S(2)}) collective-permute-start(f32[34,18,1]{2,1,0:T(8,128)S(1)} %get-tuple-element.30), channel_id=1, source_target_pairs={{0,1},{2,3},{4,5},{6,7},{8,9},{10,11},{12,13},{14,15},{16,17},{18,... | collective-permute-start | bytes 7352 | tf_op jit(solution)/shard_map/ppermute | solution.py:25
  288.2 1.7 copy-start.2
where the time goes:
time: 462 us; the launch traced here: 459 us
  starting transfers between devices  179 us (39%)
  blocking collectives  158 us (34%)
  waiting for transfers between devices  83 us (18%)
  local copies, waits for them, and re-layouts  17.5 us (4%)
  other arithmetic  10.7 us (2%)
  matrix products  6.02 us (1%)
  between operations  4.72 us (1%)
    psum x1, blocking collectives, body(): lax.psum((jnp.sum(delta * resid_b), jnp.sum(delta * delta), jnp.sum(resid...  115 us
    ppermute x21, starting transfers between devices, with_halo(): lax.ppermute(tail, axis, [(i, (i + 1) % count) for i in range(ends)])  105 us
    ppermute x21, starting transfers between devices, with_halo(): lax.ppermute(head, axis, [((i + 1) % count, i) for i in range(ends)])  44.6 us
    ppermute x21, waiting for transfers between devices, with_halo(): lax.ppermute(head, axis, [((i + 1) % count, i) for i in range(ends)])  38.4 us
    all_to_all x1, blocking collectives, couple(): lax.all_to_all(sending.reshape(6, dom_count, capacity), 'dom', split_axis...  28 us
    all_to_all x1, starting transfers between devices, couple(): lax.all_to_all(sending.reshape(6, dom_count, capacity), 'dom', split_axis...  25.3 us
    ppermute x21, waiting for transfers between devices, with_halo(): lax.ppermute(tail, axis, [(i, (i + 1) % count) for i in range(ends)])  20.7 us
    all_to_all x1, blocking collectives, couple(): lax.all_to_all(returned.reshape(3, dom_count, capacity), 'dom', split_axi...  15.3 us
  transfers between devices with their start and end apart: 44, of which 30 were waited for; matrix products, arithmetic and copies ran while one was open for 1% of the time, Pallas kernels for 0%

commit v1 on v0

v1 whole, which is shorter than its diff:
```python
import math

import jax
import jax.numpy as jnp
from jax import lax
from jax.experimental import pallas as pl
from jax.experimental.pallas import tpu as pltpu
from jax.sharding import PartitionSpec as P

SWEEPS = 4
DOM, SUB, LANE = 64, 8, 2
CX, CY, CZ = 32, 16, 128
PTS, NS, CAP = 256, 512, 8
RX, RY = CX + 8, CY + 8
WIDE = 16

source_gain = 16.0
relaxation = 0.5
inv_radius_sq = 11.111111
epsilon = 1e-06

f32, bf16, i32 = jnp.float32, jnp.bfloat16, jnp.int32
NN = (((1,), (0,)), ((), ()))
NT = (((1,), (1,)), ((), ()))


def pieces(x, count):
    parts = []
    for _ in range(count - 1):
        head = x.astype(bf16)
        parts.append(head)
        x = x - head.astype(f32)
    parts.append(x.astype(bf16))
    return parts


def mxu(a, b, dims):
    return lax.dot_general(a, b, dims, preferred_element_type=f32)


def ones_at(rows, index):
    at = lax.broadcasted_iota(i32, (rows, index.shape[1]), 0)
    return at == index


def as_ones(mask):
    return jnp.where(mask, 1.0, 0.0).astype(bf16)


def spread(row_mask, z, values):
    weights = jnp.where(ones_at(CZ, z), values, 0.0)
    rows = as_ones(row_mask)
    total = None
    for part in pieces(weights, 3):
        term = mxu(rows, part, NT)
        total = term if total is None else total + term
    return total


def halves(row):
    return row[:, 0:128], row[:, 128:256]


def joined(ref_rows):
    return jnp.concatenate([ref_rows[0:1], ref_rows[1:2]], axis=1)


def start_kernel(rhs, coef, pold, cell, part, nrm, disp, src, rden, low, high, slot):
    points = cell[...]
    values = source_gain * jnp.sum(disp[...] * nrm[...], axis=0, keepdims=True)
    added = spread(ones_at(CX * CY, points >> 7), points & 127, values)
    src[...] = rhs[...] + added.reshape(CX, CY, CZ)
    rden[...] = 1.0 / (6.0 + coef[...])
    owner = ones_at(DOM, part[...])
    earlier = lax.broadcasted_iota(i32, (PTS, PTS), 0) < lax.broadcasted_iota(i32, (PTS, PTS), 1)
    before = mxu(as_ones(owner), as_ones(earlier), NN)
    rank = jnp.sum(jnp.where(owner, before, 0.0), axis=0, keepdims=True)
    slots = part[...].astype(f32) * CAP + rank
    slot[...] = slots
    for out, first in ((low, 0), (high, CX)):
        base3 = 0 if first == 0 else CX - 3
        base4 = 0 if first == 0 else CX - 4
        out[0:3] = src[base3 : base3 + 3]
        out[3:6] = rden[base3 : base3 + 3]
        out[6:10] = pold[base4 : base4 + 4]
        out[10] = jnp.zeros((CY, CZ), f32)
        for at, row in enumerate((*halves(points.astype(f32)), *halves(slots))):
            out[10, at : at + 1, :] = row


def sub_kernel(src, rden, pold, cell, fromhigh, fromlow, low, high):
    for out, base3, base4 in ((low, 0, 0), (high, CY - 3, CY - 4)):
        for field, own, width, base in ((0, src, 3, base3), (3, rden, 3, base3), (6, pold, 4, base4)):
            for k in range(width):
                y = base + k
                out[field + k, 0:CX, :] = own[:, y, :]
                rows_high = fromhigh[field : field + width, y, :]
                rows_low = fromlow[field : field + width, y, :]
                if width == 3:
                    gap = jnp.zeros((2, CZ), f32)
                    rest = jnp.concatenate([rows_high, gap, rows_low], axis=0)
                else:
                    rest = jnp.concatenate([rows_high, rows_low], axis=0)
                out[field + k, CX:RX, :] = rest
        out[10] = jnp.zeros((RX, CZ), f32)
        a, b = halves(cell[...].astype(f32))
        out[10, 0:1, :] = a
        out[10, 1:2, :] = b
        out[10, 2:4, :] = fromhigh[10, 0:2, :]
        out[10, 4:6, :] = fromlow[10, 0:2, :]


def lane_kernel(place, src, rden, pold, cell, fromhigh, fromlow, subhigh, sublow, esrc, erden, epold, strips, meta):
    for field, own, width, ext in ((0, src, 3, esrc), (3, rden, 3, erden), (6, pold, 4, epold)):
        ext[0:CX, 0:CY, :] = own[...]
        ext[CX : CX + width, 0:CY, :] = fromhigh[field : field + width]
        ext[RX - width : RX, 0:CY, :] = fromlow[field : field + width]
        if width == 3:
            ext[CX + 3 : CX + 5, 0:CY, :] = jnp.zeros((2, CY, CZ), f32)
            ext[:, CY + 3, :] = jnp.zeros((RX, CZ), f32)
            ext[:, CY + 4, :] = jnp.zeros((RX, CZ), f32)
        for k in range(width):
            ext[:, CY + k, :] = subhigh[field + k]
            ext[:, RY - width + k, :] = sublow[field + k]
    lane = place[1]
    shift = jnp.where(lane == 0, 4, 0)
    at = lax.broadcasted_iota(i32, (RY, CZ), 1)
    group = RX // 8
    for x in range(group):
        total = jnp.zeros((RY, CZ), f32)
        for k in range(8):
            for field, ext in enumerate((esrc, erden, epold)):
                lo = 16 * k + 4 * field
                moved = pltpu.roll(ext[k * group + x], lax.rem(lo + shift, 128), 1)
                total = jnp.where((at >= lo) & (at < lo + 4), moved, total)
        strips[x] = total
    meta[...] = jnp.zeros((RY, CZ), f32)
    a, b = halves(cell[...].astype(f32))
    meta[0:1, :] = a
    meta[1:2, :] = b
    meta[2:4, :] = fromhigh[10, 0:2, :]
    meta[4:6, :] = fromlow[10, 0:2, :]
    meta[6:12, :] = subhigh[10, 0:6, :]
    meta[12:18, :] = sublow[10, 0:6, :]
    strips[group] = meta[...]


def sweeps(source, scale, first, even, odd):
    held = first
    for number in range(SWEEPS):
        out = even if number % 2 == 0 else odd
        now = held

        def chunk(i, _, now=now, out=out):
            base = i * 8
            window = [now[lax.rem(base + RX - 1 + k, RX)] for k in range(10)]
            for k in range(8):
                x = base + k
                here = window[k + 1]
                total = window[k + 2] + window[k]
                total = total + (pltpu.roll(here, RY - 1, 0) + pltpu.roll(here, 1, 0))
                total = total + (pltpu.roll(here, 2 * CZ - 1, 1) + pltpu.roll(here, 1, 1))
                out[x] = (source[x] + total) * scale[x]
            return 0

        lax.fori_loop(0, RX // 8, chunk, 0)
        held = out
    return held


def at_points(pressure, points):
    flat = pressure.reshape(CX * CY, CZ).T
    rows = as_ones(ones_at(CX * CY, points >> 7))
    total = None
    for part in pieces(flat, 3):
        term = mxu(part, rows, NN)
        total = term if total is None else total + term
    return jnp.sum(jnp.where(ones_at(CZ, points & 127), total, 0.0), axis=0, keepdims=True)


def to_slots(values, slots):
    rank = slots & 7
    filler = [jnp.zeros((1, PTS), f32)] * (WIDE - len(values))
    block = jnp.concatenate(list(values) + filler, axis=0)
    stacked = jnp.concatenate([jnp.where(rank == r, block, 0.0) for r in range(CAP)], axis=0)
    owner = as_ones(ones_at(DOM, slots >> 3))
    total = None
    for part in pieces(stacked, 3):
        term = mxu(owner, part, NT)
        total = term if total is None else total + term
    return total


def from_slots(arrived, slots):
    rank = slots & 7
    owner = as_ones(ones_at(DOM, slots >> 3))
    flat = arrived.T
    total = None
    for part in pieces(flat, 3):
        term = mxu(part, owner, NN)
        total = term if total is None else total + term
    found = jnp.zeros((WIDE, PTS), f32)
    for r in range(CAP):
        found = found + jnp.where(rank == r, total[r * WIDE : (r + 1) * WIDE], 0.0)
    return found


def forces_at(pressure, points, nrm):
    press = at_points(pressure, points)
    return [press * nrm[c : c + 1, :] for c in range(3)]


def first_fluid_kernel(
    place, esrc, erden, epold, strips, cell, nrm, coords, disp, slot, fsrc, frden, fpold, sending, even, odd
):
    lane = place[1]
    at = lax.broadcasted_iota(i32, (RY, CZ), 1)
    keep = jnp.where(lane == 0, at, CZ - 1 - at) < 4
    group = RX // 8
    for field, (ext, full) in enumerate(((esrc, fsrc), (erden, frden), (epold, fpold))):
        full[:, :, 0:CZ] = ext[...]
        for x in range(group):
            packed = strips[x]
            for k in range(8):
                lo = 16 * k + 4 * field
                moved = pltpu.roll(packed, lax.rem(256 - lo - 4 * lane, 128), 1)
                full[k * group + x, :, CZ : 2 * CZ] = jnp.where(keep, moved, 0.0)
    held = sweeps(fsrc, frden, fpold, even, odd)
    slots = slot[...].astype(i32)
    values = forces_at(held[0:CX, 0:CY, 0:CZ], cell[...], nrm)
    values += [coords[c : c + 1, :] for c in range(3)]
    values += [disp[c : c + 1, :] for c in range(3)]
    values += [nrm[c : c + 1, :] for c in range(3)]
    values += [jnp.ones((1, PTS), f32)]
    sending[...] = to_slots(values, slots)


def second_fluid_kernel(
    place, fsrc, frden, fpold, arrived, meta, strips, cell, nrm, slot, pressure, sending, source, even, odd
):
    sub, lane = place[0], place[1]
    source[...] = fsrc[...]
    for tile in range(2):
        cells_of = meta if tile == 0 else strips.at[RX // 8]
        other = jnp.where(tile == 0, lane, 1 - lane)
        lanes = slice(tile * CZ, (tile + 1) * CZ)
        beside_x = jnp.zeros((8 * CY, CZ), f32)
        beside_y = jnp.zeros((CX * 8, CZ), f32)
        corner = jnp.zeros((64, CZ), f32)
        for dy, off_y in enumerate((0, 1, -1)):
            wanted = sub + off_y
            inside = (wanted >= 0) & (wanted < SUB)
            block = arrived[lax.rem(wanted + SUB, SUB) * LANE + other]
            block = jnp.where(inside, block, 0.0)
            for dx in range(3):
                values = joined(block[2 * dx : 2 * dx + 2])
                at = (dy * 3 + dx) * 2
                points = joined(cells_of[at : at + 2, :]).astype(i32)
                x, y, z = points >> 11, (points >> 7) & 15, points & 127
                if dx == 1:
                    x = jnp.where(x < 3, x, -1000)
                elif dx == 2:
                    x = jnp.where(x >= CX - 3, x - (CX - 8), -1000)
                if dy == 1:
                    y = jnp.where(y < 3, y, -1000000)
                elif dy == 2:
                    y = jnp.where(y >= CY - 3, y - (CY - 8), -1000000)
                if dx == 0 and dy == 0:
                    added = spread(ones_at(CX * CY, points >> 7), z, values)
                    source[0:CX, 0:CY, lanes] += added.reshape(CX, CY, CZ)
                elif dy == 0:
                    beside_x = beside_x + spread(ones_at(8 * CY, x * CY + y), z, values)
                elif dx == 0:
                    beside_y = beside_y + spread(ones_at(CX * 8, x * 8 + y), z, values)
                else:
                    corner = corner + spread(ones_at(64, x * 8 + y), z, values)
        source[CX:RX, 0:CY, lanes] += beside_x.reshape(8, CY, CZ)
        source[0:CX, CY:RY, lanes] += beside_y.reshape(CX, 8, CZ)
        source[CX:RX, CY:RY, lanes] += corner.reshape(8, 8, CZ)
    held = sweeps(source, frden, fpold, even, odd)
    own = held[0:CX, 0:CY, 0:CZ]
    pressure[...] = own
    sending[...] = to_slots(forces_at(own, cell[...], nrm), slot[...].astype(i32))


def by_slot(received):
    flat = received.T
    return jnp.concatenate([flat[r * WIDE : (r + 1) * WIDE] for r in range(CAP)], axis=1)


def by_row(values):
    flat = jnp.concatenate([values[:, r * DOM : (r + 1) * DOM] for r in range(CAP)], axis=0)
    return flat.T


def product(left, head, tail, dims):
    a, b = pieces(left, 2)
    rows = left.shape[0]
    both = mxu(jnp.concatenate([a, b], axis=0), head, dims)
    return both[:rows] + both[rows:] + mxu(a, tail, dims)


def mapped_back(forces, khead, ktail, shell):
    loading = product(forces, khead, ktail, NN) * (1.0 / math.sqrt(PTS))
    shead, stail = pieces(shell, 2)
    displaced = loading + product(loading, shead, stail, NN)
    return product(displaced, khead, ktail, NT) * (1.0 / math.sqrt(NS))


def first_structure_kernel(received, nodes, shell, returned, mapped, khead, ktail):
    for r in range(CAP):
        distance = None
        for c in range(3):
            lane = r * WIDE + 3 + c
            gap = received[:, lane : lane + 1] - nodes[c : c + 1, :]
            distance = gap * gap if distance is None else distance + gap * gap
        weight = jnp.exp(-distance * inv_radius_sq)
        head, tail = pieces(weight, 2)
        khead[r * DOM : (r + 1) * DOM, :] = head
        ktail[r * DOM : (r + 1) * DOM, :] = tail
    held = by_slot(received[...])
    back = mapped_back(held[0:WIDE], khead[...], ktail[...], shell[...])
    mapped[...] = back
    moved = (source_gain * relaxation) * jnp.sum(held[9:12] * (back[0:3] - held[6:9]), axis=0, keepdims=True)
    rows = jnp.concatenate([moved, jnp.zeros((WIDE - 1, NS), f32)], axis=0)
    own = by_row(rows)
    at = lax.broadcasted_iota(i32, own.shape, 0)
    above = jnp.where(at == DOM - 1, 0.0, pltpu.roll(own, DOM - 1, 0))
    below = jnp.where(at == 0, 0.0, pltpu.roll(own, 1, 0))
    returned[...] = own + pltpu.roll(above, 1, 1) + pltpu.roll(below, 2, 1)


def second_structure_kernel(received, before, mapped, khead, ktail, shell, returned):
    forces = by_slot(received[...])
    held = by_slot(before[...])
    back = mapped_back(forces, khead[...], ktail[...], shell[...])
    t0, t1, d0, used = mapped[0:3, :], back[0:3], held[6:9], held[12:13]
    r0 = t0 - d0
    r1 = t1 - (d0 + relaxation * r0)
    delta = r1 - r0
    sums = []
    for term in (delta * r1, delta * delta, r1 * r1):
        inner = jnp.sum(term * used, axis=0, keepdims=True)
        sums.append(jnp.broadcast_to(jnp.sum(inner, axis=1, keepdims=True), (1, NS)))
    rows = jnp.concatenate([t1, t0, *sums, jnp.zeros((WIDE - 9, NS), f32)], axis=0)
    returned[...] = by_row(rows)


def hand_out_kernel(arrived, slot, high, low, out):
    held = arrived[...]
    rows = []
    for block in range(3):
        if block == 0:
            slots = slot[...]
        else:
            slots = joined((high if block == 1 else low)[10, 2:4, :])
        found = from_slots(held, slots.astype(i32))
        rows += halves(found[block : block + 1])
    rows += [jnp.zeros((2, 128), f32)]
    payload = jnp.concatenate(rows, axis=0)
    for k in range(SUB * LANE):
        out[k] = payload


def arrive_kernel(arrived, slot, found, out):
    held = arrived[...]
    found[...] = from_slots(held, slot[...].astype(i32))
    total = jnp.sum(held, axis=0, keepdims=True)
    for k in range(SUB * LANE):
        out[k : k + 1, :] = total


def finish_kernel(found, sums, disp, rms):
    total = jnp.sum(sums[...], axis=0, keepdims=True)
    vr, vv, rr = total[:, 6:7], total[:, 7:8], total[:, 8:9]
    t1, t0 = found[0:3, :], found[3:6, :]
    disp[...] = t1 - (vr / (vv + epsilon)) * (t1 - t0)
    count = 3.0 * PTS * DOM * SUB * LANE
    rms[...] = jnp.sqrt(rr / count)


def shape(*dims, dtype=f32):
    return jax.ShapeDtypeStruct(dims, dtype)


def call(kernel, outs, args, scratch=(), scalars=0, name=None):
    specs = [pl.BlockSpec(memory_space=pltpu.SMEM)] * scalars
    specs += [pl.BlockSpec(memory_space=pltpu.VMEM)] * (len(args) - scalars)
    return pl.pallas_call(
        kernel,
        out_shape=outs,
        in_specs=specs,
        out_specs=jax.tree.map(lambda _: pl.BlockSpec(memory_space=pltpu.VMEM), outs),
        scratch_shapes=list(scratch),
        compiler_params=pltpu.CompilerParams(vmem_limit_bytes=40 * 1024 * 1024),
        name=name,
    )(*args)


def body(rhs, coef, pold, cell_index, nrm, coords, partner, nodes, shell, disp):
    place = jnp.stack([lax.axis_index("sub"), lax.axis_index("lane")]).astype(i32)
    cell = cell_index.reshape(1, PTS)
    part = partner.reshape(1, PTS)
    block, field = shape(CX, CY, CZ), shape(RX, RY, 2 * CZ)
    row = shape(DOM, CAP * WIDE)

    def pair(low, high, axis):
        count = lax.axis_size(axis)
        fromhigh = lax.ppermute(low, axis, [(i + 1, i) for i in range(count - 1)])
        fromlow = lax.ppermute(high, axis, [(i, i + 1) for i in range(count - 1)])
        return fromhigh, fromlow

    def across(rows):
        return lax.all_to_all(rows, "dom", 0, 0, tiled=True)

    slab, face = shape(11, CY, CZ), shape(11, RX, CZ)
    src, rden, low, high, slot = call(
        start_kernel, (block, block, slab, slab, shape(1, PTS)), (rhs, coef, pold, cell, part, nrm, disp), name="start"
    )
    fromhigh, fromlow = pair(low, high, "dom")
    low, high = call(sub_kernel, (face, face), (src, rden, pold, cell, fromhigh, fromlow), name="sub_faces")
    subhigh, sublow = pair(low, high, "sub")
    half = shape(RX, RY, CZ)
    esrc, erden, epold, strips, meta = call(
        lane_kernel,
        (half, half, half, shape(RX // 8 + 1, RY, CZ), shape(RY, CZ)),
        (place, src, rden, pold, cell, fromhigh, fromlow, subhigh, sublow),
        scalars=1,
        name="lane_faces",
    )
    strips = lax.ppermute(strips, "lane", [(0, 1), (1, 0)])
    grids = [pltpu.VMEM((RX, RY, 2 * CZ), f32)] * 2
    fsrc, frden, fpold, sending = call(
        first_fluid_kernel,
        (field, field, field, row),
        (place, esrc, erden, epold, strips, cell, nrm, coords, disp, slot),
        grids,
        scalars=1,
        name="first_fluid",
    )
    received = across(sending)
    square = shape(NS, NS, dtype=bf16)
    returned, mapped, khead, ktail = call(
        first_structure_kernel, (row, shape(WIDE, NS), square, square), (received, nodes, shell), name="first_structure"
    )
    arrived = across(returned)
    (spread_out,) = call(
        hand_out_kernel, (shape(SUB * LANE, 8, 128),), (arrived, slot, fromhigh, fromlow), name="hand_out"
    )
    values = lax.all_to_all(spread_out, ("sub", "lane"), 0, 0, tiled=True)
    pressure, sending = call(
        second_fluid_kernel,
        (block, row),
        (place, fsrc, frden, fpold, values, meta, strips, cell, nrm, slot),
        grids + [pltpu.VMEM((RX, RY, 2 * CZ), f32)],
        scalars=1,
        name="second_fluid",
    )
    again = across(sending)
    (returned,) = call(
        second_structure_kernel, (row,), (again, received, mapped, khead, ktail, shell), name="second_structure"
    )
    arrived = across(returned)
    found, sums = call(
        arrive_kernel, (shape(WIDE, PTS), shape(SUB * LANE, 128)), (arrived, slot), name="arrive"
    )
    sums = lax.all_to_all(sums, ("sub", "lane"), 0, 0, tiled=True)
    disp_new, rms = call(finish_kernel, (shape(3, PTS), shape(1, 1)), (found, sums), name="finish")
    return pressure, disp_new, rms.reshape(())


def solution(mesh):
    every = ("dom", "sub", "lane")
    grid, points = P(*every), P(None, every)
    return jax.shard_map(
        body,
        mesh=mesh,
        in_specs=(grid, grid, grid, P(every), points, points, P(every, None), points, P(every, None), points),
        out_specs=(grid, points, P()),
        check_vma=False,
    )
```

time: 462 us -> 165 us (0.36)
  starting transfers between devices: 179 us -> 26.5 us
  waiting for transfers between devices: 83 us -> 7.52 us
  blocking collectives: 158 us -> 106 us
  Pallas kernels: 0 us -> 18.5 us
  local copies, waits for them, and re-layouts: 17.5 us -> 4.93 us
  other arithmetic: 10.7 us -> 0.08 us
  matrix products: 6.02 us -> 0 us
    ppermute x42 -> x5, starting transfers between devices: 149 us -> 26.5 us  [the longest x2 16.1 us: pair(): fromhigh = lax.ppermute(low, axis, [(i + 1, i) for i in range(count - 1)])]
    psum x1 -> x0, blocking collectives: 115 us -> none  [body(): lax.psum((jnp.sum(delta * resid_b), jnp.sum(delta * delta), jnp.sum(resid...]
    all_to_all x2 -> x6, blocking collectives: 43.3 us -> 106 us  [the longest x4 73.4 us: across(): return lax.all_to_all(rows, 'dom', 0, 0, tiled=True)]
    ppermute x42 -> x5, waiting for transfers between devices: 59.1 us -> 7.52 us  [the longest x2 4.35 us: pair(): fromlow = lax.ppermute(high, axis, [(i, i + 1) for i in range(count - 1)])]
    all_to_all x2 -> x0, starting transfers between devices: 30.1 us -> none  [the longest x1 25.3 us: couple(): lax.all_to_all(sending.reshape(6, dom_count, capacity), 'dom', split_axis...]
    all_to_all x2 -> x0, waiting for transfers between devices: 23.8 us -> none  [the longest x1 12.3 us: couple(): lax.all_to_all(sending.reshape(6, dom_count, capacity), 'dom', split_axis...]
    pallas_call x0 -> x10, Pallas kernels: none -> 18.5 us  [call(): pl.pallas_call(kernel, out_shape=outs, in_specs=specs, out_specs=jax.tree...]
    dot_general x6 -> x0, matrix products: 6.02 us -> none  [the longest x2 2.7 us: structure(): jnp.dot(displaced, kernel.T, precision=lax.Precision.HIGHEST)]
  transfers between devices with their start and end apart: 44 -> 5, of which waited for: 30 -> 3; matrix products, arithmetic and copies ran while one was open for 1% -> 0% of each run, Pallas kernels for 0% -> 0%
where the time goes in v1:
time: 165 us; the launch traced here: 164 us
  blocking collectives  106 us (64%)
  starting transfers between devices  26.5 us (16%)
  Pallas kernels  18.5 us (11%)
  waiting for transfers between devices  7.52 us (5%)
  local copies, waits for them, and re-layouts  4.93 us (3%)
    all_to_all x4, blocking collectives, across(): return lax.all_to_all(rows, 'dom', 0, 0, tiled=True)  73.4 us
    all_to_all x1, blocking collectives, body(): values = lax.all_to_all(spread_out, ('sub', 'lane'), 0, 0, tiled=True)  20.7 us
    pallas_call x10, Pallas kernels, call(): pl.pallas_call(kernel, out_shape=outs, in_specs=specs, out_specs=jax.tree...  18.5 us
    ppermute x2, starting transfers between devices, pair(): fromhigh = lax.ppermute(low, axis, [(i + 1, i) for i in range(count - 1)])  16.1 us
    all_to_all x1, blocking collectives, body(): sums = lax.all_to_all(sums, ('sub', 'lane'), 0, 0, tiled=True)  12.1 us
    ppermute x2, starting transfers between devices, pair(): fromlow = lax.ppermute(high, axis, [(i, i + 1) for i in range(count - 1)])  8.29 us
    unnamed x26, local copies, waits for them, and re-layouts  4.93 us
    ppermute x2, waiting for transfers between devices, pair(): fromlow = lax.ppermute(high, axis, [(i, i + 1) for i in range(count - 1)])  4.35 us
  transfers between devices with their start and end apart: 5, of which 3 were waited for; matrix products, arithmetic and copies ran while one was open for 0% of the time, Pallas kernels for 0%

profile of v1, /device:TPU:1, one launch (start us, length us, event | category | flops | bytes accessed | tf_op | source)
XLA Modules:
  0.0 164.5 jit_solution(396392978468508800)
XLA Ops:
  0.6 0.0 copy-start.12
  0.6 0.0 copy-start.7
  0.7 0.7 copy-done.12
  1.3 0.0 copy-done.7
  1.3 0.0 copy-start.1
  1.3 0.9 copy-done.1
  2.3 0.0 copy-start.3
  2.3 0.9 copy-done.3
  3.2 0.0 copy-start.4
  3.2 0.9 copy-done.4
  4.2 0.0 copy-start.5
  4.2 0.7 copy-done.5
  4.9 0.0 copy-start.8
  4.9 0.7 copy-done.8
  5.6 0.0 copy-start.2
  5.6 0.4 start.1
  6.0 1.3 collective-permute-start
  7.3 6.4 %collective-permute-start.1 = (f32[11,16,128]{2,1,0:T(8,128)S(1)}, f32[11,16,128]{2,1,0:T(8,128)S(1)}, u32[]{:S(2)}, u32[]{:S(2)}) collective-permute-start(f32[11,16,128]{2,1,0:T(8,128)S(1)} %get-tuple-element.32), channel_id=1, source_target_pairs={{0,16},{16,32},{32,48},{48,64},{64,80},{80,96},{96,112},{112,128},... | collective-permute-start | bytes 270344 | tf_op jit(solution)/shard_map/ppermute | solution.py:410
  13.7 0.0 collective-permute-done.fromhigh.high
  13.7 1.5 collective-permute-done.1.fromlow.low
  15.2 0.0 copy-done.2
  15.2 0.2 sub_faces.1
  15.4 14.8 %collective-permute-start.2 = (f32[11,40,128]{2,1,0:T(8,128)S(1)}, f32[11,40,128]{2,1,0:T(8,128)S(1)}, u32[]{:S(2)}, u32[]{:S(2)}) collective-permute-start(f32[11,40,128]{2,1,0:T(8,128)S(1)} %get-tuple-element.33), channel_id=1, source_target_pairs={{2,0},{4,2},{6,4},{8,6},{10,8},{12,10},{14,12},{3,1},{5,3},{7,5},{... | collective-permute-start | bytes 675848 | tf_op jit(solution)/shard_map/ppermute | solution.py:409
  30.2 1.9 %collective-permute-start.3 = (f32[11,40,128]{2,1,0:T(8,128)S(1)}, f32[11,40,128]{2,1,0:T(8,128)S(1)}, u32[]{:S(2)}, u32[]{:S(2)}) collective-permute-start(f32[11,40,128]{2,1,0:T(8,128)S(1)} %get-tuple-element.34), channel_id=1, source_target_pairs={{0,2},{2,4},{4,6},{6,8},{8,10},{10,12},{12,14},{1,3},{3,5},{5,7},{... | collective-permute-start | bytes 675848 | tf_op jit(solution)/shard_map/ppermute | solution.py:410
  32.2 0.1 pad_add_fusion.place
  32.3 0.0 collective-permute-done.2.subhigh
  32.3 2.8 %collective-permute-done.3.sublow = f32[11,40,128]{2,1,0:T(8,128)S(1)} collective-permute-done((f32[11,40,128]{2,1,0:T(8,128)S(1)}, f32[11,40,128]{2,1,0:T(8,128)S(1)}, u32[]{:S(2)}, u32[]{:S(2)}) %collective-permute-start.3) | collective-permute-done | bytes 225312 | tf_op jit(solution)/shard_map/ppermute | solution.py:410
  35.1 0.0 copy-start.6
  35.1 0.0 copy-start.9
  35.1 0.0 copy-start.11
  35.1 1.2 lane_faces.1
  36.3 0.0 copy-start
  36.3 2.1 %collective-permute-start.4 = (f32[6,24,128]{2,1,0:T(8,128)S(1)}, f32[6,24,128]{2,1,0:T(8,128)S(1)}, u32[]{:S(2)}, u32[]{:S(2)}) collective-permute-start(f32[6,24,128]{2,1,0:T(8,128)S(1)} %get-tuple-element.38), channel_id=1, source_target_pairs={{0,1},{1,0},{2,3},{3,2},{4,5},{5,4},{6,7},{7,6},{8,9},{9,8},{10,11... | collective-permute-start | bytes 221192 | tf_op jit(solution)/shard_map/ppermute | solution.py:431
  38.4 3.2 %collective-permute-done.4.strips = f32[6,24,128]{2,1,0:T(8,128)S(1)} collective-permute-done((f32[6,24,128]{2,1,0:T(8,128)S(1)}, f32[6,24,128]{2,1,0:T(8,128)S(1)}, u32[]{:S(2)}, u32[]{:S(2)}) %collective-permute-start.4) | collective-permute-done | bytes 73760 | tf_op jit(solution)/shard_map/ppermute | solution.py:431
  41.5 0.0 copy-done.6
  41.5 0.0 copy-done.9
  41.5 0.0 copy-done.11
  41.5 5.2 %first_fluid.1 = (f32[40,24,256]{2,1,0:T(8,128)S(1)}, f32[40,24,256]{2,1,0:T(8,128)S(1)}, f32[40,24,256]{2,1,0:T(8,128)S(1)}, f32[64,128]{1,0:T(8,128)S(1)}) custom-call(s32[2]{0:T(128)S(1)} %pad_add_fusion.place, f32[40,24,128]{2,1,0:T(8,128)S(1)} %get-tuple-element.35.esrc, f32[40,24,128]{2,1,0:T(8,128)S(1)} %get-tuple-element.36.erden, ...), custom_call_target="tpu_custom_call" | custom-call | tf_op jit(solution)/shard_map/first_fluid/pallas_call | solution.py:389
  46.8 0.0 copy-start.10
  46.8 29.5 %all_to_all.60 = f32[64,1,128]{2,1,0:T(1,128)S(1)} all-to-all(f32[64,1,128]{2,1,0:T(1,128)S(1)} %bitcast.33), channel_id=1, replica_groups=mesh['dom'=64,'sub'=8,'lane'=2] {'dom'}, dimensions={0} | all-to-all | bytes 65536 | tf_op jit(solution)/shard_map/all_to_all | solution.py:414
  76.3 0.0 copy-done
  76.3 0.0 copy-done.10
  76.3 1.7 %first_structure.1 = (f32[64,128]{1,0:T(8,128)S(1)}, f32[16,512]{1,0:T(8,128)S(1)}, bf16[512,512]{1,0:T(8,128)(2,1)S(1)}, bf16[512,512]{1,0:T(8,128)(2,1)S(1)}) custom-call(f32[64,128]{1,0:T(8,128)S(1)} %bitcast.25, f32[3,512]{1,0:T(4,128)S(1)} %copy-done.10, f32[512,512]{1,0:T(8,128)S(1)} %copy-done), custom_call_target="tpu_custom_call" | custom-call | tf_op jit(solution)/shard_map/first_structure/pallas_call | solution.py:389
  78.0 14.6 %all_to_all.61 = f32[64,1,128]{2,1,0:T(1,128)S(1)} all-to-all(f32[64,1,128]{2,1,0:T(1,128)S(1)} %bitcast.34), channel_id=1, replica_groups=mesh['dom'=64,'sub'=8,'lane'=2] {'dom'}, dimensions={0} | all-to-all | bytes 65536 | tf_op jit(solution)/shard_map/all_to_all | solution.py:414
  92.6 0.4 hand_out.1
  93.0 20.7 %all_to_all.62.arrived = f32[16,8,128]{2,1,0:T(8,128)S(1)} all-to-all(f32[16,8,128]{2,1,0:T(8,128)S(1)} %hand_out.1), channel_id=1, replica_groups=mesh['dom'=64,'sub'=8,'lane'=2] {'sub','lane'}, dimensions={0} | all-to-all | bytes 131072 | tf_op jit(solution)/shard_map/all_to_all | solution.py:450
  113.7 7.2 %second_fluid.1 = (f32[32,16,128]{2,1,0:T(8,128)}, f32[64,128]{1,0:T(8,128)S(1)}) custom-call(s32[2]{0:T(128)S(1)} %pad_add_fusion.place, f32[40,24,256]{2,1,0:T(8,128)S(1)} %get-tuple-element.40.fsrc, f32[40,24,256]{2,1,0:T(8,128)S(1)} %get-tuple-element.41.frden, f32[40,24,256]{2,1,0:T(8,128)S(1)} %get-tuple-element.42.fpold, ...), custom_call_target="tpu_custom_call" | custom-call | tf_op jit(solution)/shard_map/second_fluid/pallas_call | solution.py:389
  120.9 14.6 %all_to_all.63 = f32[64,1,128]{2,1,0:T(1,128)S(1)} all-to-all(f32[64,1,128]{2,1,0:T(1,128)S(1)} %bitcast.32), channel_id=1, replica_groups=mesh['dom'=64,'sub'=8,'lane'=2] {'dom'}, dimensions={0} | all-to-all | bytes 65536 | tf_op jit(solution)/shard_map/all_to_all | solution.py:414
  135.5 1.2 second_structure.1
  136.7 14.6 %all_to_all.64 = f32[64,1,128]{2,1,0:T(1,128)S(1)} all-to-all(f32[64,1,128]{2,1,0:T(1,128)S(1)} %bitcast.28), channel_id=1, replica_groups=mesh['dom'=64,'sub'=8,'lane'=2] {'dom'}, dimensions={0} | all-to-all | bytes 65536 | tf_op jit(solution)/shard_map/all_to_all | solution.py:414
  151.3 0.3 arrive.1
  151.6 12.1 %all_to_all.65 = f32[16,1,128]{2,1,0:T(1,128)S(1)} all-to-all(f32[16,1,128]{2,1,0:T(1,128)S(1)} %bitcast.40), channel_id=1, replica_groups=mesh['dom'=64,'sub'=8,'lane'=2] {'sub','lane'}, dimensions={0} | all-to-all | bytes 16384 | tf_op jit(solution)/shard_map/all_to_all | solution.py:467
  163.7 0.8 finish.1
Async XLA Ops:
  0.6 0.7 copy-start.12
  0.6 0.7 copy-start.7
  1.3 0.9 copy-start.1
  2.3 0.9 copy-start.3
  3.2 0.9 copy-start.4
  4.2 0.7 copy-start.5
  4.9 0.7 copy-start.8
  5.6 9.6 %copy-start.2 = (f32[32,16,128]{2,1,0:T(8,128)S(1)}, f32[32,16,128]{2,1,0:T(8,128)}, u32[]{:S(2)}) copy-start(f32[32,16,128]{2,1,0:T(8,128)} %pold.5) | copy-start | bytes 786436
  6.0 7.7 %collective-permute-start = (f32[11,16,128]{2,1,0:T(8,128)S(1)}, f32[11,16,128]{2,1,0:T(8,128)S(1)}, u32[]{:S(2)}, u32[]{:S(2)}) collective-permute-start(f32[11,16,128]{2,1,0:T(8,128)S(1)} %get-tuple-element.31), channel_id=1, source_target_pairs={{16,0},{32,16},{48,32},{64,48},{80,64},{96,80},{112,96},{128,112},... | collective-permute-start | bytes 270344 | tf_op jit(solution)/shard_map/ppermute | solution.py:409
  7.3 7.9 %collective-permute-start.1 = (f32[11,16,128]{2,1,0:T(8,128)S(1)}, f32[11,16,128]{2,1,0:T(8,128)S(1)}, u32[]{:S(2)}, u32[]{:S(2)}) collective-permute-start(f32[11,16,128]{2,1,0:T(8,128)S(1)} %get-tuple-element.32), channel_id=1, source_target_pairs={{0,16},{16,32},{32,48},{48,64},{64,80},{80,96},{96,112},{112,128},... | collective-permute-start | bytes 270344 | tf_op jit(solution)/shard_map/ppermute | solution.py:410
  15.4 16.8 %collective-permute-start.2 = (f32[11,40,128]{2,1,0:T(8,128)S(1)}, f32[11,40,128]{2,1,0:T(8,128)S(1)}, u32[]{:S(2)}, u32[]{:S(2)}) collective-permute-start(f32[11,40,128]{2,1,0:T(8,128)S(1)} %get-tuple-element.33), channel_id=1, source_target_pairs={{2,0},{4,2},{6,4},{8,6},{10,8},{12,10},{14,12},{3,1},{5,3},{7,5},{... | collective-permute-start | bytes 675848 | tf_op jit(solution)/shard_map/ppermute | solution.py:409
  30.2 4.8 %collective-permute-start.3 = (f32[11,40,128]{2,1,0:T(8,128)S(1)}, f32[11,40,128]{2,1,0:T(8,128)S(1)}, u32[]{:S(2)}, u32[]{:S(2)}) collective-permute-start(f32[11,40,128]{2,1,0:T(8,128)S(1)} %get-tuple-element.34), channel_id=1, source_target_pairs={{0,2},{2,4},{4,6},{6,8},{8,10},{10,12},{12,14},{1,3},{3,5},{5,7},{... | collective-permute-start | bytes 675848 | tf_op jit(solution)/shard_map/ppermute | solution.py:410
  35.1 6.5 %copy-start.6 = (f32[3,256]{1,0:T(4,128)S(1)}, f32[3,256]{1,0:T(4,128)}, u32[]{:S(2)}) copy-start(f32[3,256]{1,0:T(4,128)} %nrm.5) | copy-start | bytes 9220
  35.1 6.5 %copy-start.9 = (f32[3,256]{1,0:T(4,128)S(1)}, f32[3,256]{1,0:T(4,128)}, u32[]{:S(2)}) copy-start(f32[3,256]{1,0:T(4,128)} %disp.3) | copy-start | bytes 9220
  35.1 6.5 %copy-start.11 = (f32[3,256]{1,0:T(4,128)S(1)}, f32[3,256]{1,0:T(4,128)}, u32[]{:S(2)}) copy-start(f32[3,256]{1,0:T(4,128)} %coords.1) | copy-start | bytes 9220
  36.3 40.0 %copy-start = (f32[512,512]{1,0:T(8,128)S(1)}, f32[512,512]{1,0:T(8,128)}, u32[]{:S(2)}) copy-start(f32[512,512]{1,0:T(8,128)} %shell.3) | copy-start | bytes 3145732
  36.3 5.2 %collective-permute-start.4 = (f32[6,24,128]{2,1,0:T(8,128)S(1)}, f32[6,24,128]{2,1,0:T(8,128)S(1)}, u32[]{:S(2)}, u32[]{:S(2)}) collective-permute-start(f32[6,24,128]{2,1,0:T(8,128)S(1)} %get-tuple-element.38), channel_id=1, source_target_pairs={{0,1},{1,0},{2,3},{3,2},{4,5},{5,4},{6,7},{7,6},{8,9},{9,8},{10,11... | collective-permute-start | bytes 221192 | tf_op jit(solution)/shard_map/ppermute | solution.py:431
  46.8 29.5 %copy-start.10 = (f32[3,512]{1,0:T(4,128)S(1)}, f32[3,512]{1,0:T(4,128)}, u32[]{:S(2)}) copy-start(f32[3,512]{1,0:T(4,128)} %nodes.1) | copy-start | bytes 18436

commit v2 on v1

v2 whole, which is shorter than its diff:
```python
import math

import jax
import jax.numpy as jnp
from jax import lax
from jax.experimental import pallas as pl
from jax.experimental.pallas import tpu as pltpu
from jax.sharding import PartitionSpec as P

SWEEPS = 4
DOM, SUB, LANE = 64, 8, 2
CX, CY, CZ = 32, 16, 128
PTS, NS, CAP = 256, 512, 8
RX, RY = CX + 8, CY + 8
WIDE = 16

source_gain = 16.0
relaxation = 0.5
inv_radius_sq = 11.111111
epsilon = 1e-06

f32, bf16, i32 = jnp.float32, jnp.bfloat16, jnp.int32
NN = (((1,), (0,)), ((), ()))
NT = (((1,), (1,)), ((), ()))


def pieces(x, count):
    parts = []
    for _ in range(count - 1):
        head = x.astype(bf16)
        parts.append(head)
        x = x - head.astype(f32)
    parts.append(x.astype(bf16))
    return parts


def mxu(a, b, dims):
    return lax.dot_general(a, b, dims, preferred_element_type=f32)


def ones_at(rows, index):
    at = lax.broadcasted_iota(i32, (rows, index.shape[1]), 0)
    return at == index


def as_ones(mask):
    return jnp.where(mask, 1.0, 0.0).astype(bf16)


def spread(rows, z, values, edge=None):
    if edge is None:
        parts = pieces(jnp.where(ones_at(CZ, z), values, 0.0), 3)
    else:
        near = jnp.where(edge == 0, z, z - (CZ - 16))
        parts = []
        for part in pieces(jnp.where(ones_at(16, near), values, 0.0), 3):
            zero = jnp.zeros_like(part)
            first, last = jnp.where(edge == 0, part, zero), jnp.where(edge == 0, zero, part)
            parts.append(jnp.concatenate([first, jnp.zeros((CZ - 32, PTS), bf16), last], axis=0))
    total = None
    for part in parts:
        term = mxu(rows, part, NT)
        total = term if total is None else total + term
    return total


def halves(row):
    return row[:, 0:128], row[:, 128:256]


def joined(ref_rows):
    return jnp.concatenate([ref_rows[0:1], ref_rows[1:2]], axis=1)


def start_kernel(
    rhs_far, coef_far, pold_far, cell_far, part_far, nrm_far, disp_far,
    src, rden, pold, low, high, slot, cell, nrm, disp, rhs, coef, part, sems,
):
    pairs = (
        (cell_far, cell), (part_far, part), (nrm_far, nrm), (disp_far, disp),
        (rhs_far, rhs), (pold_far, pold), (coef_far, coef),
    )
    copies = [pltpu.make_async_copy(a, b, sems.at[k]) for k, (a, b) in enumerate(pairs)]
    for copy in copies:
        copy.start()
    for copy in copies[:4]:
        copy.wait()
    points = cell[...]
    values = source_gain * jnp.sum(disp[...] * nrm[...], axis=0, keepdims=True)
    added = spread(as_ones(ones_at(CX * CY, points >> 7)), points & 127, values)
    owner = ones_at(DOM, part[...])
    earlier = lax.broadcasted_iota(i32, (PTS, PTS), 0) < lax.broadcasted_iota(i32, (PTS, PTS), 1)
    before = mxu(as_ones(owner), as_ones(earlier), NN)
    rank = jnp.sum(jnp.where(owner, before, 0.0), axis=0, keepdims=True)
    slot[...] = part[...].astype(f32) * CAP + rank
    copies[4].wait()
    src[...] = rhs[...] + added.reshape(CX, CY, CZ)
    copies[6].wait()
    rden[...] = 1.0 / (6.0 + coef[...])
    copies[5].wait()
    tail = jnp.concatenate([*halves(points.astype(f32)), jnp.zeros((6, CZ), f32)], axis=0)
    for out, base3, base4 in ((low, 0, 0), (high, CY - 3, CY - 4)):
        for field, own, width, base in ((0, src, 3, base3), (3, rden, 3, base3), (6, pold, 4, base4)):
            for k in range(width):
                at = (field + k) * CX
                out[at : at + CX, :] = own[:, base + k, :]
        out[10 * CX : 10 * CX + 8, :] = tail


def dom_kernel(src, rden, pold, cell, slot, subhigh, sublow, low, high):
    tail = jnp.concatenate(
        [
            *halves(cell[...].astype(f32)),
            subhigh[10 * CX : 10 * CX + 2],
            sublow[10 * CX : 10 * CX + 2],
            *halves(slot[...]),
        ],
        axis=0,
    )
    for out, base3, base4 in ((low, 0, 0), (high, CX - 3, CX - 4)):
        for field, own, width, base in ((0, src, 3, base3), (3, rden, 3, base3), (6, pold, 4, base4)):
            for k in range(width):
                x, at = base + k, (field + k) * RY
                out[at : at + CY, :] = own[x]
                rows = [subhigh[(field + j) * CX + x : (field + j) * CX + x + 1] for j in range(width)]
                rows += [jnp.zeros((1, CZ), f32)] * (8 - 2 * width)
                rows += [sublow[(field + j) * CX + x : (field + j) * CX + x + 1] for j in range(width)]
                out[at + CY : at + RY, :] = jnp.concatenate(rows, axis=0)
        out[10 * RY : 10 * RY + 8, :] = tail


def lane_kernel(place, src, rden, pold, cell, subhigh, sublow, domhigh, domlow, esrc, erden, epold, strips, meta):
    for field, own, width, ext in ((0, src, 3, esrc), (3, rden, 3, erden), (6, pold, 4, epold)):
        ext[0:CX, 0:CY, :] = own[...]
        if width == 3:
            ext[0:CX, CY:RY, :] = jnp.zeros((CX, 8, CZ), f32)
            ext[CX + 3 : CX + 5] = jnp.zeros((2, RY, CZ), f32)
        for k in range(width):
            at = (field + k) * CX
            ext[0:CX, CY + k, :] = subhigh[at : at + CX]
            ext[0:CX, RY - width + k, :] = sublow[at : at + CX]
            at = (field + k) * RY
            ext[CX + k] = domhigh[at : at + RY]
            ext[RX - width + k] = domlow[at : at + RY]
    lane = place[1]
    shift = jnp.where(lane == 0, 4, 0)
    at = lax.broadcasted_iota(i32, (RY, CZ), 1)
    group = RX // 8
    for x in range(group):
        total = jnp.zeros((RY, CZ), f32)
        for k in range(8):
            for field, ext in enumerate((esrc, erden, epold)):
                lo = 16 * k + 4 * field
                moved = pltpu.roll(ext[k * group + x], lax.rem(lo + shift, 128), 1)
                total = jnp.where((at >= lo) & (at < lo + 4), moved, total)
        strips[x] = total
    a, b = halves(cell[...].astype(f32))
    cells = [a, b, subhigh[10 * CX : 10 * CX + 2], sublow[10 * CX : 10 * CX + 2]]
    cells += [domhigh[10 * RY : 10 * RY + 6], domlow[10 * RY : 10 * RY + 6], jnp.zeros((6, CZ), f32)]
    cells = jnp.concatenate(cells, axis=0)
    meta[...] = cells
    strips[group] = cells


def sweep(now, out, source, scale):
    def chunk(i, _):
        base = i * 8

        def at(pair, x):
            return jnp.concatenate([pair[0][x], pair[1][x]], axis=1)

        window = [at(now, lax.rem(base + RX - 1 + k, RX)) for k in range(10)]
        for k in range(8):
            x = base + k
            here = window[k + 1]
            total = window[k + 2] + window[k]
            total = total + (pltpu.roll(here, RY - 1, 0) + pltpu.roll(here, 1, 0))
            total = total + (pltpu.roll(here, 2 * CZ - 1, 1) + pltpu.roll(here, 1, 1))
            total = (at(source, x) + total) * at(scale, x)
            out[0][x], out[1][x] = total[:, 0:CZ], total[:, CZ : 2 * CZ]
        return 0

    lax.fori_loop(0, RX // 8, chunk, 0)


def last_sweep(now, source, scale, write):
    def chunk(i, _):
        base = i * 8
        window = [now[0][lax.rem(base + RX - 1 + k, RX)] for k in range(10)]
        for k in range(8):
            x = base + k
            here = window[k + 1]
            total = window[k + 2] + window[k]
            total = total + (pltpu.roll(here, RY - 1, 0) + pltpu.roll(here, 1, 0))
            wide = jnp.concatenate([here[0:CY], now[1][x, 0:CY]], axis=1)
            beside = pltpu.roll(wide, 2 * CZ - 1, 1) + pltpu.roll(wide, 1, 1)
            total = total[0:CY] + beside[:, 0:CZ]
            write(x, (source[0][x, 0:CY] + total) * scale[0][x, 0:CY])
        return 0

    lax.fori_loop(0, CX // 8, chunk, 0)


def forces_at(pressure, points, nrm):
    at_z = as_ones(ones_at(CZ, points & 127))
    total = None
    for part in pieces(pressure, 3):
        term = mxu(part, at_z, NN)
        total = term if total is None else total + term
    press = jnp.sum(jnp.where(ones_at(CX * CY, points >> 7), total, 0.0), axis=0, keepdims=True)
    return [press * nrm[c : c + 1, :] for c in range(3)]


def first_fluid_kernel(
    place, esrc, erden, epold, strips, cell, nrm, coords, disp, slot,
    pressure, xrden, sending, xsrc, xpold, even0, even1, odd0, odd1,
):
    lane = place[1]
    at = lax.broadcasted_iota(i32, (RY, CZ), 1)
    keep = jnp.where(lane == 0, at, CZ - 1 - at) < 4
    group = RX // 8
    for x in range(group):
        packed = strips[1 - lane, x]
        for field, beside in enumerate((xsrc, xrden, xpold)):
            for k in range(8):
                lo = 16 * k + 4 * field
                moved = pltpu.roll(packed, lax.rem(256 - lo - 4 * lane, 128), 1)
                beside[k * group + x] = jnp.where(keep, moved, 0.0)
    source, scale = (esrc, xsrc), (erden, xrden)
    even, odd = (even0, even1), (odd0, odd1)
    sweep((epold, xpold), even, source, scale)
    sweep(even, odd, source, scale)
    sweep(odd, even, source, scale)

    def write(x, value):
        pressure[x] = value

    last_sweep(even, source, scale, write)
    slots = slot[...].astype(i32)
    values = forces_at(pressure[...].reshape(CX * CY, CZ), cell[...], nrm)
    values += [coords[c : c + 1, :] for c in range(3)]
    values += [disp[c : c + 1, :] for c in range(3)]
    values += [nrm[c : c + 1, :] for c in range(3)]
    values += [jnp.ones((1, PTS), f32)]
    sending[...] = to_slots(values, slots)


def second_fluid_kernel(
    place, erden, xrden, before, arrived, meta, strips, cell, nrm, slot,
    pressure_far, sending, src0, src1, even0, even1, odd0, odd1, pressure, sem,
):
    sub, lane = place[0], place[1]
    scale = (erden, xrden)
    for tile, (source, now) in enumerate(((src0, even0), (src1, even1))):
        cells = meta[...] if tile == 0 else strips[1 - lane, RX // 8]
        other = lane if tile == 0 else 1 - lane
        beside_x = jnp.zeros((8 * CY, CZ), f32)
        beside_y = jnp.zeros((CX * 8, CZ), f32)
        corner = jnp.zeros((64, CZ), f32)
        for dy, off_y in enumerate((0, 1, -1)):
            wanted = sub + off_y
            inside = (wanted >= 0) & (wanted < SUB)
            block = arrived[lax.rem(wanted + SUB, SUB) * LANE + other]
            block = jnp.where(inside, block, 0.0)
            for dx in range(3):
                values = joined(block[2 * dx : 2 * dx + 2])
                at = (dx * 3 + dy) * 2
                points = joined(cells[at : at + 2]).astype(i32)
                x, y, z = points >> 11, (points >> 7) & 15, points & 127
                if dx == 1:
                    x = jnp.where(x < 3, x, -1000)
                elif dx == 2:
                    x = jnp.where(x >= CX - 3, x - (CX - 8), -1000)
                if dy == 1:
                    y = jnp.where(y < 3, y, -1000000)
                elif dy == 2:
                    y = jnp.where(y >= CY - 3, y - (CY - 8), -1000000)
                edge = None if tile == 0 else lane
                if dx == 0 and dy == 0:
                    middle = spread(as_ones(ones_at(CX * CY, points >> 7)), z, values, edge)
                elif dy == 0:
                    beside_x = beside_x + spread(as_ones(ones_at(8 * CY, x * CY + y)), z, values, edge)
                elif dx == 0:
                    beside_y = beside_y + spread(as_ones(ones_at(CX * 8, x * 8 + y)), z, values, edge)
                else:
                    corner = corner + spread(as_ones(ones_at(64, x * 8 + y)), z, values, edge)
        for xs, ys, part in (
            (slice(0, CX), slice(0, CY), middle.reshape(CX, CY, CZ)),
            (slice(CX, RX), slice(0, CY), beside_x.reshape(8, CY, CZ)),
            (slice(0, CX), slice(CY, RY), beside_y.reshape(CX, 8, CZ)),
            (slice(CX, RX), slice(CY, RY), corner.reshape(8, 8, CZ)),
        ):
            source[xs, ys, :] = part
            now[xs, ys, :] = part * scale[tile][xs, ys, :]
    source, even, odd = (src0, src1), (even0, even1), (odd0, odd1)
    sweep(even, odd, source, scale)
    sweep(odd, even, source, scale)

    def write(x, value):
        pressure[x] = before[x] + value

    last_sweep(even, source, scale, write)
    copy = pltpu.make_async_copy(pressure, pressure_far, sem)
    copy.start()
    sending[...] = to_slots(forces_at(pressure[...].reshape(CX * CY, CZ), cell[...], nrm), slot[...].astype(i32))
    copy.wait()


def to_slots(values, slots):
    rank = slots & 7
    filler = [jnp.zeros((1, PTS), f32)] * (WIDE - len(values))
    block = jnp.concatenate(list(values) + filler, axis=0)
    stacked = jnp.concatenate([jnp.where(rank == r, block, 0.0) for r in range(CAP)], axis=0)
    owner = as_ones(ones_at(DOM, slots >> 3))
    total = None
    for part in pieces(stacked, 3):
        term = mxu(owner, part, NT)
        total = term if total is None else total + term
    return total


def from_slots(arrived, slots):
    rank = slots & 7
    owner = as_ones(ones_at(DOM, slots >> 3))
    flat = arrived.T
    total = None
    for part in pieces(flat, 3):
        term = mxu(part, owner, NN)
        total = term if total is None else total + term
    found = jnp.zeros((WIDE, PTS), f32)
    for r in range(CAP):
        found = found + jnp.where(rank == r, total[r * WIDE : (r + 1) * WIDE], 0.0)
    return found


def by_slot(received):
    flat = received.T
    return jnp.concatenate([flat[r * WIDE : (r + 1) * WIDE] for r in range(CAP)], axis=1)


def by_row(values):
    flat = jnp.concatenate([values[:, r * DOM : (r + 1) * DOM] for r in range(CAP)], axis=0)
    return flat.T


def product(left, head, tail, dims):
    a, b = pieces(left, 2)
    rows = left.shape[0]
    both = mxu(jnp.concatenate([a, b], axis=0), head, dims)
    return both[:rows] + both[rows:] + mxu(a, tail, dims)


def mapped_back(forces, khead, ktail, shell):
    loading = product(forces, khead, ktail, NN) * (1.0 / math.sqrt(PTS))
    shead, stail = pieces(shell, 2)
    displaced = loading + product(loading, shead, stail, NN)
    return product(displaced, khead, ktail, NT) * (1.0 / math.sqrt(NS))


def first_structure_kernel(received, nodes, shell, returned, mapped, khead, ktail):
    for r in range(CAP):
        distance = None
        for c in range(3):
            lane = r * WIDE + 3 + c
            gap = received[:, lane : lane + 1] - nodes[c : c + 1, :]
            distance = gap * gap if distance is None else distance + gap * gap
        weight = jnp.exp(-distance * inv_radius_sq)
        head, tail = pieces(weight, 2)
        khead[r * DOM : (r + 1) * DOM, :] = head
        ktail[r * DOM : (r + 1) * DOM, :] = tail
    held = by_slot(received[...])
    back = mapped_back(held[0:WIDE], khead[...], ktail[...], shell[...])
    mapped[...] = back
    moved = (source_gain * relaxation) * jnp.sum(held[9:12] * (back[0:3] - held[6:9]), axis=0, keepdims=True)
    rows = jnp.concatenate([moved, jnp.zeros((WIDE - 1, NS), f32)], axis=0)
    own = by_row(rows)
    at = lax.broadcasted_iota(i32, own.shape, 0)
    above = jnp.where(at == DOM - 1, 0.0, pltpu.roll(own, DOM - 1, 0))
    below = jnp.where(at == 0, 0.0, pltpu.roll(own, 1, 0))
    returned[...] = own + pltpu.roll(above, 1, 1) + pltpu.roll(below, 2, 1)


def second_structure_kernel(received, before, mapped, khead, ktail, shell, returned):
    forces = by_slot(received[...])
    held = by_slot(before[...])
    back = mapped_back(forces, khead[...], ktail[...], shell[...])
    t0, t1, d0, used = mapped[0:3, :], back[0:3], held[6:9], held[12:13]
    r0 = t0 - d0
    r1 = t1 - (d0 + relaxation * r0)
    delta = r1 - r0
    sums = []
    for term in (delta * r1, delta * delta, r1 * r1):
        inner = jnp.sum(term * used, axis=0, keepdims=True)
        sums.append(jnp.broadcast_to(jnp.sum(inner, axis=1, keepdims=True), (1, NS)))
    rows = jnp.concatenate([t1, t0, *sums, jnp.zeros((WIDE - 9, NS), f32)], axis=0)
    returned[...] = by_row(rows)


def hand_out_kernel(arrived, slot, high, low, out):
    held = arrived[...]
    rows = []
    for block in range(3):
        if block == 0:
            slots = slot[...]
        else:
            slots = joined((high if block == 1 else low)[10 * RY + 6 : 10 * RY + 8])
        found = from_slots(held, slots.astype(i32))
        rows += halves(found[block : block + 1])
    rows += [jnp.zeros((2, 128), f32)]
    payload = jnp.concatenate(rows, axis=0)
    for k in range(SUB * LANE):
        out[k] = payload


def arrive_kernel(arrived, slot, found, out):
    held = arrived[...]
    found[...] = from_slots(held, slot[...].astype(i32))
    total = jnp.sum(held, axis=0, keepdims=True)
    for k in range(SUB * LANE):
        out[k : k + 1, :] = total


def finish_kernel(found, sums, disp, rms):
    total = jnp.sum(sums[...], axis=0, keepdims=True)
    vr, vv, rr = total[:, 6:7], total[:, 7:8], total[:, 8:9]
    t1, t0 = found[0:3, :], found[3:6, :]
    disp[...] = t1 - (vr / (vv + epsilon)) * (t1 - t0)
    count = 3.0 * PTS * DOM * SUB * LANE
    rms[...] = jnp.sqrt(rr / count)


def shape(*dims, dtype=f32):
    return jax.ShapeDtypeStruct(dims, dtype)


def call(kernel, outs, args, scratch=(), scalars=0, name=None, far=(), far_out=()):
    def spec(k):
        space = pltpu.SMEM if k < scalars else pltpu.HBM if k in far else pltpu.VMEM
        return pl.BlockSpec(memory_space=space)

    return pl.pallas_call(
        kernel,
        out_shape=outs,
        in_specs=[spec(k) for k in range(len(args))],
        out_specs=tuple(
            pl.BlockSpec(memory_space=pltpu.HBM if k in far_out else pltpu.VMEM) for k in range(len(outs))
        ),
        scratch_shapes=list(scratch),
        compiler_params=pltpu.CompilerParams(vmem_limit_bytes=40 * 1024 * 1024),
        name=name,
    )(*args)


def body(rhs, coef, pold, cell_index, nrm, coords, partner, nodes, shell, disp):
    place = jnp.stack([lax.axis_index("sub"), lax.axis_index("lane")]).astype(i32)
    cell = cell_index.reshape(1, PTS)
    part = partner.reshape(1, PTS)
    block, half = shape(CX, CY, CZ), shape(RX, RY, CZ)
    row = shape(DOM, CAP * WIDE)

    def pair(low, high, axis):
        count = lax.axis_size(axis)
        fromhigh = lax.ppermute(low, axis, [(i + 1, i) for i in range(count - 1)])
        fromlow = lax.ppermute(high, axis, [(i, i + 1) for i in range(count - 1)])
        return fromhigh, fromlow

    def across(rows):
        return lax.all_to_all(rows, "dom", 0, 0, tiled=True)

    face, slab = shape(10 * CX + 8, CZ), shape(10 * RY + 8, CZ)
    src, rden, pold, low, high, slot, cell, nrm, disp = call(
        start_kernel,
        (block, block, block, face, face, shape(1, PTS), shape(1, PTS, dtype=i32), shape(3, PTS), shape(3, PTS)),
        (rhs, coef, pold, cell, part, nrm, disp),
        [pltpu.VMEM((CX, CY, CZ), f32)] * 2 + [pltpu.VMEM((1, PTS), i32), pltpu.SemaphoreType.DMA((7,))],
        name="start",
        far=range(7),
    )
    subhigh, sublow = pair(low, high, "sub")
    low, high = call(dom_kernel, (slab, slab), (src, rden, pold, cell, slot, subhigh, sublow), name="dom_slabs")
    domhigh, domlow = pair(low, high, "dom")
    esrc, erden, epold, strips, meta = call(
        lane_kernel,
        (half, half, half, shape(RX // 8 + 1, RY, CZ), shape(RY, CZ)),
        (place, src, rden, pold, cell, subhigh, sublow, domhigh, domlow),
        scalars=1,
        name="lane_strips",
    )
    strips = lax.all_gather(strips, "lane")
    grid = pltpu.VMEM((RX, RY, CZ), f32)
    pressure, xrden, sending = call(
        first_fluid_kernel,
        (block, half, row),
        (place, esrc, erden, epold, strips, cell, nrm, coords, disp, slot),
        [grid] * 6,
        scalars=1,
        name="first_fluid",
    )
    received = across(sending)
    square = shape(NS, NS, dtype=bf16)
    returned, mapped, khead, ktail = call(
        first_structure_kernel, (row, shape(WIDE, NS), square, square), (received, nodes, shell), name="first_structure"
    )
    arrived = across(returned)
    (spread_out,) = call(
        hand_out_kernel, (shape(SUB * LANE, 8, 128),), (arrived, slot, domhigh, domlow), name="hand_out"
    )
    values = lax.all_to_all(spread_out, ("sub", "lane"), 0, 0, tiled=True)
    pressure, sending = call(
        second_fluid_kernel,
        (block, row),
        (place, erden, xrden, pressure, values, meta, strips, cell, nrm, slot),
        [grid] * 6 + [pltpu.VMEM((CX, CY, CZ), f32), pltpu.SemaphoreType.DMA],
        scalars=1,
        name="second_fluid",
        far_out=(0,),
    )
    again = across(sending)
    (returned,) = call(
        second_structure_kernel, (row,), (again, received, mapped, khead, ktail, shell), name="second_structure"
    )
    arrived = across(returned)
    found, sums = call(
        arrive_kernel, (shape(WIDE, PTS), shape(SUB * LANE, 128)), (arrived, slot), name="arrive"
    )
    sums = lax.all_to_all(sums, ("sub", "lane"), 0, 0, tiled=True)
    disp_new, rms = call(finish_kernel, (shape(3, PTS), shape(1, 1)), (found, sums), name="finish")
    return pressure, disp_new, rms.reshape(())


def solution(mesh):
    every = ("dom", "sub", "lane")
    grid, points = P(*every), P(None, every)
    return jax.shard_map(
        body,
        mesh=mesh,
        in_specs=(grid, grid, grid, P(every), points, points, P(every, None), points, P(every, None), points),
        out_specs=(grid, points, P()),
        check_vma=False,
    )
```

time: 165 us -> 162 us (0.982)
  starting transfers between devices: 26.5 us -> 23.3 us
  blocking collectives: 106 us -> 109 us
  waiting for transfers between devices: 7.52 us -> 5.4 us
    all_gather x0 -> x1, blocking collectives: none -> 4.35 us  [body(): strips = lax.all_gather(strips, 'lane')]
    ppermute x1 -> x0, waiting for transfers between devices: 3.17 us -> none  [body(): strips = lax.ppermute(strips, 'lane', [(0, 1), (1, 0)])]
    all_to_all x4, blocking collectives: 73.4 us -> 70.8 us  [across(): return lax.all_to_all(rows, 'dom', 0, 0, tiled=True)]
    ppermute x2, starting transfers between devices: 8.29 us -> 5.91 us  [pair(): fromlow = lax.ppermute(high, axis, [(i, i + 1) for i in range(count - 1)])]
    ppermute x1 -> x0, starting transfers between devices: 2.05 us -> none  [body(): strips = lax.ppermute(strips, 'lane', [(0, 1), (1, 0)])]
    unnamed x26 -> x20, local copies, waits for them, and re-layouts: 4.93 us -> 4.94 us
  transfers between devices with their start and end apart: 5 -> 4, of which waited for: 3 -> 3; matrix products, arithmetic and copies ran while one was open for 0% -> 0% of each run, Pallas kernels for 0% -> 0%
where the time goes in v2:
time: 162 us; the launch traced here: 161 us
  blocking collectives  109 us (67%)
  starting transfers between devices  23.3 us (14%)
  Pallas kernels  17.4 us (11%)
  waiting for transfers between devices  5.4 us (3%)
  local copies, waits for them, and re-layouts  4.94 us (3%)
    all_to_all x4, blocking collectives, across(): return lax.all_to_all(rows, 'dom', 0, 0, tiled=True)  70.8 us
    all_to_all x1, blocking collectives, body(): values = lax.all_to_all(spread_out, ('sub', 'lane'), 0, 0, tiled=True)  22.2 us
    pallas_call x10, Pallas kernels, call(): pl.pallas_call(kernel, out_shape=outs, in_specs=[spec(k) for k in range(l...  17.4 us
    ppermute x2, starting transfers between devices, pair(): fromhigh = lax.ppermute(low, axis, [(i + 1, i) for i in range(count - 1)])  17.4 us
    all_to_all x1, blocking collectives, body(): sums = lax.all_to_all(sums, ('sub', 'lane'), 0, 0, tiled=True)  12.1 us
    ppermute x2, starting transfers between devices, pair(): fromlow = lax.ppermute(high, axis, [(i, i + 1) for i in range(count - 1)])  5.91 us
    unnamed x20, local copies, waits for them, and re-layouts  4.94 us
    all_gather x1, blocking collectives, body(): strips = lax.all_gather(strips, 'lane')  4.35 us
  transfers between devices with their start and end apart: 4, of which 3 were waited for; matrix products, arithmetic and copies ran while one was open for 0% of the time, Pallas kernels for 0%

profile of v2, /device:TPU:1, one launch (start us, length us, event | category | flops | bytes accessed | tf_op | source)
XLA Modules:
  0.0 161.3 jit_solution(8347667407072260273)
XLA Ops:
  0.6 0.0 copy-start.9
  0.6 0.0 copy-start.8
  0.7 0.7 copy-done.9
  1.3 0.0 copy-done.8
  1.3 0.0 copy-start.1
  1.3 0.9 copy-done.1
  2.3 0.0 copy-start.2
  2.3 0.9 copy-done.2
  3.2 0.0 copy-start.3
  3.2 0.9 copy-done.3
  4.2 0.0 copy-start.5
  4.2 0.7 copy-done.5
  4.9 0.0 copy-start.6
  4.9 0.7 copy-done.6
  5.6 0.8 start.1
  6.3 16.1 %collective-permute-start = (f32[328,128]{1,0:T(8,128)S(1)}, f32[328,128]{1,0:T(8,128)S(1)}, u32[]{:S(2)}, u32[]{:S(2)}) collective-permute-start(f32[328,128]{1,0:T(8,128)S(1)} %get-tuple-element.36), channel_id=1, source_target_pairs={{2,0},{4,2},{6,4},{8,6},{10,8},{12,10},{14,12},{3,1},{5,3},{7,5},{... | collective-permute-start | bytes 503816 | tf_op jit(solution)/shard_map/ppermute | solution.py:463
  22.4 1.9 %collective-permute-start.1 = (f32[328,128]{1,0:T(8,128)S(1)}, f32[328,128]{1,0:T(8,128)S(1)}, u32[]{:S(2)}, u32[]{:S(2)}) collective-permute-start(f32[328,128]{1,0:T(8,128)S(1)} %get-tuple-element.37), channel_id=1, source_target_pairs={{0,2},{2,4},{4,6},{6,8},{8,10},{10,12},{12,14},{1,3},{3,5},{5,7},{... | collective-permute-start | bytes 503816 | tf_op jit(solution)/shard_map/ppermute | solution.py:464
  24.3 0.0 collective-permute-done.subhigh
  24.4 2.3 %collective-permute-done.1.sublow = f32[328,128]{1,0:T(8,128)S(1)} collective-permute-done((f32[328,128]{1,0:T(8,128)S(1)}, f32[328,128]{1,0:T(8,128)S(1)}, u32[]{:S(2)}, u32[]{:S(2)}) %collective-permute-start.1) | collective-permute-done | bytes 167968 | tf_op jit(solution)/shard_map/ppermute | solution.py:464
  26.6 0.1 dom_slabs.1
  26.7 1.3 collective-permute-start.2
  28.0 4.0 %collective-permute-start.3 = (f32[248,128]{1,0:T(8,128)S(1)}, f32[248,128]{1,0:T(8,128)S(1)}, u32[]{:S(2)}, u32[]{:S(2)}) collective-permute-start(f32[248,128]{1,0:T(8,128)S(1)} %get-tuple-element.40), channel_id=1, source_target_pairs={{0,16},{16,32},{32,48},{48,64},{64,80},{80,96},{96,112},{112,128},... | collective-permute-start | bytes 380936 | tf_op jit(solution)/shard_map/ppermute | solution.py:464
  32.0 0.1 pad_add_fusion.place
  32.1 1.3 collective-permute-done.2.domhigh.high
  33.4 1.8 %collective-permute-done.3.domlow.low = f32[248,128]{1,0:T(8,128)S(1)} collective-permute-done((f32[248,128]{1,0:T(8,128)S(1)}, f32[248,128]{1,0:T(8,128)S(1)}, u32[]{:S(2)}, u32[]{:S(2)}) %collective-permute-start.3) | collective-permute-done | bytes 127008 | tf_op jit(solution)/shard_map/ppermute | solution.py:464
  35.2 0.0 copy-start.7
  35.2 1.2 lane_strips.1
  36.4 0.0 copy-start
  36.4 4.3 %all-gather = f32[12,24,128]{2,1,0:T(8,128)S(1)} all-gather(f32[6,24,128]{2,1,0:T(8,128)S(1)} %get-tuple-element.44), channel_id=2, replica_groups=mesh['dom'=64,'sub'=8,'lane'=2] {'lane'}, dimensions={0}, use_global_device_ids=true | all-gather | bytes 221184 | tf_op jit(solution)/shard_map/all_gather | solution.py:489
  40.7 0.0 copy-done.7
  40.7 5.0 %first_fluid.1 = (f32[32,16,128]{2,1,0:T(8,128)S(1)}, f32[40,24,128]{2,1,0:T(8,128)S(1)}, f32[64,128]{1,0:T(8,128)S(1)}) custom-call(s32[2]{0:T(128)S(1)} %pad_add_fusion.place, f32[40,24,128]{2,1,0:T(8,128)S(1)} %get-tuple-element.42.esrc, f32[40,24,128]{2,1,0:T(8,128)S(1)} %get-tuple-element.41.erden, f32[40,24,128]{2,1,0:T(8,128)S(1)} %get-tuple-element.43.epold, ...), custom_call_target="tpu_custom_call" | custom-call | tf_op jit(solution)/shard_map/first_fluid/pallas_call | solution.py:441
  45.7 0.0 copy-start.4
  45.7 26.9 %all_to_all.60 = f32[64,1,128]{2,1,0:T(1,128)S(1)} all-to-all(f32[64,1,128]{2,1,0:T(1,128)S(1)} %bitcast.36), channel_id=1, replica_groups=mesh['dom'=64,'sub'=8,'lane'=2] {'dom'}, dimensions={0} | all-to-all | bytes 65536 | tf_op jit(solution)/shard_map/all_to_all | solution.py:468
  72.6 0.0 copy-done
  72.6 0.0 copy-done.4
  72.6 1.7 %first_structure.1 = (f32[64,128]{1,0:T(8,128)S(1)}, f32[16,512]{1,0:T(8,128)S(1)}, bf16[512,512]{1,0:T(8,128)(2,1)S(1)}, bf16[512,512]{1,0:T(8,128)(2,1)S(1)}) custom-call(f32[64,128]{1,0:T(8,128)S(1)} %bitcast.28, f32[3,512]{1,0:T(4,128)S(1)} %copy-done.4, f32[512,512]{1,0:T(8,128)S(1)} %copy-done), custom_call_target="tpu_custom_call" | custom-call | tf_op jit(solution)/shard_map/first_structure/pallas_call | solution.py:441
  74.4 14.6 %all_to_all.61 = f32[64,1,128]{2,1,0:T(1,128)S(1)} all-to-all(f32[64,1,128]{2,1,0:T(1,128)S(1)} %bitcast.37), channel_id=1, replica_groups=mesh['dom'=64,'sub'=8,'lane'=2] {'dom'}, dimensions={0} | all-to-all | bytes 65536 | tf_op jit(solution)/shard_map/all_to_all | solution.py:468
  89.0 0.4 hand_out.1
  89.4 22.2 %all_to_all.62.arrived = f32[16,8,128]{2,1,0:T(8,128)S(1)} all-to-all(f32[16,8,128]{2,1,0:T(8,128)S(1)} %hand_out.1), channel_id=1, replica_groups=mesh['dom'=64,'sub'=8,'lane'=2] {'sub','lane'}, dimensions={0} | all-to-all | bytes 131072 | tf_op jit(solution)/shard_map/all_to_all | solution.py:508
  111.5 6.1 %second_fluid.1 = (f32[32,16,128]{2,1,0:T(8,128)}, f32[64,128]{1,0:T(8,128)S(1)}) custom-call(s32[2]{0:T(128)S(1)} %pad_add_fusion.place, f32[40,24,128]{2,1,0:T(8,128)S(1)} %get-tuple-element.41.erden, f32[40,24,128]{2,1,0:T(8,128)S(1)} %get-tuple-element.47.xrden, f32[32,16,128]{2,1,0:T(8,128)S(1)} %get-tuple-element.48.before, ...), custom_call_target="tpu_custom_call" | custom-call | tf_op jit(solution)/shard_map/second_fluid/pallas_call | solution.py:441
  117.7 14.6 %all_to_all.63 = f32[64,1,128]{2,1,0:T(1,128)S(1)} all-to-all(f32[64,1,128]{2,1,0:T(1,128)S(1)} %bitcast.35), channel_id=1, replica_groups=mesh['dom'=64,'sub'=8,'lane'=2] {'dom'}, dimensions={0} | all-to-all | bytes 65536 | tf_op jit(solution)/shard_map/all_to_all | solution.py:468
  132.3 1.2 second_structure.1
  133.5 14.6 %all_to_all.64 = f32[64,1,128]{2,1,0:T(1,128)S(1)} all-to-all(f32[64,1,128]{2,1,0:T(1,128)S(1)} %bitcast.31), channel_id=1, replica_groups=mesh['dom'=64,'sub'=8,'lane'=2] {'dom'}, dimensions={0} | all-to-all | bytes 65536 | tf_op jit(solution)/shard_map/all_to_all | solution.py:468
  148.1 0.3 arrive.1
  148.4 12.1 %all_to_all.65 = f32[16,1,128]{2,1,0:T(1,128)S(1)} all-to-all(f32[16,1,128]{2,1,0:T(1,128)S(1)} %bitcast.38), channel_id=1, replica_groups=mesh['dom'=64,'sub'=8,'lane'=2] {'sub','lane'}, dimensions={0} | all-to-all | bytes 16384 | tf_op jit(solution)/shard_map/all_to_all | solution.py:526
  160.5 0.8 finish.1
Async XLA Ops:
  0.6 0.7 copy-start.9
  0.6 0.7 copy-start.8
  1.3 0.9 copy-start.1
  2.3 0.9 copy-start.2
  3.2 0.9 copy-start.3
  4.2 0.7 copy-start.5
  4.9 0.7 copy-start.6
  6.3 18.0 %collective-permute-start = (f32[328,128]{1,0:T(8,128)S(1)}, f32[328,128]{1,0:T(8,128)S(1)}, u32[]{:S(2)}, u32[]{:S(2)}) collective-permute-start(f32[328,128]{1,0:T(8,128)S(1)} %get-tuple-element.36), channel_id=1, source_target_pairs={{2,0},{4,2},{6,4},{8,6},{10,8},{12,10},{14,12},{3,1},{5,3},{7,5},{... | collective-permute-start | bytes 503816 | tf_op jit(solution)/shard_map/ppermute | solution.py:463
  22.4 4.2 %collective-permute-start.1 = (f32[328,128]{1,0:T(8,128)S(1)}, f32[328,128]{1,0:T(8,128)S(1)}, u32[]{:S(2)}, u32[]{:S(2)}) collective-permute-start(f32[328,128]{1,0:T(8,128)S(1)} %get-tuple-element.37), channel_id=1, source_target_pairs={{0,2},{2,4},{4,6},{6,8},{8,10},{10,12},{12,14},{1,3},{3,5},{5,7},{... | collective-permute-start | bytes 503816 | tf_op jit(solution)/shard_map/ppermute | solution.py:464
  26.7 6.7 %collective-permute-start.2 = (f32[248,128]{1,0:T(8,128)S(1)}, f32[248,128]{1,0:T(8,128)S(1)}, u32[]{:S(2)}, u32[]{:S(2)}) collective-permute-start(f32[248,128]{1,0:T(8,128)S(1)} %get-tuple-element.39), channel_id=1, source_target_pairs={{16,0},{32,16},{48,32},{64,48},{80,64},{96,80},{112,96},{128,112},... | collective-permute-start | bytes 380936 | tf_op jit(solution)/shard_map/ppermute | solution.py:463
  28.0 7.2 %collective-permute-start.3 = (f32[248,128]{1,0:T(8,128)S(1)}, f32[248,128]{1,0:T(8,128)S(1)}, u32[]{:S(2)}, u32[]{:S(2)}) collective-permute-start(f32[248,128]{1,0:T(8,128)S(1)} %get-tuple-element.40), channel_id=1, source_target_pairs={{0,16},{16,32},{32,48},{48,64},{64,80},{80,96},{96,112},{112,128},... | collective-permute-start | bytes 380936 | tf_op jit(solution)/shard_map/ppermute | solution.py:464
  35.2 5.5 %copy-start.7 = (f32[3,256]{1,0:T(4,128)S(1)}, f32[3,256]{1,0:T(4,128)}, u32[]{:S(2)}) copy-start(f32[3,256]{1,0:T(4,128)} %coords.1) | copy-start | bytes 9220
  36.4 36.3 %copy-start = (f32[512,512]{1,0:T(8,128)S(1)}, f32[512,512]{1,0:T(8,128)}, u32[]{:S(2)}) copy-start(f32[512,512]{1,0:T(8,128)} %shell.3) | copy-start | bytes 3145732
  45.7 27.0 %copy-start.4 = (f32[3,512]{1,0:T(4,128)S(1)}, f32[3,512]{1,0:T(4,128)}, u32[]{:S(2)}) copy-start(f32[3,512]{1,0:T(4,128)} %nodes.1) | copy-start | bytes 18436

commit v3 on v2

--- a/solution.py
+++ b/solution.py
@@ -49,11 +49,11 @@
 
 def spread(rows, z, values, edge=None):
     if edge is None:
-        parts = pieces(jnp.where(ones_at(CZ, z), values, 0.0), 3)
+        parts = pieces(jnp.where(ones_at(CZ, z), values, 0.0), 2)
     else:
-        near = jnp.where(edge == 0, z, z - (CZ - 16))
+        beside = jnp.where(edge == 0, z, z - (CZ - 16))
         parts = []
-        for part in pieces(jnp.where(ones_at(16, near), values, 0.0), 3):
+        for part in pieces(jnp.where(ones_at(16, beside), values, 0.0), 2):
             zero = jnp.zeros_like(part)
             first, last = jnp.where(edge == 0, part, zero), jnp.where(edge == 0, zero, part)
             parts.append(jnp.concatenate([first, jnp.zeros((CZ - 32, PTS), bf16), last], axis=0))
@@ -162,49 +162,38 @@
     strips[group] = cells
 
 
-def sweep(now, out, source, scale):
-    def chunk(i, _):
-        base = i * 8
-
-        def at(pair, x):
-            return jnp.concatenate([pair[0][x], pair[1][x]], axis=1)
-
-        window = [at(now, lax.rem(base + RX - 1 + k, RX)) for k in range(10)]
-        for k in range(8):
-            x = base + k
-            here = window[k + 1]
-            total = window[k + 2] + window[k]
-            total = total + (pltpu.roll(here, RY - 1, 0) + pltpu.roll(here, 1, 0))
-            total = total + (pltpu.roll(here, 2 * CZ - 1, 1) + pltpu.roll(here, 1, 1))
-            total = (at(source, x) + total) * at(scale, x)
-            out[0][x], out[1][x] = total[:, 0:CZ], total[:, CZ : 2 * CZ]
-        return 0
-
-    lax.fori_loop(0, RX // 8, chunk, 0)
+def near(width):
+    return [*range(CX + width), *range(RX - width, RX)]
+
+
+def both(pair, x):
+    return jnp.concatenate([pair[0][x], pair[1][x]], axis=1)
+
+
+def sweep(now, out, source, scale, width):
+    for x in near(width):
+        here = both(now, x)
+        total = both(now, (x + 1) % RX) + both(now, (x - 1) % RX)
+        total = total + (pltpu.roll(here, RY - 1, 0) + pltpu.roll(here, 1, 0))
+        total = total + (pltpu.roll(here, 2 * CZ - 1, 1) + pltpu.roll(here, 1, 1))
+        total = (both(source, x) + total) * both(scale, x)
+        out[0][x], out[1][x] = total[:, 0:CZ], total[:, CZ : 2 * CZ]
 
 
 def last_sweep(now, source, scale, write):
-    def chunk(i, _):
-        base = i * 8
-        window = [now[0][lax.rem(base + RX - 1 + k, RX)] for k in range(10)]
-        for k in range(8):
-            x = base + k
-            here = window[k + 1]
-            total = window[k + 2] + window[k]
-            total = total + (pltpu.roll(here, RY - 1, 0) + pltpu.roll(here, 1, 0))
-            wide = jnp.concatenate([here[0:CY], now[1][x, 0:CY]], axis=1)
-            beside = pltpu.roll(wide, 2 * CZ - 1, 1) + pltpu.roll(wide, 1, 1)
-            total = total[0:CY] + beside[:, 0:CZ]
-            write(x, (source[0][x, 0:CY] + total) * scale[0][x, 0:CY])
-        return 0
-
-    lax.fori_loop(0, CX // 8, chunk, 0)
+    for x in range(CX):
+        here = now[0][x]
+        total = now[0][(x + 1) % RX, 0:CY] + now[0][(x - 1) % RX, 0:CY]
+        total = total + (pltpu.roll(here, RY - 1, 0) + pltpu.roll(here, 1, 0))[0:CY]
+        wide = jnp.concatenate([here[0:CY], now[1][x, 0:CY]], axis=1)
+        beside = pltpu.roll(wide, 2 * CZ - 1, 1) + pltpu.roll(wide, 1, 1)
+        write(x, (source[0][x, 0:CY] + (total + beside[:, 0:CZ])) * scale[0][x, 0:CY])
 
 
 def forces_at(pressure, points, nrm):
     at_z = as_ones(ones_at(CZ, points & 127))
     total = None
-    for part in pieces(pressure, 3):
+    for part in pieces(pressure, 2):
         term = mxu(part, at_z, NN)
         total = term if total is None else total + term
     press = jnp.sum(jnp.where(ones_at(CX * CY, points >> 7), total, 0.0), axis=0, keepdims=True)
@@ -228,9 +217,9 @@
                 beside[k * group + x] = jnp.where(keep, moved, 0.0)
     source, scale = (esrc, xsrc), (erden, xrden)
     even, odd = (even0, even1), (odd0, odd1)
-    sweep((epold, xpold), even, source, scale)
-    sweep(even, odd, source, scale)
-    sweep(odd, even, source, scale)
+    sweep((epold, xpold), even, source, scale, 3)
+    sweep(even, odd, source, scale, 2)
+    sweep(odd, even, source, scale, 1)
 
     def write(x, value):
         pressure[x] = value
@@ -242,7 +231,7 @@
     values += [disp[c : c + 1, :] for c in range(3)]
     values += [nrm[c : c + 1, :] for c in range(3)]
     values += [jnp.ones((1, PTS), f32)]
-    sending[...] = to_slots(values, slots)
+    sending[...] = to_slots(values, slots, 3)
 
 
 def second_fluid_kernel(
@@ -293,8 +282,8 @@
             source[xs, ys, :] = part
             now[xs, ys, :] = part * scale[tile][xs, ys, :]
     source, even, odd = (src0, src1), (even0, even1), (odd0, odd1)
-    sweep(even, odd, source, scale)
-    sweep(odd, even, source, scale)
+    sweep(even, odd, source, scale, 2)
+    sweep(odd, even, source, scale, 1)
 
     def write(x, value):
         pressure[x] = before[x] + value
@@ -302,18 +291,18 @@
     last_sweep(even, source, scale, write)
     copy = pltpu.make_async_copy(pressure, pressure_far, sem)
     copy.start()
-    sending[...] = to_slots(forces_at(pressure[...].reshape(CX * CY, CZ), cell[...], nrm), slot[...].astype(i32))
+    sending[...] = to_slots(forces_at(pressure[...].reshape(CX * CY, CZ), cell[...], nrm), slot[...].astype(i32), 2)
     copy.wait()
 
 
-def to_slots(values, slots):
+def to_slots(values, slots, count):
     rank = slots & 7
     filler = [jnp.zeros((1, PTS), f32)] * (WIDE - len(values))
     block = jnp.concatenate(list(values) + filler, axis=0)
     stacked = jnp.concatenate([jnp.where(rank == r, block, 0.0) for r in range(CAP)], axis=0)
     owner = as_ones(ones_at(DOM, slots >> 3))
     total = None
-    for part in pieces(stacked, 3):
+    for part in pieces(stacked, count):
         term = mxu(owner, part, NT)
         total = term if total is None else total + term
     return total
@@ -324,7 +313,7 @@
     owner = as_ones(ones_at(DOM, slots >> 3))
     flat = arrived.T
     total = None
-    for part in pieces(flat, 3):
+    for part in pieces(flat, 2):
         term = mxu(part, owner, NN)
         total = term if total is None else total + term
     found = jnp.zeros((WIDE, PTS), f32)
@@ -471,7 +460,7 @@
     src, rden, pold, low, high, slot, cell, nrm, disp = call(
         start_kernel,
         (block, block, block, face, face, shape(1, PTS), shape(1, PTS, dtype=i32), shape(3, PTS), shape(3, PTS)),
-        (rhs, coef, pold, cell, part, nrm, disp),
+        [pltpu.with_memory_space_constraint(x, pltpu.HBM) for x in (rhs, coef, pold, cell, part, nrm, disp)],
         [pltpu.VMEM((CX, CY, CZ), f32)] * 2 + [pltpu.VMEM((1, PTS), i32), pltpu.SemaphoreType.DMA((7,))],
         name="start",
         far=range(7),

time: 162 us -> 153 us (0.944)
  local copies, waits for them, and re-layouts: 4.94 us -> 0.04 us
  Pallas kernels: 17.4 us -> 14 us
    unnamed x20 -> x6, local copies, waits for them, and re-layouts: 4.94 us -> 0.04 us
    pallas_call x10, Pallas kernels: 17.4 us -> 14 us  [call(): pl.pallas_call(kernel, out_shape=outs, in_specs=[spec(k) for k in range(l...]
where the time goes in v3:
time: 153 us
  blocking collectives  109 us (71%)
  starting transfers between devices  23.3 us (15%)
  Pallas kernels  14 us (9%)
  waiting for transfers between devices  5.4 us (4%)
    all_to_all x4, blocking collectives, across(): return lax.all_to_all(rows, 'dom', 0, 0, tiled=True)  70.8 us
    all_to_all x1, blocking collectives, body(): values = lax.all_to_all(spread_out, ('sub', 'lane'), 0, 0, tiled=True)  22.2 us
    ppermute x2, starting transfers between devices, pair(): fromhigh = lax.ppermute(low, axis, [(i + 1, i) for i in range(count - 1)])  17.4 us
    pallas_call x10, Pallas kernels, call(): pl.pallas_call(kernel, out_shape=outs, in_specs=[spec(k) for k in range(l...  14 us
    all_to_all x1, blocking collectives, body(): sums = lax.all_to_all(sums, ('sub', 'lane'), 0, 0, tiled=True)  12.1 us
    ppermute x2, starting transfers between devices, pair(): fromlow = lax.ppermute(high, axis, [(i, i + 1) for i in range(count - 1)])  5.91 us
    all_gather x1, blocking collectives, body(): strips = lax.all_gather(strips, 'lane')  4.35 us
    ppermute x2, waiting for transfers between devices, pair(): fromlow = lax.ppermute(high, axis, [(i, i + 1) for i in range(count - 1)])  4.06 us
  transfers between devices with their start and end apart: 4, of which 3 were waited for; matrix products, arithmetic and copies ran while one was open for 0% of the time, Pallas kernels for 0%

profile of v3, /device:TPU:1, one launch (start us, length us, event | category | flops | bytes accessed | tf_op | source)
XLA Modules:
  0.0 153.0 jit_solution(16490617121525148091)
XLA Ops:
  0.6 1.5 start.1
  2.1 16.1 %collective-permute-start = (f32[328,128]{1,0:T(8,128)S(1)}, f32[328,128]{1,0:T(8,128)S(1)}, u32[]{:S(2)}, u32[]{:S(2)}) collective-permute-start(f32[328,128]{1,0:T(8,128)S(1)} %get-tuple-element.36), channel_id=1, source_target_pairs={{2,0},{4,2},{6,4},{8,6},{10,8},{12,10},{14,12},{3,1},{5,3},{7,5},{... | collective-permute-start | bytes 503816 | tf_op jit(solution)/shard_map/ppermute | solution.py:452
  18.2 1.9 %collective-permute-start.1 = (f32[328,128]{1,0:T(8,128)S(1)}, f32[328,128]{1,0:T(8,128)S(1)}, u32[]{:S(2)}, u32[]{:S(2)}) collective-permute-start(f32[328,128]{1,0:T(8,128)S(1)} %get-tuple-element.37), channel_id=1, source_target_pairs={{0,2},{2,4},{4,6},{6,8},{8,10},{10,12},{12,14},{1,3},{3,5},{5,7},{... | collective-permute-start | bytes 503816 | tf_op jit(solution)/shard_map/ppermute | solution.py:453
  20.1 0.0 collective-permute-done.subhigh
  20.1 2.3 %collective-permute-done.1.sublow = f32[328,128]{1,0:T(8,128)S(1)} collective-permute-done((f32[328,128]{1,0:T(8,128)S(1)}, f32[328,128]{1,0:T(8,128)S(1)}, u32[]{:S(2)}, u32[]{:S(2)}) %collective-permute-start.1) | collective-permute-done | bytes 167968 | tf_op jit(solution)/shard_map/ppermute | solution.py:453
  22.4 0.1 dom_slabs.1
  22.4 1.3 collective-permute-start.2
  23.7 4.0 %collective-permute-start.3 = (f32[248,128]{1,0:T(8,128)S(1)}, f32[248,128]{1,0:T(8,128)S(1)}, u32[]{:S(2)}, u32[]{:S(2)}) collective-permute-start(f32[248,128]{1,0:T(8,128)S(1)} %get-tuple-element.40), channel_id=1, source_target_pairs={{0,16},{16,32},{32,48},{48,64},{64,80},{80,96},{96,112},{112,128},... | collective-permute-start | bytes 380936 | tf_op jit(solution)/shard_map/ppermute | solution.py:453
  27.7 0.1 pad_add_fusion.place
  27.8 1.3 collective-permute-done.2.domhigh.high
  29.1 1.8 %collective-permute-done.3.domlow.low = f32[248,128]{1,0:T(8,128)S(1)} collective-permute-done((f32[248,128]{1,0:T(8,128)S(1)}, f32[248,128]{1,0:T(8,128)S(1)}, u32[]{:S(2)}, u32[]{:S(2)}) %collective-permute-start.3) | collective-permute-done | bytes 127008 | tf_op jit(solution)/shard_map/ppermute | solution.py:453
  30.9 0.0 copy-start.2
  30.9 1.2 lane_strips.1
  32.1 0.0 copy-start
  32.1 4.3 %all-gather = f32[12,24,128]{2,1,0:T(8,128)S(1)} all-gather(f32[6,24,128]{2,1,0:T(8,128)S(1)} %get-tuple-element.44), channel_id=2, replica_groups=mesh['dom'=64,'sub'=8,'lane'=2] {'lane'}, dimensions={0}, use_global_device_ids=true | all-gather | bytes 221184 | tf_op jit(solution)/shard_map/all_gather | solution.py:478
  36.5 0.0 copy-done.2
  36.5 3.1 %first_fluid.1 = (f32[32,16,128]{2,1,0:T(8,128)S(1)}, f32[40,24,128]{2,1,0:T(8,128)S(1)}, f32[64,128]{1,0:T(8,128)S(1)}) custom-call(s32[2]{0:T(128)S(1)} %pad_add_fusion.place, f32[40,24,128]{2,1,0:T(8,128)S(1)} %get-tuple-element.42.esrc, f32[40,24,128]{2,1,0:T(8,128)S(1)} %get-tuple-element.41.erden, f32[40,24,128]{2,1,0:T(8,128)S(1)} %get-tuple-element.43.epold, ...), custom_call_target="tpu_custom_call" | custom-call | tf_op jit(solution)/shard_map/first_fluid/pallas_call | solution.py:430
  39.6 0.0 copy-start.1
  39.6 26.9 %all_to_all.60 = f32[64,1,128]{2,1,0:T(1,128)S(1)} all-to-all(f32[64,1,128]{2,1,0:T(1,128)S(1)} %bitcast.36), channel_id=1, replica_groups=mesh['dom'=64,'sub'=8,'lane'=2] {'dom'}, dimensions={0} | all-to-all | bytes 65536 | tf_op jit(solution)/shard_map/all_to_all | solution.py:457
  66.6 0.0 copy-done
  66.6 0.0 copy-done.1
  66.6 1.7 %first_structure.1 = (f32[64,128]{1,0:T(8,128)S(1)}, f32[16,512]{1,0:T(8,128)S(1)}, bf16[512,512]{1,0:T(8,128)(2,1)S(1)}, bf16[512,512]{1,0:T(8,128)(2,1)S(1)}) custom-call(f32[64,128]{1,0:T(8,128)S(1)} %bitcast.28, f32[3,512]{1,0:T(4,128)S(1)} %copy-done.1, f32[512,512]{1,0:T(8,128)S(1)} %copy-done), custom_call_target="tpu_custom_call" | custom-call | tf_op jit(solution)/shard_map/first_structure/pallas_call | solution.py:430
  68.3 14.6 %all_to_all.61 = f32[64,1,128]{2,1,0:T(1,128)S(1)} all-to-all(f32[64,1,128]{2,1,0:T(1,128)S(1)} %bitcast.37), channel_id=1, replica_groups=mesh['dom'=64,'sub'=8,'lane'=2] {'dom'}, dimensions={0} | all-to-all | bytes 65536 | tf_op jit(solution)/shard_map/all_to_all | solution.py:457
  82.9 0.3 hand_out.1
  83.2 22.2 %all_to_all.62.arrived = f32[16,8,128]{2,1,0:T(8,128)S(1)} all-to-all(f32[16,8,128]{2,1,0:T(8,128)S(1)} %hand_out.1), channel_id=1, replica_groups=mesh['dom'=64,'sub'=8,'lane'=2] {'sub','lane'}, dimensions={0} | all-to-all | bytes 131072 | tf_op jit(solution)/shard_map/all_to_all | solution.py:497
  105.4 3.9 %second_fluid.1 = (f32[32,16,128]{2,1,0:T(8,128)}, f32[64,128]{1,0:T(8,128)S(1)}) custom-call(s32[2]{0:T(128)S(1)} %pad_add_fusion.place, f32[40,24,128]{2,1,0:T(8,128)S(1)} %get-tuple-element.41.erden, f32[40,24,128]{2,1,0:T(8,128)S(1)} %get-tuple-element.47.xrden, f32[32,16,128]{2,1,0:T(8,128)S(1)} %get-tuple-element.48.before, ...), custom_call_target="tpu_custom_call" | custom-call | tf_op jit(solution)/shard_map/second_fluid/pallas_call | solution.py:430
  109.3 14.6 %all_to_all.63 = f32[64,1,128]{2,1,0:T(1,128)S(1)} all-to-all(f32[64,1,128]{2,1,0:T(1,128)S(1)} %bitcast.35), channel_id=1, replica_groups=mesh['dom'=64,'sub'=8,'lane'=2] {'dom'}, dimensions={0} | all-to-all | bytes 65536 | tf_op jit(solution)/shard_map/all_to_all | solution.py:457
  124.0 1.2 second_structure.1
  125.2 14.6 %all_to_all.64 = f32[64,1,128]{2,1,0:T(1,128)S(1)} all-to-all(f32[64,1,128]{2,1,0:T(1,128)S(1)} %bitcast.31), channel_id=1, replica_groups=mesh['dom'=64,'sub'=8,'lane'=2] {'dom'}, dimensions={0} | all-to-all | bytes 65536 | tf_op jit(solution)/shard_map/all_to_all | solution.py:457
  139.8 0.2 arrive.1
  140.1 12.1 %all_to_all.65 = f32[16,1,128]{2,1,0:T(1,128)S(1)} all-to-all(f32[16,1,128]{2,1,0:T(1,128)S(1)} %bitcast.38), channel_id=1, replica_groups=mesh['dom'=64,'sub'=8,'lane'=2] {'sub','lane'}, dimensions={0} | all-to-all | bytes 16384 | tf_op jit(solution)/shard_map/all_to_all | solution.py:515
  152.2 0.8 finish.1
Async XLA Ops:
  2.1 18.0 %collective-permute-start = (f32[328,128]{1,0:T(8,128)S(1)}, f32[328,128]{1,0:T(8,128)S(1)}, u32[]{:S(2)}, u32[]{:S(2)}) collective-permute-start(f32[328,128]{1,0:T(8,128)S(1)} %get-tuple-element.36), channel_id=1, source_target_pairs={{2,0},{4,2},{6,4},{8,6},{10,8},{12,10},{14,12},{3,1},{5,3},{7,5},{... | collective-permute-start | bytes 503816 | tf_op jit(solution)/shard_map/ppermute | solution.py:452
  18.2 4.2 %collective-permute-start.1 = (f32[328,128]{1,0:T(8,128)S(1)}, f32[328,128]{1,0:T(8,128)S(1)}, u32[]{:S(2)}, u32[]{:S(2)}) collective-permute-start(f32[328,128]{1,0:T(8,128)S(1)} %get-tuple-element.37), channel_id=1, source_target_pairs={{0,2},{2,4},{4,6},{6,8},{8,10},{10,12},{12,14},{1,3},{3,5},{5,7},{... | collective-permute-start | bytes 503816 | tf_op jit(solution)/shard_map/ppermute | solution.py:453
  22.4 6.7 %collective-permute-start.2 = (f32[248,128]{1,0:T(8,128)S(1)}, f32[248,128]{1,0:T(8,128)S(1)}, u32[]{:S(2)}, u32[]{:S(2)}) collective-permute-start(f32[248,128]{1,0:T(8,128)S(1)} %get-tuple-element.39), channel_id=1, source_target_pairs={{16,0},{32,16},{48,32},{64,48},{80,64},{96,80},{112,96},{128,112},... | collective-permute-start | bytes 380936 | tf_op jit(solution)/shard_map/ppermute | solution.py:452
  23.7 7.2 %collective-permute-start.3 = (f32[248,128]{1,0:T(8,128)S(1)}, f32[248,128]{1,0:T(8,128)S(1)}, u32[]{:S(2)}, u32[]{:S(2)}) collective-permute-start(f32[248,128]{1,0:T(8,128)S(1)} %get-tuple-element.40), channel_id=1, source_target_pairs={{0,16},{16,32},{32,48},{48,64},{64,80},{80,96},{96,112},{112,128},... | collective-permute-start | bytes 380936 | tf_op jit(solution)/shard_map/ppermute | solution.py:453
  30.9 5.5 %copy-start.2 = (f32[3,256]{1,0:T(4,128)S(1)}, f32[3,256]{1,0:T(4,128)}, u32[]{:S(2)}) copy-start(f32[3,256]{1,0:T(4,128)} %coords.1) | copy-start | bytes 9220
  32.1 34.5 %copy-start = (f32[512,512]{1,0:T(8,128)S(1)}, f32[512,512]{1,0:T(8,128)}, u32[]{:S(2)}) copy-start(f32[512,512]{1,0:T(8,128)} %shell.3) | copy-start | bytes 3145732
  39.6 27.0 %copy-start.1 = (f32[3,512]{1,0:T(4,128)S(1)}, f32[3,512]{1,0:T(4,128)}, u32[]{:S(2)}) copy-start(f32[3,512]{1,0:T(4,128)} %nodes.1) | copy-start | bytes 18436

commit v4 on v3

v4 whole, which is shorter than its diff:
```python
import math

import jax
import jax.numpy as jnp
from jax import lax
from jax.experimental import pallas as pl
from jax.experimental.pallas import tpu as pltpu
from jax.sharding import PartitionSpec as P

SWEEPS = 4
DOM, SUB, LANE = 64, 8, 2
CX, CY, CZ = 32, 16, 128
PTS, NS, CAP = 256, 512, 8
RX, RY = CX + 8, CY + 8
WIDE = 16
FACE, SLAB = 10 * CX, 10 * RY

source_gain = 16.0
relaxation = 0.5
inv_radius_sq = 11.111111
epsilon = 1e-06

f32, bf16, i32 = jnp.float32, jnp.bfloat16, jnp.int32
NN = (((1,), (0,)), ((), ()))
NT = (((1,), (1,)), ((), ()))


def pieces(x, count):
    parts = []
    for _ in range(count - 1):
        head = x.astype(bf16)
        parts.append(head)
        x = x - head.astype(f32)
    parts.append(x.astype(bf16))
    return parts


def mxu(a, b, dims):
    return lax.dot_general(a, b, dims, preferred_element_type=f32)


def ones_at(rows, index):
    at = lax.broadcasted_iota(i32, (rows, index.shape[1]), 0)
    return at == index


def as_ones(mask):
    return jnp.where(mask, 1.0, 0.0).astype(bf16)


def spread(rows, z, values, edge=None):
    if edge is None:
        parts = pieces(jnp.where(ones_at(CZ, z), values, 0.0), 2)
    else:
        beside = jnp.where(edge == 0, z, z - (CZ - 16))
        parts = []
        for part in pieces(jnp.where(ones_at(16, beside), values, 0.0), 2):
            zero = jnp.zeros_like(part)
            first, last = jnp.where(edge == 0, part, zero), jnp.where(edge == 0, zero, part)
            parts.append(jnp.concatenate([first, jnp.zeros((CZ - 32, PTS), bf16), last], axis=0))
    total = None
    for part in parts:
        term = mxu(rows, part, NT)
        total = term if total is None else total + term
    return total


def halves(row):
    return row[:, 0:128], row[:, 128:256]


def joined(ref_rows):
    return jnp.concatenate([ref_rows[0:1], ref_rows[1:2]], axis=1)


def up_down(core, beside, across):
    return jnp.where(core == 0, beside, across), jnp.where(core == 0, across, beside)


def start_kernel(
    rhs_far, coef_far, pold_far, cell_far, part_far, nrm_far, disp_far, coords_far,
    src, rden, pold, strips, slot, cell, nrm, disp, coords, rhs, coef, part, sems,
):
    pairs = (
        (cell_far, cell), (part_far, part), (nrm_far, nrm), (disp_far, disp),
        (rhs_far, rhs), (pold_far, pold), (coef_far, coef), (coords_far, coords),
    )
    copies = [pltpu.make_async_copy(a, b, sems.at[k]) for k, (a, b) in enumerate(pairs)]
    for copy in copies:
        copy.start()
    for copy in copies[:4]:
        copy.wait()
    points = cell[...]
    values = source_gain * jnp.sum(disp[...] * nrm[...], axis=0, keepdims=True)
    added = spread(as_ones(ones_at(CX * CY, points >> 7)), points & 127, values)
    owner = ones_at(DOM, part[...])
    earlier = lax.broadcasted_iota(i32, (PTS, PTS), 0) < lax.broadcasted_iota(i32, (PTS, PTS), 1)
    before = mxu(as_ones(owner), as_ones(earlier), NN)
    rank = jnp.sum(jnp.where(owner, before, 0.0), axis=0, keepdims=True)
    slot[...] = part[...].astype(f32) * CAP + rank
    copies[4].wait()
    src[...] = rhs[...] + added.reshape(CX, CY, CZ)
    copies[6].wait()
    rden[...] = 1.0 / (6.0 + coef[...])
    copies[5].wait()
    copies[7].wait()
    shift = jnp.where(lax.axis_index("lane") == 0, 4, 0)
    at = lax.broadcasted_iota(i32, (CY, CZ), 1)
    for x4 in range(4):
        strips[x4 * CY : (x4 + 1) * CY, :] = packed([lambda k, f=f: f[4 * k + x4] for f in (src, rden, pold)], at, shift)
    tail = [*halves(points.astype(f32)), *halves(slot[...]), jnp.zeros((4, CZ), f32)]
    strips[64:72, :] = jnp.concatenate(tail, axis=0)


def packed(fields, at, shift):
    total = jnp.zeros(at.shape, f32)
    for k in range(8):
        for number, field in enumerate(fields):
            lo = 16 * k + 4 * number
            total = jnp.where((at >= lo) & (at < lo + 4), pltpu.roll(field(k), lax.rem(lo + shift, 128), 1), total)
    return total


def unpacked(rows, lo, lane, keep):
    return jnp.where(keep, pltpu.roll(rows, lax.rem(256 - lo - 4 * lane, 128), 1), 0.0)


def edges(lane, rows):
    at = lax.broadcasted_iota(i32, (rows, CZ), 1)
    return jnp.where(lane == 0, at, CZ - 1 - at) < 4


def faces_kernel(src, rden, pold, cell, lanes, across, beside):
    core, lane = lax.rem(lax.axis_index("sub"), 2), lax.axis_index("lane")
    for field, own, width in ((0, src, 3), (3, rden, 3), (6, pold, 4)):
        for k in range(width):
            at = (field + k) * CX
            low, high = own[:, k, :], own[:, CY - width + k, :]
            beside[at : at + CX, :], across[at : at + CX, :] = up_down(core, high, low)
    other = lanes[1 - lane]
    for x4 in range(4):
        at, low, high = FACE + 4 * x4, other[x4 * CY : x4 * CY + 4], other[(x4 + 1) * CY - 4 : (x4 + 1) * CY]
        beside[at : at + 4, :], across[at : at + 4, :] = up_down(core, high, low)
    tail = jnp.concatenate([*halves(cell[...].astype(f32)), other[64:66], jnp.zeros((4, CZ), f32)], axis=0)
    beside[FACE + 16 : FACE + 24, :] = tail
    across[FACE + 16 : FACE + 24, :] = tail


def dom_kernel(
    src, rden, pold, cell, slot, fromacross, cores, lanes, beside, across, subhigh, sublow, beyond, tails, slabs
):
    core, lane = lax.rem(lax.axis_index("sub"), 2), lax.axis_index("lane")
    subhigh[...], sublow[...] = up_down(core, cores[1 - core], fromacross[...])
    other = lanes[1 - lane]
    cellhigh, celllow = subhigh[FACE + 16 : FACE + 24], sublow[FACE + 16 : FACE + 24]
    tail = [*halves(cell[...].astype(f32)), cellhigh[0:2], celllow[0:2], *halves(slot[...])]
    tails[0:8] = jnp.concatenate(tail, axis=0)
    tails[8:16] = jnp.concatenate([other[64:66], cellhigh[2:4], celllow[2:4], other[66:68]], axis=0)
    for x4 in range(4):
        at = FACE + 4 * x4
        sides = subhigh[at : at + 4], sublow[at : at + 4]
        beyond[x4] = jnp.concatenate([other[x4 * CY : (x4 + 1) * CY], *sides], axis=0)
    at = lax.broadcasted_iota(i32, (RY, CZ), 1)
    low, high = slabs.at[0], slabs.at[1]
    for out, base3, base4, group in ((low, 0, 0, 0), (high, CX - 3, CX - 4, 7)):
        for field, own, width, base in ((0, src, 3, base3), (3, rden, 3, base3), (6, pold, 4, base4)):
            for k in range(width):
                x, row = base + k, (field + k) * RY
                out[row : row + CY, :] = own[x]
                rows = [subhigh[(field + j) * CX + x : (field + j) * CX + x + 1] for j in range(width)]
                rows += [jnp.zeros((1, CZ), f32)] * (8 - 2 * width)
                rows += [sublow[(field + j) * CX + x : (field + j) * CX + x + 1] for j in range(width)]
                out[row + CY : row + RY, :] = jnp.concatenate(rows, axis=0)
        total = jnp.zeros((RY, CZ), f32)
        for j in range(4):
            moved = pltpu.roll(beyond[j], (16 * j - 16 * group) % 128, 1)
            total = jnp.where((at >= 16 * j) & (at < 16 * j + 16), moved, total)
        out[SLAB : SLAB + RY, :] = total
        out[SLAB + RY : SLAB + RY + 16, :] = tails[...]
    beside[...], across[...] = up_down(lax.rem(lax.axis_index("dom"), 2), high[...], low[...])


def ring_kernel(src, rden, pold, subhigh, sublow, beyond, esrc, erden, epold, xsrc, xrden, xpold):
    for field, own, width, ext in ((0, src, 3, esrc), (3, rden, 3, erden), (6, pold, 4, epold)):
        ext[:, 0:CY, :] = own[...]
        if width == 3:
            ext[:, CY:RY, :] = jnp.zeros((CX, 8, CZ), f32)
        for k in range(width):
            at = (field + k) * CX
            ext[:, CY + k, :] = subhigh[at : at + CX]
            ext[:, RY - width + k, :] = sublow[at : at + CX]
    lane = lax.axis_index("lane")
    keep = edges(lane, RY)
    for x4 in range(4):
        rows = beyond[x4]
        for field, beside in enumerate((xsrc, xrden, xpold)):
            for k in range(8):
                beside[4 * k + x4] = unpacked(rows, 16 * k + 4 * field, lane, keep)


def near(width):
    return [*range(CX + width), *range(RX - width, RX)]


def ring(own, other, own_halo=None, other_halo=None):
    def layer(x):
        if x < CX or own_halo is None:
            return jnp.concatenate([own[x], other[x]], axis=1)
        return jnp.concatenate([own_halo(x - CX), other_halo[x - CX]], axis=1)

    return layer


def sweep(now, out, source, scale, width):
    for x in near(width):
        here = now(x)
        total = now((x + 1) % RX) + now((x - 1) % RX)
        total = total + (pltpu.roll(here, RY - 1, 0) + pltpu.roll(here, 1, 0))
        total = total + (pltpu.roll(here, 2 * CZ - 1, 1) + pltpu.roll(here, 1, 1))
        total = (source(x) + total) * scale(x)
        out[0][x], out[1][x] = total[:, 0:CZ], total[:, CZ : 2 * CZ]


def last_sweep(now, source, scale, write):
    for x in range(CX):
        here = now[0][x]
        total = now[0][(x + 1) % RX, 0:CY] + now[0][(x - 1) % RX, 0:CY]
        total = total + (pltpu.roll(here, RY - 1, 0) + pltpu.roll(here, 1, 0))[0:CY]
        wide = jnp.concatenate([here[0:CY], now[1][x, 0:CY]], axis=1)
        beside = pltpu.roll(wide, 2 * CZ - 1, 1) + pltpu.roll(wide, 1, 1)
        write(x, (source[x, 0:CY] + (total + beside[:, 0:CZ])) * scale[x, 0:CY])


def forces_at(pressure, points, nrm):
    at_z = as_ones(ones_at(CZ, points & 127))
    total = None
    for part in pieces(pressure, 2):
        term = mxu(part, at_z, NN)
        total = term if total is None else total + term
    press = jnp.sum(jnp.where(ones_at(CX * CY, points >> 7), total, 0.0), axis=0, keepdims=True)
    return [press * nrm[c : c + 1, :] for c in range(3)]


def first_fluid_kernel(
    esrc, erden, epold, xsrc, xrden, xpold, doms, fromacross, tails, cell, nrm, coords, disp, slot,
    pressure, hrden0, hrden1, meta, sending, hsrc1, hpold1, domhigh, domlow, even0, even1, odd0, odd1,
):
    lane, pair = lax.axis_index("lane"), lax.rem(lax.axis_index("dom"), 2)
    domhigh[...], domlow[...] = up_down(pair, doms[1 - pair], fromacross[...])
    keep = edges(lane, RY)
    for base, slab in ((0, domhigh), (4, domlow)):
        rows = slab[SLAB : SLAB + RY]
        for j in range(4):
            for field, halo in enumerate((hsrc1, hrden1, hpold1)):
                halo[base + j] = unpacked(rows, 16 * j + 4 * field, lane, keep)

    def halo(field, width):
        def layer(x):
            slab, k = (domhigh, x) if x < 4 else (domlow, x - (8 - width))
            return slab[(field + k) * RY : (field + k + 1) * RY]

        return layer

    for x in range(8):
        hrden0[x] = jnp.zeros((RY, CZ), f32) if x in (3, 4) else halo(3, 3)(x)
    source = ring(esrc, xsrc, halo(0, 3), hsrc1)
    scale = ring(erden, xrden, halo(3, 3), hrden1)
    even, odd = (even0, even1), (odd0, odd1)
    sweep(ring(epold, xpold, halo(6, 4), hpold1), even, source, scale, 3)
    sweep(ring(*even), odd, source, scale, 2)
    sweep(ring(*odd), even, source, scale, 1)

    def write(x, value):
        pressure[x] = value

    last_sweep(even, esrc, erden, write)
    slots = slot[...].astype(i32)
    values = forces_at(pressure[...].reshape(CX * CY, CZ), cell[...], nrm)
    values += [coords[c : c + 1, :] for c in range(3)]
    values += [disp[c : c + 1, :] for c in range(3)]
    values += [nrm[c : c + 1, :] for c in range(3)]
    values += [jnp.ones((1, PTS), f32)]
    sending[...] = to_slots(values, slots, 3)
    for tile in range(2):
        own = tails[8 * tile : 8 * tile + 8]
        at = SLAB + RY + 8 * tile
        up, down = domhigh[at : at + 8], domlow[at : at + 8]
        meta[24 * tile : 24 * tile + 24] = jnp.concatenate([own[0:6], up[0:6], down[0:6], own[6:], up[6:], down[6:]], axis=0)


def placed(values, points, dx, dy, edge):
    x, y, z = points >> 11, (points >> 7) & 15, points & 127
    if dx == 1:
        x = jnp.where(x < 3, x, -1000)
    elif dx == 2:
        x = jnp.where(x >= CX - 3, x - (CX - 8), -1000)
    if dy == 1:
        y = jnp.where(y < 3, y, -1000000)
    elif dy == 2:
        y = jnp.where(y >= CY - 3, y - (CY - 8), -1000000)
    wide, deep = CY if dy == 0 else 8, CX if dx == 0 else 8
    return spread(as_ones(ones_at(deep * wide, x * wide + y)), z, values, edge).reshape(deep, wide, CZ)


def own_rows_kernel(values, meta, src0, src1):
    lane = lax.axis_index("lane")
    for tile, source in enumerate((src0, src1)):
        parts = []
        for dx in range(3):
            at, row = 6 * tile + 2 * dx, 24 * tile + 6 * dx
            points = joined(meta[row : row + 2]).astype(i32)
            parts.append(placed(joined(values[at : at + 2]), points, dx, 0, None if tile == 0 else lane))
        source[0:CX] = parts[0]
        source[CX:RX] = parts[1] + parts[2]


def second_fluid_kernel(
    erden, xrden, hrden0, hrden1, before, own0, own1, fromacross, cores, meta, cell, nrm, slot,
    pressure_far, sending, src0, src1, even0, even1, odd0, odd1, pressure, fromhigh, fromlow, sem,
):
    lane, core = lax.axis_index("lane"), lax.rem(lax.axis_index("sub"), 2)
    fromhigh[...], fromlow[...] = up_down(core, cores[1 - core], fromacross[...])
    for tile, (source, now, own, scale, halo) in enumerate(
        ((src0, even0, own0, erden, hrden0), (src1, even1, own1, xrden, hrden1))
    ):
        beside = [None] * 3
        for dy, values in ((1, fromhigh), (2, fromlow)):
            for dx in range(3):
                at, row = 6 * tile + 2 * dx, 24 * tile + 6 * dx + 2 * dy
                points = joined(meta[row : row + 2]).astype(i32)
                part = placed(joined(values[at : at + 2]), points, dx, dy, None if tile == 0 else lane)
                beside[dx] = part if dy == 1 else beside[dx] + part
        for ys, part in ((slice(0, CY), own[0:CX]), (slice(CY, RY), beside[0])):
            source[0:CX, ys, :] = part
            now[0:CX, ys, :] = part * scale[:, ys, :]
        for ys, part in ((slice(0, CY), own[CX:RX]), (slice(CY, RY), beside[1] + beside[2])):
            source[CX:RX, ys, :] = part
            now[CX:RX, ys, :] = part * halo[:, ys, :]
    even, odd = (even0, even1), (odd0, odd1)
    source = ring(src0, src1)
    scale = ring(erden, xrden, lambda x: hrden0[x], hrden1)
    sweep(ring(*even), odd, source, scale, 2)
    sweep(ring(*odd), even, source, scale, 1)

    def write(x, value):
        pressure[x] = before[x] + value

    last_sweep(even, src0, erden, write)
    copy = pltpu.make_async_copy(pressure, pressure_far, sem)
    copy.start()
    sending[...] = to_slots(forces_at(pressure[...].reshape(CX * CY, CZ), cell[...], nrm), slot[...].astype(i32), 2)
    copy.wait()


def to_slots(values, slots, count):
    rank = slots & 7
    filler = [jnp.zeros((1, PTS), f32)] * (WIDE - len(values))
    block = jnp.concatenate(list(values) + filler, axis=0)
    stacked = jnp.concatenate([jnp.where(rank == r, block, 0.0) for r in range(CAP)], axis=0)
    owner = as_ones(ones_at(DOM, slots >> 3))
    total = None
    for part in pieces(stacked, count):
        term = mxu(owner, part, NT)
        total = term if total is None else total + term
    return total


def from_slots(arrived, slots):
    rank = slots & 7
    owner = as_ones(ones_at(DOM, slots >> 3))
    flat = arrived.T
    total = None
    for part in pieces(flat, 2):
        term = mxu(part, owner, NN)
        total = term if total is None else total + term
    found = jnp.zeros((WIDE, PTS), f32)
    for r in range(CAP):
        found = found + jnp.where(rank == r, total[r * WIDE : (r + 1) * WIDE], 0.0)
    return found


def by_slot(received):
    flat = received.T
    return jnp.concatenate([flat[r * WIDE : (r + 1) * WIDE] for r in range(CAP)], axis=1)


def by_row(values):
    flat = jnp.concatenate([values[:, r * DOM : (r + 1) * DOM] for r in range(CAP)], axis=0)
    return flat.T


def product(left, head, tail, dims):
    a, b = pieces(left, 2)
    rows = left.shape[0]
    both = mxu(jnp.concatenate([a, b], axis=0), head, dims)
    return both[:rows] + both[rows:] + mxu(a, tail, dims)


def mapped_back(forces, khead, ktail, shell):
    loading = product(forces, khead, ktail, NN) * (1.0 / math.sqrt(PTS))
    shead, stail = pieces(shell, 2)
    displaced = loading + product(loading, shead, stail, NN)
    return product(displaced, khead, ktail, NT) * (1.0 / math.sqrt(NS))


def first_structure_kernel(received, nodes, shell, returned, mapped, khead, ktail):
    for r in range(CAP):
        distance = None
        for c in range(3):
            lane = r * WIDE + 3 + c
            gap = received[:, lane : lane + 1] - nodes[c : c + 1, :]
            distance = gap * gap if distance is None else distance + gap * gap
        weight = jnp.exp(-distance * inv_radius_sq)
        head, tail = pieces(weight, 2)
        khead[r * DOM : (r + 1) * DOM, :] = head
        ktail[r * DOM : (r + 1) * DOM, :] = tail
    held = by_slot(received[...])
    back = mapped_back(held[0:WIDE], khead[...], ktail[...], shell[...])
    mapped[...] = back
    moved = (source_gain * relaxation) * jnp.sum(held[9:12] * (back[0:3] - held[6:9]), axis=0, keepdims=True)
    rows = jnp.concatenate([moved, jnp.zeros((WIDE - 1, NS), f32)], axis=0)
    own = by_row(rows)
    at = lax.broadcasted_iota(i32, own.shape, 0)
    above = jnp.where(at == DOM - 1, 0.0, pltpu.roll(own, DOM - 1, 0))
    below = jnp.where(at == 0, 0.0, pltpu.roll(own, 1, 0))
    both_lanes = own + pltpu.roll(above, 1, 1) + pltpu.roll(below, 2, 1)
    returned[0:DOM] = both_lanes
    returned[DOM : 2 * DOM] = both_lanes


def second_structure_kernel(received, before, mapped, khead, ktail, shell, returned):
    forces = by_slot(received[...])
    held = by_slot(before[...])
    back = mapped_back(forces, khead[...], ktail[...], shell[...])
    t0, t1, d0, used = mapped[0:3, :], back[0:3], held[6:9], held[12:13]
    r0 = t0 - d0
    r1 = t1 - (d0 + relaxation * r0)
    delta = r1 - r0
    sums = []
    for term in (delta * r1, delta * delta, r1 * r1):
        inner = jnp.sum(term * used, axis=0, keepdims=True)
        sums.append(jnp.broadcast_to(jnp.sum(inner, axis=1, keepdims=True), (1, NS)))
    rows = jnp.concatenate([t1, t0, *sums, jnp.zeros((WIDE - 9, NS), f32)], axis=0)
    returned[...] = by_row(rows)


def hand_out_kernel(arrived, meta, out):
    lane = lax.axis_index("lane")
    rows = []
    for tile in range(2):
        owner = lane if tile == 0 else 1 - lane
        held = arrived[pl.ds(pl.multiple_of(owner * DOM, DOM), DOM), :]
        for dx in range(3):
            at = 24 * tile + 18 + 2 * dx
            rows += halves(from_slots(held, joined(meta[at : at + 2]).astype(i32))[dx : dx + 1])
    out[...] = jnp.concatenate([*rows, jnp.zeros((4, 128), f32)], axis=0)


def arrive_kernel(arrived, slot, found, out):
    held = arrived[...]
    found[...] = from_slots(held, slot[...].astype(i32))
    total = jnp.sum(held, axis=0, keepdims=True)
    for k in range(SUB * LANE):
        out[k : k + 1, :] = total


def finish_kernel(found, sums, disp, rms):
    total = jnp.sum(sums[...], axis=0, keepdims=True)
    vr, vv, rr = total[:, 6:7], total[:, 7:8], total[:, 8:9]
    t1, t0 = found[0:3, :], found[3:6, :]
    disp[...] = t1 - (vr / (vv + epsilon)) * (t1 - t0)
    count = 3.0 * PTS * DOM * SUB * LANE
    rms[...] = jnp.sqrt(rr / count)


def shape(*dims, dtype=f32):
    return jax.ShapeDtypeStruct(dims, dtype)


def call(kernel, outs, args, scratch=(), name=None, far=(), far_out=()):
    def spec(k):
        space = pltpu.HBM if k in far else pltpu.VMEM
        return pl.BlockSpec(memory_space=space)

    return pl.pallas_call(
        kernel,
        out_shape=outs,
        in_specs=[spec(k) for k in range(len(args))],
        out_specs=tuple(
            pl.BlockSpec(memory_space=pltpu.HBM if k in far_out else pltpu.VMEM) for k in range(len(outs))
        ),
        scratch_shapes=list(scratch),
        compiler_params=pltpu.CompilerParams(vmem_limit_bytes=40 * 1024 * 1024),
        name=name,
    )(*args)


def body(rhs, coef, pold, cell_index, nrm, coords, partner, nodes, shell, disp):
    cell = cell_index.reshape(1, PTS)
    part = partner.reshape(1, PTS)
    block, main, halo = shape(CX, CY, CZ), shape(CX, RY, CZ), shape(8, RY, CZ)
    row = shape(DOM, CAP * WIDE)
    def swap(across, beside, axis):
        count = lax.axis_size(axis)
        swaps = [(i + k, i + 1 - k) for i in range(1, count - 1, 2) for k in (0, 1)]
        pairs = [[i, i + 1] for i in range(0, count, 2)]
        return lax.ppermute(across, axis, swaps), lax.all_gather(beside, axis, axis_index_groups=pairs)

    def across(rows):
        return lax.all_to_all(rows, "dom", 0, 0, tiled=True)

    face, slab = shape(FACE + 24, CZ), shape(SLAB + RY + 16, CZ)
    src, rden, pold, strips, slot, cell, nrm, disp, coords = call(
        start_kernel,
        (block, block, block, shape(72, CZ), shape(1, PTS), shape(1, PTS, dtype=i32), *[shape(3, PTS)] * 3),
        [pltpu.with_memory_space_constraint(x, pltpu.HBM) for x in (rhs, coef, pold, cell, part, nrm, disp, coords)],
        [pltpu.VMEM((CX, CY, CZ), f32)] * 2 + [pltpu.VMEM((1, PTS), i32), pltpu.SemaphoreType.DMA((8,))],
        name="start",
        far=range(8),
    )
    lanes = lax.all_gather(strips, "lane")
    further, beside = call(faces_kernel, (face, face), (src, rden, pold, cell, lanes), name="sub_faces")
    fromacross, cores = swap(further, beside, "sub")
    beside, further, subhigh, sublow, beyond, tails = call(
        dom_kernel,
        (slab, slab, face, face, shape(4, RY, CZ), shape(16, CZ)),
        (src, rden, pold, cell, slot, fromacross, cores, lanes),
        [pltpu.VMEM((2, SLAB + RY + 16, CZ), f32)],
        name="dom_slabs",
    )
    fromacross, doms = swap(further, beside, "dom")
    esrc, erden, epold, xsrc, xrden, xpold = call(
        ring_kernel, (main,) * 6, (src, rden, pold, subhigh, sublow, beyond), name="ring_fields"
    )
    grid = pltpu.VMEM((RX, RY, CZ), f32)
    pressure, hrden0, hrden1, meta, sending = call(
        first_fluid_kernel,
        (block, halo, halo, shape(48, CZ), row),
        (esrc, erden, epold, xsrc, xrden, xpold, doms, fromacross, tails, cell, nrm, coords, disp, slot),
        [pltpu.VMEM((8, RY, CZ), f32)] * 2 + [pltpu.VMEM((SLAB + RY + 16, CZ), f32)] * 2 + [grid] * 4,
        name="first_fluid",
    )
    received = across(sending)
    square = shape(NS, NS, dtype=bf16)
    returned, mapped, khead, ktail = call(
        first_structure_kernel,
        (shape(2 * DOM, CAP * WIDE), shape(WIDE, NS), square, square),
        (received, nodes, shell),
        name="first_structure",
    )
    arrived = lax.all_to_all(returned, ("lane", "dom"), 0, 0, tiled=True)
    (values,) = call(hand_out_kernel, (shape(16, 128),), (arrived, meta), name="hand_out")
    fromacross, cores = swap(values, values, "sub")
    own_rows = shape(RX, CY, CZ)
    own0, own1 = call(own_rows_kernel, (own_rows, own_rows), (values, meta), name="own_rows")
    pressure, sending = call(
        second_fluid_kernel,
        (block, row),
        (erden, xrden, hrden0, hrden1, pressure, own0, own1, fromacross, cores, meta, cell, nrm, slot),
        [grid] * 6
        + [pltpu.VMEM((CX, CY, CZ), f32), *[pltpu.VMEM((16, 128), f32)] * 2, pltpu.SemaphoreType.DMA],
        name="second_fluid",
        far_out=(0,),
    )
    again = across(sending)
    (returned,) = call(
        second_structure_kernel, (row,), (again, received, mapped, khead, ktail, shell), name="second_structure"
    )
    arrived = across(returned)
    found, sums = call(
        arrive_kernel, (shape(WIDE, PTS), shape(SUB * LANE, 128)), (arrived, slot), name="arrive"
    )
    sums = lax.all_to_all(sums, ("sub", "lane"), 0, 0, tiled=True)
    disp_new, rms = call(finish_kernel, (shape(3, PTS), shape(1, 1)), (found, sums), name="finish")
    return pressure, disp_new, rms.reshape(())


def solution(mesh):
    every = ("dom", "sub", "lane")
    grid, points = P(*every), P(None, every)
    return jax.shard_map(
        body,
        mesh=mesh,
        in_specs=(grid, grid, grid, P(every), points, points, P(every, None), points, P(every, None), points),
        out_specs=(grid, points, P()),
        check_vma=False,
    )
```

time: 153 us -> 145 us (0.948)
  starting transfers between devices: 23.3 us -> 14.6 us
  blocking collectives: 109 us -> 116 us
  waiting for transfers between devices: 5.4 us -> 0.01 us
    all_gather x1 -> x4, blocking collectives: 4.35 us -> 22.6 us  [the longest x3 18.5 us: swap(): lax.all_gather(beside, axis, axis_index_groups=pairs)]
    all_to_all x4 -> x3, blocking collectives: 70.8 us -> 58.1 us  [across(): return lax.all_to_all(rows, 'dom', 0, 0, tiled=True)]
    ppermute x4 -> x3, starting transfers between devices: 23.3 us -> 14.6 us  [swap(): lax.ppermute(across, axis, swaps)]
    all_to_all x1, blocking collectives: 12.1 us -> 18 us  [body(): sums = lax.all_to_all(sums, ('sub', 'lane'), 0, 0, tiled=True)]
    ppermute x4 -> x3, waiting for transfers between devices: 5.4 us -> 0.01 us  [swap(): lax.ppermute(across, axis, swaps)]
    all_to_all x1, blocking collectives: 22.2 us -> 17.3 us  [body(): arrived = lax.all_to_all(returned, ('lane', 'dom'), 0, 0, tiled=True)]
    pallas_call x10 -> x12, Pallas kernels: 14 us -> 12.8 us  [call(): pl.pallas_call(kernel, out_shape=outs, in_specs=[spec(k) for k in range(l...]
  transfers between devices with their start and end apart: 4 -> 3, of which waited for: 3 -> 0; matrix products, arithmetic and copies ran while one was open for 0% -> 0% of each run, Pallas kernels for 0% -> 1%
where the time goes in v4:
time: 145 us; the launch traced here: 144 us
  blocking collectives  116 us (80%)
  starting transfers between devices  14.6 us (10%)
  Pallas kernels  12.8 us (9%)
    all_to_all x3, blocking collectives, across(): return lax.all_to_all(rows, 'dom', 0, 0, tiled=True)  58.1 us
    all_gather x3, blocking collectives, swap(): lax.all_gather(beside, axis, axis_index_groups=pairs)  18.5 us
    all_to_all x1, blocking collectives, body(): sums = lax.all_to_all(sums, ('sub', 'lane'), 0, 0, tiled=True)  18 us
    all_to_all x1, blocking collectives, body(): arrived = lax.all_to_all(returned, ('lane', 'dom'), 0, 0, tiled=True)  17.3 us
    ppermute x3, starting transfers between devices, swap(): lax.ppermute(across, axis, swaps)  14.6 us
    pallas_call x12, Pallas kernels, call(): pl.pallas_call(kernel, out_shape=outs, in_specs=[spec(k) for k in range(l...  12.8 us
    all_gather x1, blocking collectives, body(): lanes = lax.all_gather(strips, 'lane')  4.04 us
  transfers between devices with their start and end apart: 3, of which 0 were waited for; matrix products, arithmetic and copies ran while one was open for 0% of the time, Pallas kernels for 1%

profile of v4, /device:TPU:1, one launch (start us, length us, event | category | flops | bytes accessed | tf_op | source)
XLA Modules:
  0.0 144.2 jit_solution(6691331822556226405)
XLA Ops:
  0.6 1.6 %start.1 = (f32[32,16,128]{2,1,0:T(8,128)S(1)}, f32[32,16,128]{2,1,0:T(8,128)S(1)}, f32[32,16,128]{2,1,0:T(8,128)S(1)}, f32[72,128]{1,0:T(8,128)S(1)}, f32[1,256...) custom-call(f32[32,16,128]{2,1,0:T(8,128)} %rhs_far.1, ...), custom_call_target="tpu_custom_call" | custom-call | tf_op jit(solution)/shard_map/start/pallas_call | solution.py:485
  2.2 4.0 %all-gather = f32[144,128]{1,0:T(8,128)S(1)} all-gather(f32[72,128]{1,0:T(8,128)S(1)} %get-tuple-element.48), channel_id=2, replica_groups=mesh['dom'=64,'sub'=8,'lane'=2] {'lane'}, dimensions={0}, use_global_device_ids=true | all-gather | bytes 110592 | tf_op jit(solution)/shard_map/all_gather | solution.py:521
  6.3 0.3 sub_faces.1
  6.5 6.0 %collective-permute-start = (f32[344,128]{1,0:T(8,128)S(1)}, f32[344,128]{1,0:T(8,128)S(1)}, u32[]{:S(2)}, u32[]{:S(2)}) collective-permute-start(f32[344,128]{1,0:T(8,128)S(1)} %get-tuple-element.49), channel_id=1, source_target_pairs={{2,4},{4,2},{6,8},{8,6},{10,12},{12,10},{3,5},{5,3},{7,9},{9,7},{1... | collective-permute-start | bytes 528392 | tf_op jit(solution)/shard_map/ppermute | solution.py:507
  12.6 11.1 %all-gather.1 = f32[688,128]{1,0:T(8,128)S(1)} all-gather(f32[344,128]{1,0:T(8,128)S(1)} %get-tuple-element.50), channel_id=3, replica_groups={{0,2},{4,6},{8,10},{12,14},{1,3},{5,7},{9,11},{13,15},{16,18},{20,22},{..., dimensions={0}, use_global_device_ids=true | all-gather | bytes 528384 | tf_op jit(solution)/shard_map/all_gather | solution.py:507
  23.7 0.0 collective-permute-done.fromacross
  23.7 0.2 dom_slabs.1
  23.8 0.7 collective-permute-start.1
  24.5 0.5 ring_fields.1
  25.0 5.7 %all-gather.2 = f32[560,128]{1,0:T(8,128)S(1)} all-gather(f32[280,128]{1,0:T(8,128)S(1)} %get-tuple-element.60), channel_id=4, replica_groups={{0,16},{32,48},{64,80},{96,112},{128,144},{160,176},{192,208},{224,240}..., dimensions={0}, use_global_device_ids=true | all-gather | bytes 430080 | tf_op jit(solution)/shard_map/all_gather | solution.py:507
  30.7 0.0 collective-permute-done.1.fromacross
  30.7 0.0 copy-start
  30.7 2.5 %first_fluid.1 = (f32[32,16,128]{2,1,0:T(8,128)S(1)}, f32[8,24,128]{2,1,0:T(8,128)S(1)}, f32[8,24,128]{2,1,0:T(8,128)S(1)}, f32[48,128]{1,0:T(8,128)S(1)}, f32[64,128]{1,0:T(8,128)S(1)}) custom-call(f32[32,24,128]{2,1,0:T(8,128)S(1)} %get-tuple-element.56.esrc, f32[32,24,128]{2,1,0:T(8,128)S(1)} %get-tuple-element.54.erden, ...), custom_call_target="tpu_custom_call" | custom-call | tf_op jit(solution)/shard_map/first_fluid/pallas_call | solution.py:485
  33.2 0.0 copy-start.1
  33.2 28.9 %all_to_all.55 = f32[64,1,128]{2,1,0:T(1,128)S(1)} all-to-all(f32[64,1,128]{2,1,0:T(1,128)S(1)} %bitcast.40), channel_id=1, replica_groups=mesh['dom'=64,'sub'=8,'lane'=2] {'dom'}, dimensions={0} | all-to-all | bytes 65536 | tf_op jit(solution)/shard_map/all_to_all | solution.py:510
  62.1 0.0 copy-done
  62.1 0.0 copy-done.1
  62.1 1.7 %first_structure.1 = (f32[128,128]{1,0:T(8,128)S(1)}, f32[16,512]{1,0:T(8,128)S(1)}, bf16[512,512]{1,0:T(8,128)(2,1)S(1)}, bf16[512,512]{1,0:T(8,128)(2,1)S(1)}) custom-call(f32[64,128]{1,0:T(8,128)S(1)} %bitcast.31, f32[3,512]{1,0:T(4,128)S(1)} %copy-done.1, f32[512,512]{1,0:T(8,128)S(1)} %copy-done), custom_call_target="tpu_custom_call" | custom-call | tf_op jit(solution)/shard_map/first_structure/pallas_call | solution.py:485
  63.8 17.3 %all_to_all.56 = f32[128,1,128]{2,1,0:T(1,128)S(1)} all-to-all(f32[128,1,128]{2,1,0:T(1,128)S(1)} %bitcast.38), channel_id=1, replica_groups=mesh['dom'=64,'sub'=8,'lane'=2] {'lane','dom'}, dimensions={0} | all-to-all | bytes 131072 | tf_op jit(solution)/shard_map/all_to_all | solution.py:551
  81.1 0.4 hand_out.1.values
  81.5 7.9 %collective-permute-start.2 = (f32[16,128]{1,0:T(8,128)S(1)}, f32[16,128]{1,0:T(8,128)S(1)}, u32[]{:S(2)}, u32[]{:S(2)}) collective-permute-start(f32[16,128]{1,0:T(8,128)S(1)} %hand_out.1.values), channel_id=1, source_target_pairs={{2,4},{4,2},{6,8},{8,6},{10,12},{12,10},{3,5},{5,3},{7,9},{9,7},{1... | collective-permute-start | bytes 24584 | tf_op jit(solution)/shard_map/ppermute | solution.py:507
  89.5 0.6 own_rows.1
  90.1 1.8 %all-gather.3 = f32[32,128]{1,0:T(8,128)S(1)} all-gather(f32[16,128]{1,0:T(8,128)S(1)} %hand_out.1.values), channel_id=5, replica_groups={{0,2},{4,6},{8,10},{12,14},{1,3},{5,7},{9,11},{13,15},{16,18},{20,22},{..., dimensions={0}, use_global_device_ids=true | all-gather | bytes 24576 | tf_op jit(solution)/shard_map/all_gather | solution.py:507
  91.9 0.0 collective-permute-done.2.fromacross
  91.9 2.7 %second_fluid.1 = (f32[32,16,128]{2,1,0:T(8,128)}, f32[64,128]{1,0:T(8,128)S(1)}) custom-call(f32[32,24,128]{2,1,0:T(8,128)S(1)} %get-tuple-element.54.erden, f32[32,24,128]{2,1,0:T(8,128)S(1)} %get-tuple-element.55.xrden, f32[8,24,128]{2,1,0:T(8,128)S(1)} %get-tuple-element.66.hrden0, f32[8,24,128]{2,1,0:T(8,128)S(1)} %get-tuple-element.67.hrden1, ...), custom_call_target="tpu_custom_call" | custom-call | tf_op jit(solution)/shard_map/second_fluid/pallas_call | solution.py:485
  94.7 14.6 %all_to_all.57 = f32[64,1,128]{2,1,0:T(1,128)S(1)} all-to-all(f32[64,1,128]{2,1,0:T(1,128)S(1)} %bitcast.41), channel_id=1, replica_groups=mesh['dom'=64,'sub'=8,'lane'=2] {'dom'}, dimensions={0} | all-to-all | bytes 65536 | tf_op jit(solution)/shard_map/all_to_all | solution.py:510
  109.3 1.2 second_structure.1
  110.5 14.6 %all_to_all.58 = f32[64,1,128]{2,1,0:T(1,128)S(1)} all-to-all(f32[64,1,128]{2,1,0:T(1,128)S(1)} %bitcast.35), channel_id=1, replica_groups=mesh['dom'=64,'sub'=8,'lane'=2] {'dom'}, dimensions={0} | all-to-all | bytes 65536 | tf_op jit(solution)/shard_map/all_to_all | solution.py:510
  125.2 0.2 arrive.1
  125.4 18.0 %all_to_all.59 = f32[16,1,128]{2,1,0:T(1,128)S(1)} all-to-all(f32[16,1,128]{2,1,0:T(1,128)S(1)} %bitcast.42), channel_id=1, replica_groups=mesh['dom'=64,'sub'=8,'lane'=2] {'sub','lane'}, dimensions={0} | all-to-all | bytes 16384 | tf_op jit(solution)/shard_map/all_to_all | solution.py:573
  143.4 0.8 finish.1
Async XLA Ops:
  6.5 17.1 %collective-permute-start = (f32[344,128]{1,0:T(8,128)S(1)}, f32[344,128]{1,0:T(8,128)S(1)}, u32[]{:S(2)}, u32[]{:S(2)}) collective-permute-start(f32[344,128]{1,0:T(8,128)S(1)} %get-tuple-element.49), channel_id=1, source_target_pairs={{2,4},{4,2},{6,8},{8,6},{10,12},{12,10},{3,5},{5,3},{7,9},{9,7},{1... | collective-permute-start | bytes 528392 | tf_op jit(solution)/shard_map/ppermute | solution.py:507
  23.8 6.9 %collective-permute-start.1 = (f32[280,128]{1,0:T(8,128)S(1)}, f32[280,128]{1,0:T(8,128)S(1)}, u32[]{:S(2)}, u32[]{:S(2)}) collective-permute-start(f32[280,128]{1,0:T(8,128)S(1)} %get-tuple-element.61), channel_id=1, source_target_pairs={{16,32},{32,16},{48,64},{64,48},{80,96},{96,80},{112,128},{128,112... | collective-permute-start | bytes 430088 | tf_op jit(solution)/shard_map/ppermute | solution.py:507
  30.7 31.4 %copy-start = (f32[512,512]{1,0:T(8,128)S(1)}, f32[512,512]{1,0:T(8,128)}, u32[]{:S(2)}) copy-start(f32[512,512]{1,0:T(8,128)} %shell.3) | copy-start | bytes 3145732
  33.2 28.9 %copy-start.1 = (f32[3,512]{1,0:T(4,128)S(1)}, f32[3,512]{1,0:T(4,128)}, u32[]{:S(2)}) copy-start(f32[3,512]{1,0:T(4,128)} %nodes.1) | copy-start | bytes 18436
  81.5 10.4 %collective-permute-start.2 = (f32[16,128]{1,0:T(8,128)S(1)}, f32[16,128]{1,0:T(8,128)S(1)}, u32[]{:S(2)}, u32[]{:S(2)}) collective-permute-start(f32[16,128]{1,0:T(8,128)S(1)} %hand_out.1.values), channel_id=1, source_target_pairs={{2,4},{4,2},{6,8},{8,6},{10,12},{12,10},{3,5},{5,3},{7,9},{9,7},{1... | collective-permute-start | bytes 24584 | tf_op jit(solution)/shard_map/ppermute | solution.py:507

commit v5 on v4

--- a/solution.py
+++ b/solution.py
@@ -83,7 +83,7 @@
 ):
     pairs = (
         (cell_far, cell), (part_far, part), (nrm_far, nrm), (disp_far, disp),
-        (rhs_far, rhs), (pold_far, pold), (coef_far, coef), (coords_far, coords),
+        (rhs_far, rhs), (coef_far, coef), (pold_far, pold), (coords_far, coords),
     )
     copies = [pltpu.make_async_copy(a, b, sems.at[k]) for k, (a, b) in enumerate(pairs)]
     for copy in copies:
@@ -100,10 +100,10 @@
     slot[...] = part[...].astype(f32) * CAP + rank
     copies[4].wait()
     src[...] = rhs[...] + added.reshape(CX, CY, CZ)
-    copies[6].wait()
+    copies[5].wait()
     rden[...] = 1.0 / (6.0 + coef[...])
-    copies[5].wait()
-    copies[7].wait()
+    for copy in copies[6:]:
+        copy.wait()
     shift = jnp.where(lax.axis_index("lane") == 0, 4, 0)
     at = lax.broadcasted_iota(i32, (CY, CZ), 1)
     for x4 in range(4):
@@ -180,7 +180,51 @@
     beside[...], across[...] = up_down(lax.rem(lax.axis_index("dom"), 2), high[...], low[...])
 
 
-def ring_kernel(src, rden, pold, subhigh, sublow, beyond, esrc, erden, epold, xsrc, xrden, xpold):
+def near(width):
+    return [*range(CX + width), *range(RX - width, RX)]
+
+
+def ring(own, other, own_halo=None, other_halo=None):
+    def layer(x):
+        if x < CX or own_halo is None:
+            return jnp.concatenate([own[x], other[x]], axis=1)
+        return jnp.concatenate([own_halo(x - CX), other_halo[x - CX]], axis=1)
+
+    return layer
+
+
+def sweep(now, out, source, scale, layers):
+    for x in layers:
+        here = now(x)
+        total = now((x + 1) % RX) + now((x - 1) % RX)
+        total = total + (pltpu.roll(here, RY - 1, 0) + pltpu.roll(here, 1, 0))
+        total = total + (pltpu.roll(here, 2 * CZ - 1, 1) + pltpu.roll(here, 1, 1))
+        total = (source(x) + total) * scale(x)
+        out[0][x], out[1][x] = total[:, 0:CZ], total[:, CZ : 2 * CZ]
+
+
+def last_sweep(now, source, scale, write, layers=range(CX)):
+    for x in layers:
+        here = now[0][x]
+        total = now[0][(x + 1) % RX, 0:CY] + now[0][(x - 1) % RX, 0:CY]
+        total = total + (pltpu.roll(here, RY - 1, 0) + pltpu.roll(here, 1, 0))[0:CY]
+        wide = jnp.concatenate([here[0:CY], now[1][x, 0:CY]], axis=1)
+        beside = pltpu.roll(wide, 2 * CZ - 1, 1) + pltpu.roll(wide, 1, 1)
+        write(x, (source[x, 0:CY] + (total + beside[:, 0:CZ])) * scale[x, 0:CY])
+
+
+def inner(number):
+    return range(number, CX - number)
+
+
+def passed(number):
+    return number, number + 1, CX - number - 2, CX - number - 1
+
+
+def ring_kernel(
+    src, rden, pold, subhigh, sublow, beyond,
+    esrc, erden, epold, xsrc, xrden, xpold, pressure, kept, even0, even1, odd0, odd1,
+):
     for field, own, width, ext in ((0, src, 3, esrc), (3, rden, 3, erden), (6, pold, 4, epold)):
         ext[:, 0:CY, :] = own[...]
         if width == 3:
@@ -196,39 +240,20 @@
         for field, beside in enumerate((xsrc, xrden, xpold)):
             for k in range(8):
                 beside[4 * k + x4] = unpacked(rows, 16 * k + 4 * field, lane, keep)
-
-
-def near(width):
-    return [*range(CX + width), *range(RX - width, RX)]
-
-
-def ring(own, other, own_halo=None, other_halo=None):
-    def layer(x):
-        if x < CX or own_halo is None:
-            return jnp.concatenate([own[x], other[x]], axis=1)
-        return jnp.concatenate([own_halo(x - CX), other_halo[x - CX]], axis=1)
-
-    return layer
-
-
-def sweep(now, out, source, scale, width):
-    for x in near(width):
-        here = now(x)
-        total = now((x + 1) % RX) + now((x - 1) % RX)
-        total = total + (pltpu.roll(here, RY - 1, 0) + pltpu.roll(here, 1, 0))
-        total = total + (pltpu.roll(here, 2 * CZ - 1, 1) + pltpu.roll(here, 1, 1))
-        total = (source(x) + total) * scale(x)
-        out[0][x], out[1][x] = total[:, 0:CZ], total[:, CZ : 2 * CZ]
-
-
-def last_sweep(now, source, scale, write):
-    for x in range(CX):
-        here = now[0][x]
-        total = now[0][(x + 1) % RX, 0:CY] + now[0][(x - 1) % RX, 0:CY]
-        total = total + (pltpu.roll(here, RY - 1, 0) + pltpu.roll(here, 1, 0))[0:CY]
-        wide = jnp.concatenate([here[0:CY], now[1][x, 0:CY]], axis=1)
-        beside = pltpu.roll(wide, 2 * CZ - 1, 1) + pltpu.roll(wide, 1, 1)
-        write(x, (source[x, 0:CY] + (total + beside[:, 0:CZ])) * scale[x, 0:CY])
+    source, scale = ring(esrc, xsrc), ring(erden, xrden)
+    now, spare = (epold, xpold), ((even0, even1), (odd0, odd1))
+    for number in (1, 2, 3):
+        out = spare[(number - 1) % 2]
+        sweep(ring(*now), out, source, scale, inner(number))
+        for k, x in enumerate(passed(number)):
+            for tile in range(2):
+                kept[number - 1, tile, k] = out[tile][x]
+        now = out
+
+    def write(x, value):
+        pressure[x] = value
+
+    last_sweep(now, esrc, erden, write, inner(4))
 
 
 def forces_at(pressure, points, nrm):
@@ -242,7 +267,7 @@
 
 
 def first_fluid_kernel(
-    esrc, erden, epold, xsrc, xrden, xpold, doms, fromacross, tails, cell, nrm, coords, disp, slot,
+    esrc, erden, epold, xsrc, xrden, xpold, partly, kept, doms, fromacross, tails, cell, nrm, coords, disp, slot,
     pressure, hrden0, hrden1, meta, sending, hsrc1, hpold1, domhigh, domlow, even0, even1, odd0, odd1,
 ):
     lane, pair = lax.axis_index("lane"), lax.rem(lax.axis_index("dom"), 2)
@@ -266,14 +291,19 @@
     source = ring(esrc, xsrc, halo(0, 3), hsrc1)
     scale = ring(erden, xrden, halo(3, 3), hrden1)
     even, odd = (even0, even1), (odd0, odd1)
-    sweep(ring(epold, xpold, halo(6, 4), hpold1), even, source, scale, 3)
-    sweep(ring(*even), odd, source, scale, 2)
-    sweep(ring(*odd), even, source, scale, 1)
+    now = ring(epold, xpold, halo(6, 4), hpold1)
+    for number, out in ((1, even), (2, odd), (3, even)):
+        sweep(now, out, source, scale, [x for x in near(4 - number) if x not in inner(number)])
+        for k, x in enumerate(passed(number)):
+            for tile in range(2):
+                out[tile][x] = kept[number - 1, tile, k]
+        now = ring(*out)
 
     def write(x, value):
         pressure[x] = value
 
-    last_sweep(even, esrc, erden, write)
+    last_sweep(even, esrc, erden, write, [x for x in range(CX) if x not in inner(4)])
+    pressure[4 : CX - 4] = partly[4 : CX - 4]
     slots = slot[...].astype(i32)
     values = forces_at(pressure[...].reshape(CX * CY, CZ), cell[...], nrm)
     values += [coords[c : c + 1, :] for c in range(3)]
@@ -316,7 +346,7 @@
 
 def second_fluid_kernel(
     erden, xrden, hrden0, hrden1, before, own0, own1, fromacross, cores, meta, cell, nrm, slot,
-    pressure_far, sending, src0, src1, even0, even1, odd0, odd1, pressure, fromhigh, fromlow, sem,
+    pressure_far, sending, src0, src1, even0, even1, odd0, odd1, pressure, fromhigh, fromlow, sems,
 ):
     lane, core = lax.axis_index("lane"), lax.rem(lax.axis_index("sub"), 2)
     fromhigh[...], fromlow[...] = up_down(core, cores[1 - core], fromacross[...])
@@ -339,17 +369,21 @@
     even, odd = (even0, even1), (odd0, odd1)
     source = ring(src0, src1)
     scale = ring(erden, xrden, lambda x: hrden0[x], hrden1)
-    sweep(ring(*even), odd, source, scale, 2)
-    sweep(ring(*odd), even, source, scale, 1)
+    sweep(ring(*even), odd, source, scale, near(2))
+    sweep(ring(*odd), even, source, scale, near(1))
 
     def write(x, value):
         pressure[x] = before[x] + value
 
-    last_sweep(even, src0, erden, write)
-    copy = pltpu.make_async_copy(pressure, pressure_far, sem)
-    copy.start()
+    copies = []
+    for k, x in enumerate(range(0, CX, 8)):
+        last_sweep(even, src0, erden, write, range(x, x + 8))
+        part = pl.ds(x, 8)
+        copies.append(pltpu.make_async_copy(pressure.at[part], pressure_far.at[part], sems.at[k]))
+        copies[-1].start()
     sending[...] = to_slots(forces_at(pressure[...].reshape(CX * CY, CZ), cell[...], nrm), slot[...].astype(i32), 2)
-    copy.wait()
+    for copy in copies:
+        copy.wait()
 
 
 def to_slots(values, slots, count):
@@ -521,6 +555,7 @@
     lanes = lax.all_gather(strips, "lane")
     further, beside = call(faces_kernel, (face, face), (src, rden, pold, cell, lanes), name="sub_faces")
     fromacross, cores = swap(further, beside, "sub")
+    square = shape(NS, NS, dtype=bf16)
     beside, further, subhigh, sublow, beyond, tails = call(
         dom_kernel,
         (slab, slab, face, face, shape(4, RY, CZ), shape(16, CZ)),
@@ -529,19 +564,22 @@
         name="dom_slabs",
     )
     fromacross, doms = swap(further, beside, "dom")
-    esrc, erden, epold, xsrc, xrden, xpold = call(
-        ring_kernel, (main,) * 6, (src, rden, pold, subhigh, sublow, beyond), name="ring_fields"
-    )
     grid = pltpu.VMEM((RX, RY, CZ), f32)
+    esrc, erden, epold, xsrc, xrden, xpold, partly, kept = call(
+        ring_kernel,
+        (*[main] * 6, block, shape(3, 2, 4, RY, CZ)),
+        (src, rden, pold, subhigh, sublow, beyond),
+        [pltpu.VMEM((CX, RY, CZ), f32)] * 4,
+        name="ring_fields",
+    )
     pressure, hrden0, hrden1, meta, sending = call(
         first_fluid_kernel,
         (block, halo, halo, shape(48, CZ), row),
-        (esrc, erden, epold, xsrc, xrden, xpold, doms, fromacross, tails, cell, nrm, coords, disp, slot),
+        (esrc, erden, epold, xsrc, xrden, xpold, partly, kept, doms, fromacross, tails, cell, nrm, coords, disp, slot),
         [pltpu.VMEM((8, RY, CZ), f32)] * 2 + [pltpu.VMEM((SLAB + RY + 16, CZ), f32)] * 2 + [grid] * 4,
         name="first_fluid",
     )
     received = across(sending)
-    square = shape(NS, NS, dtype=bf16)
     returned, mapped, khead, ktail = call(
         first_structure_kernel,
         (shape(2 * DOM, CAP * WIDE), shape(WIDE, NS), square, square),
@@ -558,7 +596,7 @@
         (block, row),
         (erden, xrden, hrden0, hrden1, pressure, own0, own1, fromacross, cores, meta, cell, nrm, slot),
         [grid] * 6
-        + [pltpu.VMEM((CX, CY, CZ), f32), *[pltpu.VMEM((16, 128), f32)] * 2, pltpu.SemaphoreType.DMA],
+        + [pltpu.VMEM((CX, CY, CZ), f32), *[pltpu.VMEM((16, 128), f32)] * 2, pltpu.SemaphoreType.DMA((4,))],
         name="second_fluid",
         far_out=(0,),
     )

time: 145 us -> 144 us (level)
  transfers between devices with their start and end apart: 3 -> 3, of which waited for: 0 -> 0; matrix products, arithmetic and copies ran while one was open for 0% -> 0% of each run, Pallas kernels for 1% -> 2%
where the time goes in v5:
time: 144 us
  blocking collectives  115 us (80%)
  starting transfers between devices  14.9 us (10%)
  Pallas kernels  12.4 us (9%)
    all_to_all x3, blocking collectives, across(): return lax.all_to_all(rows, 'dom', 0, 0, tiled=True)  57.6 us
    all_gather x3, blocking collectives, swap(): lax.all_gather(beside, axis, axis_index_groups=pairs)  18.5 us
    all_to_all x1, blocking collectives, body(): sums = lax.all_to_all(sums, ('sub', 'lane'), 0, 0, tiled=True)  18 us
    all_to_all x1, blocking collectives, body(): arrived = lax.all_to_all(returned, ('lane', 'dom'), 0, 0, tiled=True)  17.3 us
    ppermute x3, starting transfers between devices, swap(): lax.ppermute(across, axis, swaps)  14.9 us
    pallas_call x12, Pallas kernels, call(): pl.pallas_call(kernel, out_shape=outs, in_specs=[spec(k) for k in range(l...  12.4 us
    all_gather x1, blocking collectives, body(): lanes = lax.all_gather(strips, 'lane')  4.04 us
  transfers between devices with their start and end apart: 3, of which 0 were waited for; matrix products, arithmetic and copies ran while one was open for 0% of the time, Pallas kernels for 2%

profile of v5, /device:TPU:1, one launch (start us, length us, event | category | flops | bytes accessed | tf_op | source)
XLA Modules:
  0.0 143.5 jit_solution(12798826922953421249)
XLA Ops:
  0.6 1.5 %start.1 = (f32[32,16,128]{2,1,0:T(8,128)S(1)}, f32[32,16,128]{2,1,0:T(8,128)S(1)}, f32[32,16,128]{2,1,0:T(8,128)S(1)}, f32[72,128]{1,0:T(8,128)S(1)}, f32[1,256...) custom-call(f32[32,16,128]{2,1,0:T(8,128)} %rhs_far.1, ...), custom_call_target="tpu_custom_call" | custom-call | tf_op jit(solution)/shard_map/start/pallas_call | solution.py:519
  2.2 4.0 %all-gather = f32[144,128]{1,0:T(8,128)S(1)} all-gather(f32[72,128]{1,0:T(8,128)S(1)} %get-tuple-element.50), channel_id=2, replica_groups=mesh['dom'=64,'sub'=8,'lane'=2] {'lane'}, dimensions={0}, use_global_device_ids=true | all-gather | bytes 110592 | tf_op jit(solution)/shard_map/all_gather | solution.py:555
  6.2 0.3 sub_faces.1
  6.5 6.0 %collective-permute-start = (f32[344,128]{1,0:T(8,128)S(1)}, f32[344,128]{1,0:T(8,128)S(1)}, u32[]{:S(2)}, u32[]{:S(2)}) collective-permute-start(f32[344,128]{1,0:T(8,128)S(1)} %get-tuple-element.51), channel_id=1, source_target_pairs={{2,4},{4,2},{6,8},{8,6},{10,12},{12,10},{3,5},{5,3},{7,9},{9,7},{1... | collective-permute-start | bytes 528392 | tf_op jit(solution)/shard_map/ppermute | solution.py:541
  12.5 11.1 %all-gather.1 = f32[688,128]{1,0:T(8,128)S(1)} all-gather(f32[344,128]{1,0:T(8,128)S(1)} %get-tuple-element.52), channel_id=3, replica_groups={{0,2},{4,6},{8,10},{12,14},{1,3},{5,7},{9,11},{13,15},{16,18},{20,22},{..., dimensions={0}, use_global_device_ids=true | all-gather | bytes 528384 | tf_op jit(solution)/shard_map/all_gather | solution.py:541
  23.6 0.0 collective-permute-done.fromacross
  23.6 0.2 dom_slabs.1
  23.8 0.7 collective-permute-start.1
  24.5 1.9 %ring_fields.1 = (f32[32,24,128]{2,1,0:T(8,128)S(1)}, f32[32,24,128]{2,1,0:T(8,128)S(1)}, f32[32,24,128]{2,1,0:T(8,128)S(1)}, f32[32,24,128]{2,1,0:T(8,128)S(1)}...) custom-call(f32[32,16,128]{2,1,0:T(8,128)S(1)} %get-tuple-element.45, ...), custom_call_target="tpu_custom_call" | custom-call | tf_op jit(solution)/shard_map/ring_fields/pallas_call | solution.py:519
  26.4 5.7 %all-gather.2 = f32[560,128]{1,0:T(8,128)S(1)} all-gather(f32[280,128]{1,0:T(8,128)S(1)} %get-tuple-element.64), channel_id=4, replica_groups={{0,16},{32,48},{64,80},{96,112},{128,144},{160,176},{192,208},{224,240}..., dimensions={0}, use_global_device_ids=true | all-gather | bytes 430080 | tf_op jit(solution)/shard_map/all_gather | solution.py:541
  32.0 0.0 collective-permute-done.1.fromacross
  32.0 0.0 copy-start
  32.0 1.0 first_fluid.1
  33.0 0.0 copy-start.1
  33.0 28.3 %all_to_all.55 = f32[64,1,128]{2,1,0:T(1,128)S(1)} all-to-all(f32[64,1,128]{2,1,0:T(1,128)S(1)} %bitcast.40), channel_id=1, replica_groups=mesh['dom'=64,'sub'=8,'lane'=2] {'dom'}, dimensions={0} | all-to-all | bytes 65536 | tf_op jit(solution)/shard_map/all_to_all | solution.py:544
  61.4 0.0 copy-done
  61.4 0.0 copy-done.1
  61.4 1.7 %first_structure.1 = (f32[128,128]{1,0:T(8,128)S(1)}, f32[16,512]{1,0:T(8,128)S(1)}, bf16[512,512]{1,0:T(8,128)(2,1)S(1)}, bf16[512,512]{1,0:T(8,128)(2,1)S(1)}) custom-call(f32[64,128]{1,0:T(8,128)S(1)} %bitcast.31, f32[3,512]{1,0:T(4,128)S(1)} %copy-done.1, f32[512,512]{1,0:T(8,128)S(1)} %copy-done), custom_call_target="tpu_custom_call" | custom-call | tf_op jit(solution)/shard_map/first_structure/pallas_call | solution.py:519
  63.1 17.3 %all_to_all.56 = f32[128,1,128]{2,1,0:T(1,128)S(1)} all-to-all(f32[128,1,128]{2,1,0:T(1,128)S(1)} %bitcast.38), channel_id=1, replica_groups=mesh['dom'=64,'sub'=8,'lane'=2] {'lane','dom'}, dimensions={0} | all-to-all | bytes 131072 | tf_op jit(solution)/shard_map/all_to_all | solution.py:589
  80.4 0.4 hand_out.1.values
  80.8 8.2 %collective-permute-start.2 = (f32[16,128]{1,0:T(8,128)S(1)}, f32[16,128]{1,0:T(8,128)S(1)}, u32[]{:S(2)}, u32[]{:S(2)}) collective-permute-start(f32[16,128]{1,0:T(8,128)S(1)} %hand_out.1.values), channel_id=1, source_target_pairs={{2,4},{4,2},{6,8},{8,6},{10,12},{12,10},{3,5},{5,3},{7,9},{9,7},{1... | collective-permute-start | bytes 24584 | tf_op jit(solution)/shard_map/ppermute | solution.py:541
  89.0 0.6 own_rows.1
  89.6 1.8 %all-gather.3 = f32[32,128]{1,0:T(8,128)S(1)} all-gather(f32[16,128]{1,0:T(8,128)S(1)} %hand_out.1.values), channel_id=5, replica_groups={{0,2},{4,6},{8,10},{12,14},{1,3},{5,7},{9,11},{13,15},{16,18},{20,22},{..., dimensions={0}, use_global_device_ids=true | all-gather | bytes 24576 | tf_op jit(solution)/shard_map/all_gather | solution.py:541
  91.5 0.0 collective-permute-done.2.fromacross
  91.5 2.6 %second_fluid.1 = (f32[32,16,128]{2,1,0:T(8,128)}, f32[64,128]{1,0:T(8,128)S(1)}) custom-call(f32[32,24,128]{2,1,0:T(8,128)S(1)} %get-tuple-element.56.erden, f32[32,24,128]{2,1,0:T(8,128)S(1)} %get-tuple-element.57.xrden, f32[8,24,128]{2,1,0:T(8,128)S(1)} %get-tuple-element.70.hrden0, f32[8,24,128]{2,1,0:T(8,128)S(1)} %get-tuple-element.71.hrden1, ...), custom_call_target="tpu_custom_call" | custom-call | tf_op jit(solution)/shard_map/second_fluid/pallas_call | solution.py:519
  94.0 14.6 %all_to_all.57 = f32[64,1,128]{2,1,0:T(1,128)S(1)} all-to-all(f32[64,1,128]{2,1,0:T(1,128)S(1)} %bitcast.41), channel_id=1, replica_groups=mesh['dom'=64,'sub'=8,'lane'=2] {'dom'}, dimensions={0} | all-to-all | bytes 65536 | tf_op jit(solution)/shard_map/all_to_all | solution.py:544
  108.6 1.2 second_structure.1
  109.9 14.6 %all_to_all.58 = f32[64,1,128]{2,1,0:T(1,128)S(1)} all-to-all(f32[64,1,128]{2,1,0:T(1,128)S(1)} %bitcast.35), channel_id=1, replica_groups=mesh['dom'=64,'sub'=8,'lane'=2] {'dom'}, dimensions={0} | all-to-all | bytes 65536 | tf_op jit(solution)/shard_map/all_to_all | solution.py:544
  124.5 0.2 arrive.1
  124.7 18.0 %all_to_all.59 = f32[16,1,128]{2,1,0:T(1,128)S(1)} all-to-all(f32[16,1,128]{2,1,0:T(1,128)S(1)} %bitcast.42), channel_id=1, replica_groups=mesh['dom'=64,'sub'=8,'lane'=2] {'sub','lane'}, dimensions={0} | all-to-all | bytes 16384 | tf_op jit(solution)/shard_map/all_to_all | solution.py:611
  142.7 0.8 finish.1
Async XLA Ops:
  6.5 17.1 %collective-permute-start = (f32[344,128]{1,0:T(8,128)S(1)}, f32[344,128]{1,0:T(8,128)S(1)}, u32[]{:S(2)}, u32[]{:S(2)}) collective-permute-start(f32[344,128]{1,0:T(8,128)S(1)} %get-tuple-element.51), channel_id=1, source_target_pairs={{2,4},{4,2},{6,8},{8,6},{10,12},{12,10},{3,5},{5,3},{7,9},{9,7},{1... | collective-permute-start | bytes 528392 | tf_op jit(solution)/shard_map/ppermute | solution.py:541
  23.8 8.3 %collective-permute-start.1 = (f32[280,128]{1,0:T(8,128)S(1)}, f32[280,128]{1,0:T(8,128)S(1)}, u32[]{:S(2)}, u32[]{:S(2)}) collective-permute-start(f32[280,128]{1,0:T(8,128)S(1)} %get-tuple-element.65), channel_id=1, source_target_pairs={{16,32},{32,16},{48,64},{64,48},{80,96},{96,80},{112,128},{128,112... | collective-permute-start | bytes 430088 | tf_op jit(solution)/shard_map/ppermute | solution.py:541
  32.0 29.3 %copy-start = (f32[512,512]{1,0:T(8,128)S(1)}, f32[512,512]{1,0:T(8,128)}, u32[]{:S(2)}) copy-start(f32[512,512]{1,0:T(8,128)} %shell.3) | copy-start | bytes 3145732
  33.0 28.3 %copy-start.1 = (f32[3,512]{1,0:T(4,128)S(1)}, f32[3,512]{1,0:T(4,128)}, u32[]{:S(2)}) copy-start(f32[3,512]{1,0:T(4,128)} %nodes.1) | copy-start | bytes 18436
  80.8 10.7 %collective-permute-start.2 = (f32[16,128]{1,0:T(8,128)S(1)}, f32[16,128]{1,0:T(8,128)S(1)}, u32[]{:S(2)}, u32[]{:S(2)}) collective-permute-start(f32[16,128]{1,0:T(8,128)S(1)} %hand_out.1.values), channel_id=1, source_target_pairs={{2,4},{4,2},{6,8},{8,6},{10,12},{12,10},{3,5},{5,3},{7,9},{9,7},{1... | collective-permute-start | bytes 24584 | tf_op jit(solution)/shard_map/ppermute | solution.py:541

commit v6 on v5

--- a/solution.py
+++ b/solution.py
@@ -79,7 +79,7 @@
 
 def start_kernel(
     rhs_far, coef_far, pold_far, cell_far, part_far, nrm_far, disp_far, coords_far,
-    src, rden, pold, strips, slot, cell, nrm, disp, coords, rhs, coef, part, sems,
+    src, rden, pold, across, strips, slot, cell, nrm, disp, coords, rhs, coef, part, sems,
 ):
     pairs = (
         (cell_far, cell), (part_far, part), (nrm_far, nrm), (disp_far, disp),
@@ -104,6 +104,11 @@
     rden[...] = 1.0 / (6.0 + coef[...])
     for copy in copies[6:]:
         copy.wait()
+    core = lax.rem(lax.axis_index("sub"), 2)
+    for field, own, width in ((0, src, 3), (3, rden, 3), (6, pold, 4)):
+        for k in range(width):
+            at = (field + k) * CX
+            across[at : at + CX, :] = jnp.where(core == 0, own[:, k, :], own[:, CY - width + k, :])
     shift = jnp.where(lax.axis_index("lane") == 0, 4, 0)
     at = lax.broadcasted_iota(i32, (CY, CZ), 1)
     for x4 in range(4):
@@ -130,27 +135,27 @@
     return jnp.where(lane == 0, at, CZ - 1 - at) < 4
 
 
-def faces_kernel(src, rden, pold, cell, lanes, across, beside):
+def faces_kernel(src, rden, pold, cell, lanes, extra, beside):
     core, lane = lax.rem(lax.axis_index("sub"), 2), lax.axis_index("lane")
     for field, own, width in ((0, src, 3), (3, rden, 3), (6, pold, 4)):
         for k in range(width):
             at = (field + k) * CX
-            low, high = own[:, k, :], own[:, CY - width + k, :]
-            beside[at : at + CX, :], across[at : at + CX, :] = up_down(core, high, low)
+            beside[at : at + CX, :] = jnp.where(core == 0, own[:, CY - width + k, :], own[:, k, :])
     other = lanes[1 - lane]
     for x4 in range(4):
-        at, low, high = FACE + 4 * x4, other[x4 * CY : x4 * CY + 4], other[(x4 + 1) * CY - 4 : (x4 + 1) * CY]
-        beside[at : at + 4, :], across[at : at + 4, :] = up_down(core, high, low)
+        at, low, high = 4 * x4, other[x4 * CY : x4 * CY + 4], other[(x4 + 1) * CY - 4 : (x4 + 1) * CY]
+        beside[FACE + at : FACE + at + 4, :], extra[at : at + 4, :] = up_down(core, high, low)
     tail = jnp.concatenate([*halves(cell[...].astype(f32)), other[64:66], jnp.zeros((4, CZ), f32)], axis=0)
     beside[FACE + 16 : FACE + 24, :] = tail
-    across[FACE + 16 : FACE + 24, :] = tail
+    extra[16:24, :] = tail
 
 
 def dom_kernel(
-    src, rden, pold, cell, slot, fromacross, cores, lanes, beside, across, subhigh, sublow, beyond, tails, slabs
+    src, rden, pold, cell, slot, fromacross, extra, cores, lanes, beside, across, subhigh, sublow, beyond, tails, slabs
 ):
     core, lane = lax.rem(lax.axis_index("sub"), 2), lax.axis_index("lane")
-    subhigh[...], sublow[...] = up_down(core, cores[1 - core], fromacross[...])
+    for rows, far in ((slice(0, FACE), fromacross), (slice(FACE, FACE + 24), extra)):
+        subhigh[rows], sublow[rows] = up_down(core, cores[1 - core, rows], far[...])
     other = lanes[1 - lane]
     cellhigh, celllow = subhigh[FACE + 16 : FACE + 24], sublow[FACE + 16 : FACE + 24]
     tail = [*halves(cell[...].astype(f32)), cellhigh[0:2], celllow[0:2], *halves(slot[...])]
@@ -544,22 +549,24 @@
         return lax.all_to_all(rows, "dom", 0, 0, tiled=True)
 
     face, slab = shape(FACE + 24, CZ), shape(SLAB + RY + 16, CZ)
-    src, rden, pold, strips, slot, cell, nrm, disp, coords = call(
+    src, rden, pold, further, strips, slot, cell, nrm, disp, coords = call(
         start_kernel,
-        (block, block, block, shape(72, CZ), shape(1, PTS), shape(1, PTS, dtype=i32), *[shape(3, PTS)] * 3),
+        (block, block, block, shape(FACE, CZ), shape(72, CZ), shape(1, PTS), shape(1, PTS, dtype=i32), *[shape(3, PTS)] * 3),
         [pltpu.with_memory_space_constraint(x, pltpu.HBM) for x in (rhs, coef, pold, cell, part, nrm, disp, coords)],
         [pltpu.VMEM((CX, CY, CZ), f32)] * 2 + [pltpu.VMEM((1, PTS), i32), pltpu.SemaphoreType.DMA((8,))],
         name="start",
         far=range(8),
     )
+    swaps = [(i + k, i + 1 - k) for i in (1, 3, 5) for k in (0, 1)]
+    fromacross = lax.ppermute(further, "sub", swaps)
     lanes = lax.all_gather(strips, "lane")
-    further, beside = call(faces_kernel, (face, face), (src, rden, pold, cell, lanes), name="sub_faces")
-    fromacross, cores = swap(further, beside, "sub")
+    extra, beside = call(faces_kernel, (shape(24, CZ), face), (src, rden, pold, cell, lanes), name="sub_faces")
+    extra, cores = swap(extra, beside, "sub")
     square = shape(NS, NS, dtype=bf16)
     beside, further, subhigh, sublow, beyond, tails = call(
         dom_kernel,
         (slab, slab, face, face, shape(4, RY, CZ), shape(16, CZ)),
-        (src, rden, pold, cell, slot, fromacross, cores, lanes),
+        (src, rden, pold, cell, slot, fromacross, extra, cores, lanes),
         [pltpu.VMEM((2, SLAB + RY + 16, CZ), f32)],
         name="dom_slabs",
     )

time: 144 us -> 143 us (level)
  blocking collectives: 115 us -> 111 us
  starting transfers between devices: 14.9 us -> 18.6 us
    ppermute x0 -> x1, starting transfers between devices: none -> 5.44 us  [body(): fromacross = lax.ppermute(further, 'sub', swaps)]
    all_to_all x1, blocking collectives: 18 us -> 15.7 us  [body(): sums = lax.all_to_all(sums, ('sub', 'lane'), 0, 0, tiled=True)]
    all_gather x3, blocking collectives: 18.5 us -> 16.7 us  [swap(): lax.all_gather(beside, axis, axis_index_groups=pairs)]
    ppermute x3, starting transfers between devices: 14.9 us -> 13.2 us  [swap(): lax.ppermute(across, axis, swaps)]
  transfers between devices with their start and end apart: 3 -> 4, of which waited for: 0 -> 0; matrix products, arithmetic and copies ran while one was open for 0% -> 0% of each run, Pallas kernels for 2% -> 2%
where the time goes in v6:
time: 143 us
  blocking collectives  111 us (78%)
  starting transfers between devices  18.6 us (13%)
  Pallas kernels  12.4 us (9%)
    all_to_all x3, blocking collectives, across(): return lax.all_to_all(rows, 'dom', 0, 0, tiled=True)  57.9 us
    all_to_all x1, blocking collectives, body(): arrived = lax.all_to_all(returned, ('lane', 'dom'), 0, 0, tiled=True)  17.3 us
    all_gather x3, blocking collectives, swap(): lax.all_gather(beside, axis, axis_index_groups=pairs)  16.7 us
    all_to_all x1, blocking collectives, body(): sums = lax.all_to_all(sums, ('sub', 'lane'), 0, 0, tiled=True)  15.7 us
    ppermute x3, starting transfers between devices, swap(): lax.ppermute(across, axis, swaps)  13.2 us
    pallas_call x12, Pallas kernels, call(): pl.pallas_call(kernel, out_shape=outs, in_specs=[spec(k) for k in range(l...  12.4 us
    ppermute x1, starting transfers between devices, body(): fromacross = lax.ppermute(further, 'sub', swaps)  5.44 us
    all_gather x1, blocking collectives, body(): lanes = lax.all_gather(strips, 'lane')  3.49 us
  transfers between devices with their start and end apart: 4, of which 0 were waited for; matrix products, arithmetic and copies ran while one was open for 0% of the time, Pallas kernels for 2%

profile of v6, /device:TPU:1, one launch (start us, length us, event | category | flops | bytes accessed | tf_op | source)
XLA Modules:
  0.0 142.9 jit_solution(816223378876132548)
XLA Ops:
  0.6 1.6 %start.1 = (f32[32,16,128]{2,1,0:T(8,128)S(1)}, f32[32,16,128]{2,1,0:T(8,128)S(1)}, f32[32,16,128]{2,1,0:T(8,128)S(1)}, f32[320,128]{1,0:T(8,128)S(1)}, f32[72,1...) custom-call(f32[32,16,128]{2,1,0:T(8,128)} %rhs_far.1, ...), custom_call_target="tpu_custom_call" | custom-call | tf_op jit(solution)/shard_map/start/pallas_call | solution.py:524
  2.2 5.4 %collective-permute-start = (f32[320,128]{1,0:T(8,128)S(1)}, f32[320,128]{1,0:T(8,128)S(1)}, u32[]{:S(2)}, u32[]{:S(2)}) collective-permute-start(f32[320,128]{1,0:T(8,128)S(1)} %get-tuple-element.51), channel_id=1, source_target_pairs={{2,4},{4,2},{6,8},{8,6},{10,12},{12,10},{3,5},{5,3},{7,9},{9,7},{1... | collective-permute-start | bytes 491528 | tf_op jit(solution)/shard_map/ppermute | solution.py:561
  7.7 3.5 %all-gather = f32[144,128]{1,0:T(8,128)S(1)} all-gather(f32[72,128]{1,0:T(8,128)S(1)} %get-tuple-element.52), channel_id=2, replica_groups=mesh['dom'=64,'sub'=8,'lane'=2] {'lane'}, dimensions={0}, use_global_device_ids=true | all-gather | bytes 110592 | tf_op jit(solution)/shard_map/all_gather | solution.py:562
  11.2 0.2 sub_faces.1
  11.3 3.7 %collective-permute-start.1 = (f32[24,128]{1,0:T(8,128)S(1)}, f32[24,128]{1,0:T(8,128)S(1)}, u32[]{:S(2)}, u32[]{:S(2)}) collective-permute-start(f32[24,128]{1,0:T(8,128)S(1)} %get-tuple-element.53), channel_id=1, source_target_pairs={{2,4},{4,2},{6,8},{8,6},{10,12},{12,10},{3,5},{5,3},{7,9},{9,7},{1... | collective-permute-start | bytes 36872 | tf_op jit(solution)/shard_map/ppermute | solution.py:546
  15.0 9.2 %all-gather.1 = f32[688,128]{1,0:T(8,128)S(1)} all-gather(f32[344,128]{1,0:T(8,128)S(1)} %get-tuple-element.54), channel_id=3, replica_groups={{0,2},{4,6},{8,10},{12,14},{1,3},{5,7},{9,11},{13,15},{16,18},{20,22},{..., dimensions={0}, use_global_device_ids=true | all-gather | bytes 528384 | tf_op jit(solution)/shard_map/all_gather | solution.py:546
  24.2 0.0 collective-permute-done.1.extra
  24.2 0.0 collective-permute-done.fromacross
  24.2 0.2 dom_slabs.1
  24.4 0.7 collective-permute-start.2
  25.1 1.9 %ring_fields.1 = (f32[32,24,128]{2,1,0:T(8,128)S(1)}, f32[32,24,128]{2,1,0:T(8,128)S(1)}, f32[32,24,128]{2,1,0:T(8,128)S(1)}, f32[32,24,128]{2,1,0:T(8,128)S(1)}...) custom-call(f32[32,16,128]{2,1,0:T(8,128)S(1)} %get-tuple-element.46, ...), custom_call_target="tpu_custom_call" | custom-call | tf_op jit(solution)/shard_map/ring_fields/pallas_call | solution.py:524
  27.0 5.7 %all-gather.2 = f32[560,128]{1,0:T(8,128)S(1)} all-gather(f32[280,128]{1,0:T(8,128)S(1)} %get-tuple-element.66), channel_id=4, replica_groups={{0,16},{32,48},{64,80},{96,112},{128,144},{160,176},{192,208},{224,240}..., dimensions={0}, use_global_device_ids=true | all-gather | bytes 430080 | tf_op jit(solution)/shard_map/all_gather | solution.py:546
  32.7 0.0 collective-permute-done.2.fromacross
  32.7 0.0 copy-start
  32.7 1.0 first_fluid.1
  33.6 0.0 copy-start.1
  33.7 28.6 %all_to_all.55 = f32[64,1,128]{2,1,0:T(1,128)S(1)} all-to-all(f32[64,1,128]{2,1,0:T(1,128)S(1)} %bitcast.40), channel_id=1, replica_groups=mesh['dom'=64,'sub'=8,'lane'=2] {'dom'}, dimensions={0} | all-to-all | bytes 65536 | tf_op jit(solution)/shard_map/all_to_all | solution.py:549
  62.3 0.0 copy-done
  62.3 0.0 copy-done.1
  62.3 1.7 %first_structure.1 = (f32[128,128]{1,0:T(8,128)S(1)}, f32[16,512]{1,0:T(8,128)S(1)}, bf16[512,512]{1,0:T(8,128)(2,1)S(1)}, bf16[512,512]{1,0:T(8,128)(2,1)S(1)}) custom-call(f32[64,128]{1,0:T(8,128)S(1)} %bitcast.31, f32[3,512]{1,0:T(4,128)S(1)} %copy-done.1, f32[512,512]{1,0:T(8,128)S(1)} %copy-done), custom_call_target="tpu_custom_call" | custom-call | tf_op jit(solution)/shard_map/first_structure/pallas_call | solution.py:524
  64.0 17.3 %all_to_all.56 = f32[128,1,128]{2,1,0:T(1,128)S(1)} all-to-all(f32[128,1,128]{2,1,0:T(1,128)S(1)} %bitcast.38), channel_id=1, replica_groups=mesh['dom'=64,'sub'=8,'lane'=2] {'lane','dom'}, dimensions={0} | all-to-all | bytes 131072 | tf_op jit(solution)/shard_map/all_to_all | solution.py:596
  81.3 0.4 hand_out.1.values
  81.7 8.9 %collective-permute-start.3 = (f32[16,128]{1,0:T(8,128)S(1)}, f32[16,128]{1,0:T(8,128)S(1)}, u32[]{:S(2)}, u32[]{:S(2)}) collective-permute-start(f32[16,128]{1,0:T(8,128)S(1)} %hand_out.1.values), channel_id=1, source_target_pairs={{2,4},{4,2},{6,8},{8,6},{10,12},{12,10},{3,5},{5,3},{7,9},{9,7},{1... | collective-permute-start | bytes 24584 | tf_op jit(solution)/shard_map/ppermute | solution.py:546
  90.6 0.6 own_rows.1
  91.3 1.8 %all-gather.3 = f32[32,128]{1,0:T(8,128)S(1)} all-gather(f32[16,128]{1,0:T(8,128)S(1)} %hand_out.1.values), channel_id=5, replica_groups={{0,2},{4,6},{8,10},{12,14},{1,3},{5,7},{9,11},{13,15},{16,18},{20,22},{..., dimensions={0}, use_global_device_ids=true | all-gather | bytes 24576 | tf_op jit(solution)/shard_map/all_gather | solution.py:546
  93.1 0.0 collective-permute-done.3.fromacross
  93.1 2.6 %second_fluid.1 = (f32[32,16,128]{2,1,0:T(8,128)}, f32[64,128]{1,0:T(8,128)S(1)}) custom-call(f32[32,24,128]{2,1,0:T(8,128)S(1)} %get-tuple-element.58.erden, f32[32,24,128]{2,1,0:T(8,128)S(1)} %get-tuple-element.59.xrden, f32[8,24,128]{2,1,0:T(8,128)S(1)} %get-tuple-element.72.hrden0, f32[8,24,128]{2,1,0:T(8,128)S(1)} %get-tuple-element.73.hrden1, ...), custom_call_target="tpu_custom_call" | custom-call | tf_op jit(solution)/shard_map/second_fluid/pallas_call | solution.py:524
  95.7 14.6 %all_to_all.57 = f32[64,1,128]{2,1,0:T(1,128)S(1)} all-to-all(f32[64,1,128]{2,1,0:T(1,128)S(1)} %bitcast.41), channel_id=1, replica_groups=mesh['dom'=64,'sub'=8,'lane'=2] {'dom'}, dimensions={0} | all-to-all | bytes 65536 | tf_op jit(solution)/shard_map/all_to_all | solution.py:549
  110.3 1.2 second_structure.1
  111.5 14.6 %all_to_all.58 = f32[64,1,128]{2,1,0:T(1,128)S(1)} all-to-all(f32[64,1,128]{2,1,0:T(1,128)S(1)} %bitcast.35), channel_id=1, replica_groups=mesh['dom'=64,'sub'=8,'lane'=2] {'dom'}, dimensions={0} | all-to-all | bytes 65536 | tf_op jit(solution)/shard_map/all_to_all | solution.py:549
  126.2 0.2 arrive.1
  126.4 15.7 %all_to_all.59 = f32[16,1,128]{2,1,0:T(1,128)S(1)} all-to-all(f32[16,1,128]{2,1,0:T(1,128)S(1)} %bitcast.42), channel_id=1, replica_groups=mesh['dom'=64,'sub'=8,'lane'=2] {'sub','lane'}, dimensions={0} | all-to-all | bytes 16384 | tf_op jit(solution)/shard_map/all_to_all | solution.py:618
  142.1 0.8 finish.1
Async XLA Ops:
  2.2 22.0 %collective-permute-start = (f32[320,128]{1,0:T(8,128)S(1)}, f32[320,128]{1,0:T(8,128)S(1)}, u32[]{:S(2)}, u32[]{:S(2)}) collective-permute-start(f32[320,128]{1,0:T(8,128)S(1)} %get-tuple-element.51), channel_id=1, source_target_pairs={{2,4},{4,2},{6,8},{8,6},{10,12},{12,10},{3,5},{5,3},{7,9},{9,7},{1... | collective-permute-start | bytes 491528 | tf_op jit(solution)/shard_map/ppermute | solution.py:561
  11.3 12.9 %collective-permute-start.1 = (f32[24,128]{1,0:T(8,128)S(1)}, f32[24,128]{1,0:T(8,128)S(1)}, u32[]{:S(2)}, u32[]{:S(2)}) collective-permute-start(f32[24,128]{1,0:T(8,128)S(1)} %get-tuple-element.53), channel_id=1, source_target_pairs={{2,4},{4,2},{6,8},{8,6},{10,12},{12,10},{3,5},{5,3},{7,9},{9,7},{1... | collective-permute-start | bytes 36872 | tf_op jit(solution)/shard_map/ppermute | solution.py:546
  24.4 8.3 %collective-permute-start.2 = (f32[280,128]{1,0:T(8,128)S(1)}, f32[280,128]{1,0:T(8,128)S(1)}, u32[]{:S(2)}, u32[]{:S(2)}) collective-permute-start(f32[280,128]{1,0:T(8,128)S(1)} %get-tuple-element.67), channel_id=1, source_target_pairs={{16,32},{32,16},{48,64},{64,48},{80,96},{96,80},{112,128},{128,112... | collective-permute-start | bytes 430088 | tf_op jit(solution)/shard_map/ppermute | solution.py:546
  32.7 29.6 %copy-start = (f32[512,512]{1,0:T(8,128)S(1)}, f32[512,512]{1,0:T(8,128)}, u32[]{:S(2)}) copy-start(f32[512,512]{1,0:T(8,128)} %shell.3) | copy-start | bytes 3145732
  33.6 28.7 %copy-start.1 = (f32[3,512]{1,0:T(4,128)S(1)}, f32[3,512]{1,0:T(4,128)}, u32[]{:S(2)}) copy-start(f32[3,512]{1,0:T(4,128)} %nodes.1) | copy-start | bytes 18436
  81.7 11.4 %collective-permute-start.3 = (f32[16,128]{1,0:T(8,128)S(1)}, f32[16,128]{1,0:T(8,128)S(1)}, u32[]{:S(2)}, u32[]{:S(2)}) collective-permute-start(f32[16,128]{1,0:T(8,128)S(1)} %hand_out.1.values), channel_id=1, source_target_pairs={{2,4},{4,2},{6,8},{8,6},{10,12},{12,10},{3,5},{5,3},{7,9},{9,7},{1... | collective-permute-start | bytes 24584 | tf_op jit(solution)/shard_map/ppermute | solution.py:546
